TPU v7x, 32 devices: a whole 2x2x4 slice. The times are simulated.
32 devices in a mesh: sq: 8 (over y, x, core), tp: 4 (over z).
Axes of the slice: x: 2, y: 2, z: 4, core: 2. Of those that a mesh axis runs over, the one named last changes fastest.
Arguments:
- inputs: bfloat16 [2048, 4, 2048], P('sq', None, 'tp'), may hold values from -6 to 6
- lengths: int32 [4], replicated, may hold values from 256 to 2048, as said below
- routes: int32 [2048, 4, 8], P('sq'), may hold values from 0 to 15, all different within a row; in each aligned block of 1024 rows (0 to 1023, 1024 to 2047, ..., all dimensions but the last counted through in order) at most 1024 rows name the same one
- attn_gain: float32 [2048], replicated, may hold values from 0.5 to 1.5
- w_query: bfloat16 [2048, 2048], P(None, 'tp'), may hold values from -0.125 to 0.125
- w_key: bfloat16 [2048, 2048], P(None, 'tp'), may hold values from -0.125 to 0.125
- w_value: bfloat16 [2048, 2048], P(None, 'tp'), may hold values from -0.125 to 0.125
- query_gain: float32 [2048], P('tp'), may hold values from 0.1 to 1.9
- key_gain: float32 [2048], P('tp'), may hold values from 0.1 to 1.9
- w_out: bfloat16 [2048, 2048], P('tp'), may hold values from -2 to 2
- ffn_gain: float32 [2048], replicated, may hold values from 0.5 to 1.5
- router: bfloat16 [2048, 16], replicated, may hold values from -0.0625 to 0.0625
- w_gate: bfloat16 [16, 2048, 1024], P('tp'), may hold values from -0.125 to 0.125
- w_up: bfloat16 [16, 2048, 1024], P('tp'), may hold values from -0.125 to 0.125
- w_down: bfloat16 [16, 1024, 2048], P('tp'), may hold values from -1.5859375 to 1.5859375
- cotangent: bfloat16 [2048, 4, 2048], P('sq', None, 'tp'), may hold values from -6 to 6
Outputs:
- output: bfloat16 [2048, 4, 2048], P('sq', None, 'tp')
- input_grad: float32 [2048, 4, 2048], P('sq', None, 'tp')
- attn_gain_grad: float32 [2048], replicated
- w_query_grad: float32 [2048, 2048], P('sq', 'tp')
- w_key_grad: float32 [2048, 2048], P('sq', 'tp')
- w_value_grad: float32 [2048, 2048], P('sq', 'tp')
- query_gain_grad: float32 [2048], replicated
- key_gain_grad: float32 [2048], replicated
- w_out_grad: float32 [2048, 2048], P('tp', 'sq')
- ffn_gain_grad: float32 [2048], replicated
- router_grad: float32 [2048, 16], replicated
- w_gate_grad: float32 [16, 2048, 1024], P('tp', 'sq')
- w_up_grad: float32 [16, 2048, 1024], P('tp', 'sq')
- w_down_grad: float32 [16, 1024, 2048], P('tp', None, 'sq')
Inputs may be any that keep to these rules, and one draw needn't show every extreme that they name: `routes`: each row names 8 different experts. In the rows of one index of sq (aligned blocks of 1024 rows in the array's order) no expert is named by more than 1024 rows, a bound that some block reaches. `lengths`: positions at or past a sequence's length are padding: no query attends to them. Some sequence has all 2048 positions valid.
All inputs are finite; a program needn't handle non-finite values.
Results may differ from a plain program's by a relative error of at most 0.028.
Values may be sent and summed in bfloat16 or wider, within the bound.
No kernel may reach another device: no remote copies, remote signals or barrier semaphores. Data moves between devices by JAX's collectives and lax.ppermute only.
A program may use at most 512 MiB of HBM per device.

v0:
```python
import jax
import jax.numpy as jnp
from jax import lax
from jax.sharding import PartitionSpec as P

HEADS = 16
HD = 128


EPSILON = 1e-05
ROTARY_BASE = 10000.0
NEGATIVE = -1e30


def shifted(block, axis, distance):
    devices = range(lax.axis_size(axis))
    route = [((i - distance) % len(devices), i) for i in devices]
    return lax.ppermute(block, axis, route)


def rotary_tables(positions, head_size):
    exponent = jnp.arange(head_size // 2, dtype=jnp.float32) * 2.0 / head_size
    frequency = ROTARY_BASE ** (-exponent)
    angles = positions.astype(jnp.float32)[:, None] * frequency[None, :]
    cosine = jnp.concatenate([jnp.cos(angles), jnp.cos(angles)], axis=-1)
    sine_table = jnp.concatenate([jnp.sin(angles), jnp.sin(angles)], axis=-1)
    return (cosine, sine_table)


def rotate_forward(values, cosine, sine_table):
    half_width = values.shape[-1] // 2
    turned = jnp.concatenate([-values[..., half_width:], values[..., :half_width]], axis=-1)
    return values * cosine[:, None, None, :] + turned * sine_table[:, None, None, :]


def rotate_backward(gradients, cosine, sine_table):
    half_width = gradients.shape[-1] // 2
    scaled = gradients * sine_table[:, None, None, :]
    turned = jnp.concatenate([scaled[..., half_width:], -scaled[..., :half_width]], axis=-1)
    return gradients * cosine[:, None, None, :] + turned


def key_allowed(query_pos, key_pos, lengths):
    causal = key_pos[None, :] <= query_pos[:, None]
    inside = key_pos[None, :] < lengths[:, None]
    return causal[None, None, :, :] & inside[:, None, None, :]


def score_grads(
    queries, out_grads, logsum, deltas, query_pos, keys, values, key_pos, lengths, scaling
):
    scores = (
        jnp.einsum("qshd,kshd->shqk", queries, keys, preferred_element_type=jnp.float32) * scaling
    )
    allowed = key_allowed(query_pos, key_pos, lengths)
    weights = jnp.where(allowed, jnp.exp(scores - logsum[..., None]), 0.0)
    weight_grads = jnp.einsum(
        "qshd,kshd->shqk", out_grads, values, preferred_element_type=jnp.float32
    )
    score_grad = (weights * (weight_grads - deltas[..., None])).astype(jnp.bfloat16)
    return (weights.astype(jnp.bfloat16), score_grad)


def shards(
    inputs,
    lengths,
    routes,
    attn_gain,
    w_query,
    w_key,
    w_value,
    query_gain,
    key_gain,
    w_out,
    ffn_gain,
    router,
    w_gate,
    w_up,
    w_down,
    cotangent,
):
    local_len, seq_count, feat_local = inputs.shape
    model_width, head_cols = w_query.shape
    heads_local = head_cols // HD
    tp_rank = lax.axis_index("tp")
    tp_count = lax.axis_size("tp")
    sq_rank = lax.axis_index("sq")
    sq_count = lax.axis_size("sq")
    scaling = HD ** (-0.5)
    token_count = local_len * seq_count
    query_pos = sq_rank * local_len + jnp.arange(local_len, dtype=jnp.int32)
    cosine, sine_table = rotary_tables(query_pos, HD)
    column_start = tp_rank * feat_local
    head_start = tp_rank * head_cols
    owned = jnp.arange(model_width, dtype=jnp.int32) // feat_local == tp_rank
    head_shape = (local_len, seq_count, heads_local, HD)
    rows_low, grad_low = (
        lax.all_gather(inputs, "tp", axis=2, tiled=True),
        lax.all_gather(cotangent, "tp", axis=2, tiled=True),
    )
    rows = rows_low.astype(jnp.float32)
    inv_first = lax.rsqrt(jnp.mean(rows * rows, axis=-1, keepdims=True) + EPSILON)
    normed_first = rows * inv_first
    attn_in = (normed_first * attn_gain).astype(jnp.bfloat16)
    query_raw = jnp.dot(attn_in, w_query, preferred_element_type=jnp.float32)
    key_raw = jnp.dot(attn_in, w_key, preferred_element_type=jnp.float32)
    value_low = jnp.dot(attn_in, w_value, preferred_element_type=jnp.float32).astype(jnp.bfloat16)
    query_square, key_square = lax.psum(
        (jnp.sum(query_raw * query_raw, axis=-1), jnp.sum(key_raw * key_raw, axis=-1)), "tp"
    )
    inv_query = lax.rsqrt(query_square / (HEADS * HD) + EPSILON)[..., None]
    inv_key = lax.rsqrt(key_square / (HEADS * HD) + EPSILON)[..., None]
    query_hat = query_raw * inv_query
    key_hat = key_raw * inv_key
    query_low = rotate_forward(
        (query_hat * query_gain).reshape(head_shape), cosine, sine_table
    ).astype(jnp.bfloat16)
    key_low = rotate_forward((key_hat * key_gain).reshape(head_shape), cosine, sine_table).astype(
        jnp.bfloat16
    )
    value_heads = value_low.reshape(head_shape)
    stat_shape = (seq_count, heads_local, local_len)
    running = jnp.full(stat_shape, NEGATIVE, jnp.float32)
    key_piece = lax.all_gather(key_low, "sq", axis=0, tiled=True)
    value_piece = lax.all_gather(value_heads, "sq", axis=0, tiled=True)
    key_pos = jnp.arange(key_piece.shape[0], dtype=jnp.int32)
    scores = (
        jnp.einsum("qshd,kshd->shqk", query_low, key_piece, preferred_element_type=jnp.float32)
        * scaling
    )
    allowed = key_allowed(query_pos, key_pos, lengths)
    scores = jnp.where(allowed, scores, NEGATIVE)
    newest = jnp.maximum(running, jnp.max(scores, axis=-1))
    weights = jnp.where(allowed, jnp.exp(scores - newest[..., None]), 0.0)
    weight_sum = jnp.sum(weights, axis=-1)
    accum = jnp.einsum(
        "shqk,kshd->shqd",
        weights.astype(jnp.bfloat16),
        value_piece,
        preferred_element_type=jnp.float32,
    )
    running, weight_sum, accum = (newest, weight_sum, accum)
    attn_heads = accum / weight_sum[..., None]
    logsum = running + jnp.log(weight_sum)
    attn_low = (
        jnp.transpose(attn_heads, (2, 0, 1, 3))
        .reshape(local_len, seq_count, head_cols)
        .astype(jnp.bfloat16)
    )
    branch = lax.psum(
        jnp.dot(attn_low, w_out, preferred_element_type=jnp.float32).astype(jnp.bfloat16), "tp"
    ).astype(jnp.float32)
    middle = rows + branch
    inv_second = lax.rsqrt(jnp.mean(middle * middle, axis=-1, keepdims=True) + EPSILON)
    normed_second = middle * inv_second
    ffn_in = (normed_second * ffn_gain).astype(jnp.bfloat16)
    flat_in = ffn_in.reshape(token_count, model_width)
    probabilities = jax.nn.softmax(
        jnp.dot(flat_in, router, preferred_element_type=jnp.float32), axis=-1
    )
    flat_routes = routes.reshape(token_count, routes.shape[2])
    experts_local = w_gate.shape[0]
    experts_total = experts_local * tp_count
    expert_ids = jnp.arange(experts_total, dtype=jnp.int32)
    chosen = jnp.sum(
        jnp.where(
            flat_routes[:, :, None] == expert_ids[None, None, :], probabilities[:, None, :], 0.0
        ),
        axis=2,
    )
    capacity = 2 * token_count * flat_routes.shape[1] // experts_total
    token_ids = jnp.arange(token_count, dtype=jnp.int32)
    mixture = jnp.zeros((token_count, model_width), jnp.float32)
    kept_slots = []
    for expert_slot in range(experts_local):
        expert_id = tp_rank * experts_local + expert_slot
        matched = flat_routes == expert_id
        present = jnp.any(matched, axis=1)
        gate_value = jnp.sum(jnp.where(matched, chosen, 0.0), axis=1)
        ordinal = jnp.cumsum(present.astype(jnp.int32), dtype=jnp.int32) - 1
        target = jnp.where(present, ordinal, capacity)
        slot_rows = jnp.zeros((capacity,), jnp.int32).at[target].set(token_ids, mode="drop")
        slot_gate = jnp.zeros((capacity,), jnp.float32).at[target].set(gate_value, mode="drop")
        slot_live = jnp.zeros((capacity,), jnp.float32).at[target].set(1.0, mode="drop")
        expert_in = flat_in[slot_rows]
        gate_pre = jnp.dot(expert_in, w_gate[expert_slot], preferred_element_type=jnp.float32)
        up_pre = jnp.dot(expert_in, w_up[expert_slot], preferred_element_type=jnp.float32)
        hidden_low = (jax.nn.silu(gate_pre) * up_pre).astype(jnp.bfloat16)
        expert_out = jnp.dot(hidden_low, w_down[expert_slot], preferred_element_type=jnp.float32)
        mixture = mixture.at[slot_rows].add(slot_gate[:, None] * expert_out)
        kept_slots.append(
            (
                expert_slot,
                expert_id,
                slot_rows,
                slot_gate,
                slot_live,
                expert_in,
                gate_pre,
                up_pre,
                hidden_low,
                expert_out,
            )
        )
    mixture_own = lax.psum_scatter(
        mixture.reshape(local_len, seq_count, model_width).astype(jnp.bfloat16),
        "tp",
        scatter_dimension=2,
        tiled=True,
    ).astype(jnp.float32)
    middle_own = lax.dynamic_slice_in_dim(middle, column_start, feat_local, axis=2)
    output = (middle_own + mixture_own).astype(jnp.bfloat16)
    grad_rows = grad_low.astype(jnp.float32)
    flat_grad = grad_rows.reshape(token_count, model_width)
    second_part = jnp.zeros((token_count, model_width), jnp.float32)
    prob_grad = jnp.zeros((token_count, experts_total), jnp.float32)
    gate_grads = []
    up_grads = []
    down_grads = []
    for (
        expert_slot,
        expert_id,
        slot_rows,
        slot_gate,
        slot_live,
        expert_in,
        gate_pre,
        up_pre,
        hidden_low,
        expert_out,
    ) in kept_slots:
        slot_grad = flat_grad[slot_rows]
        out_grad = (slot_gate[:, None] * slot_grad).astype(jnp.bfloat16)
        token_gate = (
            jnp.zeros((token_count,), jnp.float32)
            .at[slot_rows]
            .add(slot_live * jnp.sum(expert_out * slot_grad, axis=1))
        )
        prob_grad = prob_grad + jnp.where(
            expert_ids[None, :] == expert_id, token_gate[:, None], 0.0
        )
        hidden_grad = jnp.dot(
            out_grad, w_down[expert_slot].T, preferred_element_type=jnp.float32
        ).astype(jnp.bfloat16)
        sigmoid_gate = jax.nn.sigmoid(gate_pre)
        hidden_float = hidden_grad.astype(jnp.float32)
        gate_pre_grad = (
            hidden_float * up_pre * sigmoid_gate * (1.0 + gate_pre * (1.0 - sigmoid_gate))
        ).astype(jnp.bfloat16)
        up_pre_grad = (hidden_float * gate_pre * sigmoid_gate).astype(jnp.bfloat16)
        input_term = jnp.dot(
            gate_pre_grad, w_gate[expert_slot].T, preferred_element_type=jnp.float32
        ) + jnp.dot(up_pre_grad, w_up[expert_slot].T, preferred_element_type=jnp.float32)
        second_part = second_part.at[slot_rows].add(input_term * slot_live[:, None])
        gate_grads.append(jnp.dot(expert_in.T, gate_pre_grad, preferred_element_type=jnp.float32))
        up_grads.append(jnp.dot(expert_in.T, up_pre_grad, preferred_element_type=jnp.float32))
        down_grads.append(jnp.dot(hidden_low.T, out_grad, preferred_element_type=jnp.float32))
    inner = jnp.sum(probabilities * prob_grad, axis=-1, keepdims=True)
    logit_grad = probabilities * (prob_grad - inner)
    second_part = second_part + jnp.dot(
        logit_grad, router.astype(jnp.float32).T, precision=lax.Precision.HIGHEST
    )
    router_grad = jnp.dot(
        flat_in.T, logit_grad, precision=lax.Precision.HIGHEST, preferred_element_type=jnp.float32
    )
    second_grad = lax.psum(
        second_part.reshape(local_len, seq_count, model_width).astype(jnp.bfloat16), "tp"
    ).astype(jnp.float32)
    gained_second = second_grad * ffn_gain
    ffn_gain_part = jnp.where(owned, jnp.sum(second_grad * normed_second, axis=(0, 1)), 0.0)
    middle_grad = grad_rows + inv_second * (
        gained_second
        - normed_second * jnp.mean(gained_second * normed_second, axis=-1, keepdims=True)
    )
    middle_low = middle_grad.astype(jnp.bfloat16)
    out_weight_grad = jnp.dot(
        attn_low.reshape(token_count, head_cols).T,
        middle_low.reshape(token_count, model_width),
        preferred_element_type=jnp.float32,
    )
    attn_grad = (
        jnp.dot(middle_low, w_out.T, preferred_element_type=jnp.float32)
        .astype(jnp.bfloat16)
        .reshape(head_shape)
    )
    deltas = jnp.sum(
        jnp.transpose(attn_grad.astype(jnp.float32), (1, 2, 0, 3)) * attn_heads, axis=-1
    )
    query_zero = jnp.zeros(head_shape, jnp.float32)

    def key_turn(step, carry):
        key_piece, value_piece, key_acc, value_acc, query_acc = carry
        anchor = (sq_rank + step) % sq_count
        key_pos = anchor * local_len + jnp.arange(local_len, dtype=jnp.int32)
        weight_low, score_grad = score_grads(
            query_low,
            attn_grad,
            logsum,
            deltas,
            query_pos,
            key_piece,
            value_piece,
            key_pos,
            lengths,
            scaling,
        )
        query_acc = query_acc + scaling * jnp.einsum(
            "shqk,kshd->qshd", score_grad, key_piece, preferred_element_type=jnp.float32
        )
        key_acc = key_acc + scaling * jnp.einsum(
            "shqk,qshd->kshd", score_grad, query_low, preferred_element_type=jnp.float32
        )
        value_acc = value_acc + jnp.einsum(
            "shqk,qshd->kshd", weight_low, attn_grad, preferred_element_type=jnp.float32
        )
        key_piece, value_piece = shifted((key_piece, value_piece), "sq", -1)
        key_acc, value_acc = (
            shifted(key_acc.astype(jnp.bfloat16), "sq", -1).astype(key_acc.dtype),
            shifted(value_acc.astype(jnp.bfloat16), "sq", -1).astype(value_acc.dtype),
        )
        return (key_piece, value_piece, key_acc, value_acc, query_acc)

    finished = lax.fori_loop(
        0, sq_count, key_turn, (key_low, value_heads, query_zero, query_zero, query_zero)
    )
    key_grad = finished[2]
    value_grad = finished[3]
    query_grad = finished[4]
    query_grad_low = query_grad.astype(jnp.bfloat16)
    key_grad_low = key_grad.astype(jnp.bfloat16)
    value_raw_grad = value_grad.astype(jnp.bfloat16).reshape(local_len, seq_count, head_cols)
    query_norm_grad = rotate_backward(
        query_grad_low.astype(jnp.float32), cosine, sine_table
    ).reshape(local_len, seq_count, head_cols)
    key_norm_grad = rotate_backward(key_grad_low.astype(jnp.float32), cosine, sine_table).reshape(
        local_len, seq_count, head_cols
    )
    gained_query = query_norm_grad * query_gain
    gained_key = key_norm_grad * key_gain
    query_inner, key_inner = lax.psum(
        (jnp.sum(gained_query * query_hat, axis=-1), jnp.sum(gained_key * key_hat, axis=-1)), "tp"
    )
    query_raw_grad = (
        inv_query * (gained_query - query_hat * (query_inner / (HEADS * HD))[..., None])
    ).astype(jnp.bfloat16)
    key_raw_grad = (
        inv_key * (gained_key - key_hat * (key_inner / (HEADS * HD))[..., None])
    ).astype(jnp.bfloat16)
    query_gain_part = lax.dynamic_update_slice_in_dim(
        jnp.zeros((HEADS * HD,), jnp.float32),
        jnp.sum(query_norm_grad * query_hat, axis=(0, 1)),
        head_start,
        0,
    )
    key_gain_part = lax.dynamic_update_slice_in_dim(
        jnp.zeros((HEADS * HD,), jnp.float32),
        jnp.sum(key_norm_grad * key_hat, axis=(0, 1)),
        head_start,
        0,
    )
    first_part = (
        jnp.dot(query_raw_grad, w_query.T, preferred_element_type=jnp.float32)
        + jnp.dot(key_raw_grad, w_key.T, preferred_element_type=jnp.float32)
        + jnp.dot(value_raw_grad, w_value.T, preferred_element_type=jnp.float32)
    )
    flat_attn_in = attn_in.reshape(token_count, model_width)
    query_weight_grad = jnp.dot(
        flat_attn_in.T,
        query_raw_grad.reshape(token_count, head_cols),
        preferred_element_type=jnp.float32,
    )
    key_weight_grad = jnp.dot(
        flat_attn_in.T,
        key_raw_grad.reshape(token_count, head_cols),
        preferred_element_type=jnp.float32,
    )
    value_weight_grad = jnp.dot(
        flat_attn_in.T,
        value_raw_grad.reshape(token_count, head_cols),
        preferred_element_type=jnp.float32,
    )
    first_inner = jnp.sum(first_part * attn_gain * normed_first, axis=-1, keepdims=True)
    first_grad, first_inner_sum = (
        lax.psum_scatter(
            first_part.astype(jnp.bfloat16), "tp", scatter_dimension=2, tiled=True
        ).astype(jnp.float32),
        lax.psum_scatter(
            jnp.broadcast_to(first_inner, (local_len, seq_count, tp_count)).astype(jnp.bfloat16),
            "tp",
            scatter_dimension=2,
            tiled=True,
        ).astype(jnp.float32),
    )
    normed_own = lax.dynamic_slice_in_dim(normed_first, column_start, feat_local, axis=2)
    gain_own = lax.dynamic_slice_in_dim(attn_gain, column_start, feat_local, axis=0)
    middle_grad_own = lax.dynamic_slice_in_dim(middle_grad, column_start, feat_local, axis=2)
    input_grad = middle_grad_own + inv_first * (
        gain_own * first_grad - normed_own * first_inner_sum / model_width
    )
    attn_gain_part = lax.dynamic_update_slice_in_dim(
        jnp.zeros((model_width,), jnp.float32),
        jnp.sum(first_grad * normed_own, axis=(0, 1)),
        column_start,
        0,
    )
    weight_out = (
        lax.psum_scatter(
            query_weight_grad.astype(jnp.bfloat16), "sq", scatter_dimension=0, tiled=True
        ).astype(jnp.float32),
        lax.psum_scatter(
            key_weight_grad.astype(jnp.bfloat16), "sq", scatter_dimension=0, tiled=True
        ).astype(jnp.float32),
        lax.psum_scatter(
            value_weight_grad.astype(jnp.bfloat16), "sq", scatter_dimension=0, tiled=True
        ).astype(jnp.float32),
        lax.psum_scatter(
            out_weight_grad.astype(jnp.bfloat16), "sq", scatter_dimension=1, tiled=True
        ).astype(jnp.float32),
        lax.psum_scatter(
            jnp.stack(gate_grads).astype(jnp.bfloat16), "sq", scatter_dimension=1, tiled=True
        ).astype(jnp.float32),
        lax.psum_scatter(
            jnp.stack(up_grads).astype(jnp.bfloat16), "sq", scatter_dimension=1, tiled=True
        ).astype(jnp.float32),
        lax.psum_scatter(
            jnp.stack(down_grads).astype(jnp.bfloat16), "sq", scatter_dimension=2, tiled=True
        ).astype(jnp.float32),
    )
    small_out = lax.psum(
        (attn_gain_part, query_gain_part, key_gain_part, ffn_gain_part, router_grad), ("sq", "tp")
    )
    return (
        output,
        input_grad,
        small_out[0],
        weight_out[0],
        weight_out[1],
        weight_out[2],
        small_out[1],
        small_out[2],
        weight_out[3],
        small_out[3],
        small_out[4],
        weight_out[4],
        weight_out[5],
        weight_out[6],
    )


def solution(mesh):
    placed = (
        P("sq", None, "tp"),
        P(),
        P("sq", None, None),
        P(),
        P(None, "tp"),
        P(None, "tp"),
        P(None, "tp"),
        P("tp"),
        P("tp"),
        P("tp", None),
        P(),
        P(),
        P("tp", None, None),
        P("tp", None, None),
        P("tp", None, None),
        P("sq", None, "tp"),
    )
    return jax.shard_map(
        shards,
        mesh=mesh,
        in_specs=placed,
        out_specs=(
            P("sq", None, "tp"),
            P("sq", None, "tp"),
            P(),
            P("sq", "tp"),
            P("sq", "tp"),
            P("sq", "tp"),
            P(),
            P(),
            P("tp", "sq"),
            P(),
            P(),
            P("tp", "sq", None),
            P("tp", "sq", None),
            P("tp", None, "sq"),
        ),
        check_vma=False,
    )
```

profile of v0, /device:TPU:0, one launch (start us, length us, event | category | flops | bytes accessed | tf_op | source)
XLA Modules:
  0.0 2493.5 jit_solution(8971015118409575062)
XLA Ops:
  10.7 83.0 %all-gather.5.cloned.1.call-done = bf16[256,4,2048]{2,0,1:T(8,128)(2,1)} async-done(((bf16[256,4,512]{2,0,1:T(8,128)(2,1)}), bf16[256,4,2048]{2,0,1:T(8,128)(2,1)}) %all-gather.5.cloned.1.call-update) | async-done | bytes 4194320 | tf_op jit(solution)/shard_map/all_gather | solution.py:98
  137.1 39.5 %all-gather.7.cloned.1.call-done = bf16[2048,4,4,128]{3,0,2,1:T(8,128)(2,1)} async-done(((bf16[256,4,4,128]{3,0,2,1:T(8,128)(2,1)}), bf16[2048,4,4,128]{3,0,2,1:T(8,128)(2,1)}) %all-gather.7.cloned.1.call-update) | async-done | bytes 8388624 | tf_op jit(solution)/shard_map/all_gather | solution.py:124
  176.6 17.4 fusion.15
  194.0 16.7 fusion.16
  210.6 24.4 all-gather.9.cloned.1.call-done
  235.1 19.4 fusion.167
  260.8 18.0 fusion.259
  343.8 12.4 gather_fusion.4
  356.2 12.3 gather_fusion.7
  368.5 12.4 gather_fusion.6
  381.0 12.4 gather_fusion.5
  393.3 80.9 %all-reduce.8.cloned.1.call-done = bf16[256,4,2048]{2,0,1:T(8,128)(2,1)} async-done(((bf16[256,4,2048]{2,0,1:T(8,128)(2,1)}), bf16[256,4,2048]{2,0,1:T(8,128)(2,1)}) %all-reduce.8.cloned.1.call-update) | async-done | bytes 4194320 | tf_op jit(solution)/shard_map/psum | solution.py:150
  494.6 11.9 gather_fusion
  506.6 11.6 gather_fusion.3
  518.1 11.6 gather_fusion.2
  529.7 11.5 gather_fusion.1
  610.5 10.8 multiply_reduce_fusion.4
  621.3 10.8 multiply_reduce_fusion.1
  632.2 10.8 multiply_reduce_fusion.2
  700.3 12.5 fusion.50
  736.9 12.5 fusion.55
  773.8 12.5 fusion.60
  810.3 12.5 fusion.65
  842.5 23.6 scatter_custom_fusion.20
  866.2 23.8 scatter_custom_fusion.21
  890.0 23.6 scatter_custom_fusion.22
  913.6 24.0 scatter_custom_fusion.23
  959.9 151.7 %all-reduce.10.cloned.1.call-done = bf16[256,4,2048]{2,0,1:T(8,128)(2,1)} async-done(((bf16[256,4,2048]{2,0,1:T(8,128)(2,1)}), bf16[256,4,2048]{2,0,1:T(8,128)(2,1)}) %all-reduce.10.cloned.1.call-update) | async-done | bytes 4194320 | tf_op jit(solution)/shard_map/psum | solution.py:266
  1141.2 495.4 %while.24 = (s32[]{:T(128)}, bf16[256,4,4,128]{3,0,2,1:T(8,128)(2,1)}, bf16[256,4,4,128]{3,0,2,1:T(8,128)(2,1)}, f32[256,4,4,128]{3,0,2,1:T(8,128)}, f32[256,4,4...) while((s32[]{:T(128)}, ...), condition=%wide.region_62.63_spmd.clone, body=%wide.region_61.62_spmd.clone.sunk | while | flops 1359283712 | bytes 98492016 | solution.py:323
  1191.0 11.3 collective-permute-done.1
  1253.0 11.3 collective-permute-done.1
  1315.0 11.3 collective-permute-done.1
  1377.0 11.3 collective-permute-done.1
  1439.0 11.3 collective-permute-done.1
  1501.0 11.3 collective-permute-done.1
  1563.1 11.3 collective-permute-done.1
  1625.1 11.3 collective-permute-done.1
  1705.8 19.4 scatter_custom_fusion.2
  1725.3 22.4 scatter_custom_fusion.5
  1747.7 22.6 scatter_custom_fusion.8
  1770.3 22.4 scatter_custom_fusion.11
  1826.3 11.3 multiply_reduce_fusion
  1972.0 25.4 %reduce-scatter.12.cloned.1.call-done = bf16[256,4,512]{2,0,1:T(8,128)(2,1)} async-done(((bf16[256,4,2048]{2,0,1:T(8,128)(2,1)}), bf16[256,4,512]{2,0,1:T(8,128)(2,1)}) %reduce-scatter.12.cloned.1.call-update) | async-done | bytes 1048592 | tf_op jit(solution)/shard_map/reduce_scatter | solution.py:384
  2003.5 41.8 %all-reduce.1 = (f32[2048]{0:T(1024)}, f32[2048]{0:T(1024)}, f32[2048]{0:T(1024)}, f32[2048]{0:T(1024)}) all-reduce(f32[2048]{0:T(1024)S(1)} %dynamic_update_slice.9, f32[2048]{0:T(1024)S(1)} %dynamic_update_slice.10, f32[2048]{0:T(1024)S(1)} %dynamic_update_slice.11, f32[2048]{0:T(1024)S(1)} %fusion.209), channel_id=1, replica_groups=mesh['sq'=8,'tp'=4] {'sq','tp'}, use_global_device_ids=true, to_apply=%region_71.72 | all-reduce | flops 8192 | bytes 65536 | tf_op jit(solution)/shard_map/psum | solution.py:429
  2045.3 72.7 %reduce-scatter.22.cloned.1.call-done = bf16[4,256,1024]{2,1,0:T(8,128)(2,1)} async-done(((bf16[4,2048,1024]{2,1,0:T(8,128)(2,1)}), bf16[4,256,1024]{2,1,0:T(8,128)(2,1)}) %reduce-scatter.22.cloned.1.call-update) | async-done | bytes 2097168 | tf_op jit(solution)/shard_map/reduce_scatter | solution.py:419
  2122.0 115.3 %reduce-scatter.24.cloned.1.call-done = bf16[4,256,1024]{2,1,0:T(8,128)(2,1)} async-done(((bf16[4,2048,1024]{2,1,0:T(8,128)(2,1)}), bf16[4,256,1024]{2,1,0:T(8,128)(2,1)}) %reduce-scatter.24.cloned.1.call-update) | async-done | bytes 2097168 | tf_op jit(solution)/shard_map/reduce_scatter | solution.py:422
  2241.4 115.3 %reduce-scatter.26.cloned.1.call-done = bf16[4,1024,256]{2,1,0:T(8,128)(2,1)} async-done(((bf16[4,1024,2048]{2,1,0:T(8,128)(2,1)}), bf16[4,1024,256]{2,1,0:T(8,128)(2,1)}) %reduce-scatter.26.cloned.1.call-update) | async-done | bytes 2097168 | tf_op jit(solution)/shard_map/reduce_scatter | solution.py:425
  2360.7 124.5 %all-reduce.12.cloned.1.call-done = f32[2048,16]{0,1:T(8,128)} async-done(((f32[2048,16]{0,1:T(8,128)}), f32[2048,16]{0,1:T(8,128)}) %all-reduce.12.cloned.1.call-update) | async-done | bytes 131088 | tf_op jit(solution)/shard_map/psum | solution.py:429
  (836 shorter events, 1067.8 us)
Async XLA Ops:
  7.2 86.5 %all-gather.5.cloned.1.call-start = ((), (), s32[]{:S(2)}) async-start(), calls=%async_computation.9 | async-start | bytes 5242880 | tf_op jit(solution)/shard_map/all_gather | solution.py:98
  9.8 166.8 %all-gather.7.cloned.1.call-start = ((), (), s32[]{:S(2)}) async-start(), calls=%async_computation.10 | async-start | bytes 9437184 | tf_op jit(solution)/shard_map/all_gather | solution.py:124
  123.0 112.0 %all-gather.9.cloned.1.call-start = ((), (), s32[]{:S(2)}) async-start(), calls=%async_computation.11 | async-start | bytes 9437184 | tf_op jit(solution)/shard_map/all_gather | solution.py:125
  131.3 193.2 %all-gather.11.cloned.1.call-start = ((), (), s32[]{:S(2)}) async-start(), calls=%async_computation.14 | async-start | bytes 5242880 | tf_op jit(solution)/shard_map/all_gather | solution.py:99
  133.8 340.4 %all-reduce.8.cloned.1.call-start = ((), (), s32[]{:S(2)}) async-start(), calls=%async_computation.12 | async-start | bytes 8388608 | tf_op jit(solution)/shard_map/psum | solution.py:150
  259.8 851.7 %all-reduce.10.cloned.1.call-start = ((), (), s32[]{:S(2)}) async-start(), calls=%async_computation.15 | async-start | bytes 8388608 | tf_op jit(solution)/shard_map/psum | solution.py:266
  957.4 1003.3 %reduce-scatter.14.cloned.1.call-start = ((), (), s32[]{:S(2)}) async-start(), calls=%async_computation.17 | async-start | bytes 2359296 | tf_op jit(solution)/shard_map/reduce_scatter | solution.py:407
  1154.2 14.5 collective-permute-start.2
  1158.9 21.0 collective-permute-start.3
  1159.6 31.4 %collective-permute-start = (bf16[256,4,4,128]{3,0,2,1:T(8,128)(2,1)S(1)}, bf16[256,4,4,128]{3,0,2,1:T(8,128)(2,1)}, u32[]{:S(2)}, u32[]{:S(2)}) collective-permute-start(bf16[256,4,4,128]{3,0,2,1:T(8,128)(2,1)S(1)} %copy.236), channel_id=1, source_target_pairs={{4,0},{8,4},{12,8},{16,12},{20,16},{24,20},{28,24},{0,28},{5,1},{9... | collective-permute-start | bytes 3145736 | tf_op jit(solution)/shard_map/while/body/eval_jaxpr/ppermute | solution.py:18
  1159.6 42.7 %collective-permute-start.1 = (bf16[256,4,4,128]{3,0,2,1:T(8,128)(2,1)}, bf16[256,4,4,128]{3,0,2,1:T(8,128)(2,1)}, u32[]{:S(2)}, u32[]{:S(2)}) collective-permute-start(bf16[256,4,4,128]{3,0,2,1:T(8,128)(2,1)} %copy.237), channel_id=1, source_target_pairs={{4,0},{8,4},{12,8},{16,12},{20,16},{24,20},{28,24},{0,28},{5,1},{9... | collective-permute-start | bytes 3145736 | tf_op jit(solution)/shard_map/while/body/eval_jaxpr/ppermute | solution.py:18
  1215.2 15.4 collective-permute-start.2
  1220.9 21.0 collective-permute-start.3
  1220.9 32.1 %collective-permute-start = (bf16[256,4,4,128]{3,0,2,1:T(8,128)(2,1)S(1)}, bf16[256,4,4,128]{3,0,2,1:T(8,128)(2,1)}, u32[]{:S(2)}, u32[]{:S(2)}) collective-permute-start(bf16[256,4,4,128]{3,0,2,1:T(8,128)(2,1)S(1)} %copy.236), channel_id=1, source_target_pairs={{4,0},{8,4},{12,8},{16,12},{20,16},{24,20},{28,24},{0,28},{5,1},{9... | collective-permute-start | bytes 3145736 | tf_op jit(solution)/shard_map/while/body/eval_jaxpr/ppermute | solution.py:18
  1220.9 43.4 %collective-permute-start.1 = (bf16[256,4,4,128]{3,0,2,1:T(8,128)(2,1)}, bf16[256,4,4,128]{3,0,2,1:T(8,128)(2,1)}, u32[]{:S(2)}, u32[]{:S(2)}) collective-permute-start(bf16[256,4,4,128]{3,0,2,1:T(8,128)(2,1)} %copy.237), channel_id=1, source_target_pairs={{4,0},{8,4},{12,8},{16,12},{20,16},{24,20},{28,24},{0,28},{5,1},{9... | collective-permute-start | bytes 3145736 | tf_op jit(solution)/shard_map/while/body/eval_jaxpr/ppermute | solution.py:18
  1277.2 15.4 collective-permute-start.2
  1282.9 21.0 collective-permute-start.3
  1282.9 32.1 %collective-permute-start = (bf16[256,4,4,128]{3,0,2,1:T(8,128)(2,1)S(1)}, bf16[256,4,4,128]{3,0,2,1:T(8,128)(2,1)}, u32[]{:S(2)}, u32[]{:S(2)}) collective-permute-start(bf16[256,4,4,128]{3,0,2,1:T(8,128)(2,1)S(1)} %copy.236), channel_id=1, source_target_pairs={{4,0},{8,4},{12,8},{16,12},{20,16},{24,20},{28,24},{0,28},{5,1},{9... | collective-permute-start | bytes 3145736 | tf_op jit(solution)/shard_map/while/body/eval_jaxpr/ppermute | solution.py:18
  1282.9 43.4 %collective-permute-start.1 = (bf16[256,4,4,128]{3,0,2,1:T(8,128)(2,1)}, bf16[256,4,4,128]{3,0,2,1:T(8,128)(2,1)}, u32[]{:S(2)}, u32[]{:S(2)}) collective-permute-start(bf16[256,4,4,128]{3,0,2,1:T(8,128)(2,1)} %copy.237), channel_id=1, source_target_pairs={{4,0},{8,4},{12,8},{16,12},{20,16},{24,20},{28,24},{0,28},{5,1},{9... | collective-permute-start | bytes 3145736 | tf_op jit(solution)/shard_map/while/body/eval_jaxpr/ppermute | solution.py:18
  1339.2 15.4 collective-permute-start.2
  1344.9 21.0 collective-permute-start.3
  1344.9 32.1 %collective-permute-start = (bf16[256,4,4,128]{3,0,2,1:T(8,128)(2,1)S(1)}, bf16[256,4,4,128]{3,0,2,1:T(8,128)(2,1)}, u32[]{:S(2)}, u32[]{:S(2)}) collective-permute-start(bf16[256,4,4,128]{3,0,2,1:T(8,128)(2,1)S(1)} %copy.236), channel_id=1, source_target_pairs={{4,0},{8,4},{12,8},{16,12},{20,16},{24,20},{28,24},{0,28},{5,1},{9... | collective-permute-start | bytes 3145736 | tf_op jit(solution)/shard_map/while/body/eval_jaxpr/ppermute | solution.py:18
  1345.0 43.4 %collective-permute-start.1 = (bf16[256,4,4,128]{3,0,2,1:T(8,128)(2,1)}, bf16[256,4,4,128]{3,0,2,1:T(8,128)(2,1)}, u32[]{:S(2)}, u32[]{:S(2)}) collective-permute-start(bf16[256,4,4,128]{3,0,2,1:T(8,128)(2,1)} %copy.237), channel_id=1, source_target_pairs={{4,0},{8,4},{12,8},{16,12},{20,16},{24,20},{28,24},{0,28},{5,1},{9... | collective-permute-start | bytes 3145736 | tf_op jit(solution)/shard_map/while/body/eval_jaxpr/ppermute | solution.py:18
  1401.2 15.4 collective-permute-start.2
  1406.9 21.0 collective-permute-start.3
  1406.9 32.1 %collective-permute-start = (bf16[256,4,4,128]{3,0,2,1:T(8,128)(2,1)S(1)}, bf16[256,4,4,128]{3,0,2,1:T(8,128)(2,1)}, u32[]{:S(2)}, u32[]{:S(2)}) collective-permute-start(bf16[256,4,4,128]{3,0,2,1:T(8,128)(2,1)S(1)} %copy.236), channel_id=1, source_target_pairs={{4,0},{8,4},{12,8},{16,12},{20,16},{24,20},{28,24},{0,28},{5,1},{9... | collective-permute-start | bytes 3145736 | tf_op jit(solution)/shard_map/while/body/eval_jaxpr/ppermute | solution.py:18
  1407.0 43.4 %collective-permute-start.1 = (bf16[256,4,4,128]{3,0,2,1:T(8,128)(2,1)}, bf16[256,4,4,128]{3,0,2,1:T(8,128)(2,1)}, u32[]{:S(2)}, u32[]{:S(2)}) collective-permute-start(bf16[256,4,4,128]{3,0,2,1:T(8,128)(2,1)} %copy.237), channel_id=1, source_target_pairs={{4,0},{8,4},{12,8},{16,12},{20,16},{24,20},{28,24},{0,28},{5,1},{9... | collective-permute-start | bytes 3145736 | tf_op jit(solution)/shard_map/while/body/eval_jaxpr/ppermute | solution.py:18
  1463.2 15.4 collective-permute-start.2
  1468.9 21.0 collective-permute-start.3
  1469.0 32.1 %collective-permute-start = (bf16[256,4,4,128]{3,0,2,1:T(8,128)(2,1)S(1)}, bf16[256,4,4,128]{3,0,2,1:T(8,128)(2,1)}, u32[]{:S(2)}, u32[]{:S(2)}) collective-permute-start(bf16[256,4,4,128]{3,0,2,1:T(8,128)(2,1)S(1)} %copy.236), channel_id=1, source_target_pairs={{4,0},{8,4},{12,8},{16,12},{20,16},{24,20},{28,24},{0,28},{5,1},{9... | collective-permute-start | bytes 3145736 | tf_op jit(solution)/shard_map/while/body/eval_jaxpr/ppermute | solution.py:18
  1469.0 43.4 %collective-permute-start.1 = (bf16[256,4,4,128]{3,0,2,1:T(8,128)(2,1)}, bf16[256,4,4,128]{3,0,2,1:T(8,128)(2,1)}, u32[]{:S(2)}, u32[]{:S(2)}) collective-permute-start(bf16[256,4,4,128]{3,0,2,1:T(8,128)(2,1)} %copy.237), channel_id=1, source_target_pairs={{4,0},{8,4},{12,8},{16,12},{20,16},{24,20},{28,24},{0,28},{5,1},{9... | collective-permute-start | bytes 3145736 | tf_op jit(solution)/shard_map/while/body/eval_jaxpr/ppermute | solution.py:18
  1525.2 15.4 collective-permute-start.2
  1530.9 21.0 collective-permute-start.3
  1531.0 32.1 %collective-permute-start = (bf16[256,4,4,128]{3,0,2,1:T(8,128)(2,1)S(1)}, bf16[256,4,4,128]{3,0,2,1:T(8,128)(2,1)}, u32[]{:S(2)}, u32[]{:S(2)}) collective-permute-start(bf16[256,4,4,128]{3,0,2,1:T(8,128)(2,1)S(1)} %copy.236), channel_id=1, source_target_pairs={{4,0},{8,4},{12,8},{16,12},{20,16},{24,20},{28,24},{0,28},{5,1},{9... | collective-permute-start | bytes 3145736 | tf_op jit(solution)/shard_map/while/body/eval_jaxpr/ppermute | solution.py:18
  1531.0 43.4 %collective-permute-start.1 = (bf16[256,4,4,128]{3,0,2,1:T(8,128)(2,1)}, bf16[256,4,4,128]{3,0,2,1:T(8,128)(2,1)}, u32[]{:S(2)}, u32[]{:S(2)}) collective-permute-start(bf16[256,4,4,128]{3,0,2,1:T(8,128)(2,1)} %copy.237), channel_id=1, source_target_pairs={{4,0},{8,4},{12,8},{16,12},{20,16},{24,20},{28,24},{0,28},{5,1},{9... | collective-permute-start | bytes 3145736 | tf_op jit(solution)/shard_map/while/body/eval_jaxpr/ppermute | solution.py:18
  1587.3 15.4 collective-permute-start.2
  1593.0 21.0 collective-permute-start.3
  1593.0 32.1 %collective-permute-start = (bf16[256,4,4,128]{3,0,2,1:T(8,128)(2,1)S(1)}, bf16[256,4,4,128]{3,0,2,1:T(8,128)(2,1)}, u32[]{:S(2)}, u32[]{:S(2)}) collective-permute-start(bf16[256,4,4,128]{3,0,2,1:T(8,128)(2,1)S(1)} %copy.236), channel_id=1, source_target_pairs={{4,0},{8,4},{12,8},{16,12},{20,16},{24,20},{28,24},{0,28},{5,1},{9... | collective-permute-start | bytes 3145736 | tf_op jit(solution)/shard_map/while/body/eval_jaxpr/ppermute | solution.py:18
  1593.0 43.4 %collective-permute-start.1 = (bf16[256,4,4,128]{3,0,2,1:T(8,128)(2,1)}, bf16[256,4,4,128]{3,0,2,1:T(8,128)(2,1)}, u32[]{:S(2)}, u32[]{:S(2)}) collective-permute-start(bf16[256,4,4,128]{3,0,2,1:T(8,128)(2,1)} %copy.237), channel_id=1, source_target_pairs={{4,0},{8,4},{12,8},{16,12},{20,16},{24,20},{28,24},{0,28},{5,1},{9... | collective-permute-start | bytes 3145736 | tf_op jit(solution)/shard_map/while/body/eval_jaxpr/ppermute | solution.py:18
  1665.5 297.1 %reduce-scatter.16.cloned.1.call-start = ((), (), s32[]{:S(2)}) async-start(), calls=%async_computation.18 | async-start | bytes 2359296 | tf_op jit(solution)/shard_map/reduce_scatter | solution.py:410
  1673.3 291.0 %reduce-scatter.18.cloned.1.call-start = ((), (), s32[]{:S(2)}) async-start(), calls=%async_computation.19 | async-start | bytes 2359296 | tf_op jit(solution)/shard_map/reduce_scatter | solution.py:413
  1698.1 268.1 %reduce-scatter.20.cloned.1.call-start = ((), (), s32[]{:S(2)}) async-start(), calls=%async_computation.20 | async-start | bytes 2359296 | tf_op jit(solution)/shard_map/reduce_scatter | solution.py:416
  1705.6 262.4 %reduce-scatter.10.cloned.1.call-start = ((), (), s32[]{:S(2)}) async-start(), calls=%async_computation.13 | async-start | bytes 5242880 | tf_op jit(solution)/shard_map/reduce_scatter | solution.py:205
  1812.8 184.7 %reduce-scatter.12.cloned.1.call-start = ((), (), s32[]{:S(2)}) async-start(), calls=%async_computation.16 | async-start | bytes 5242880 | tf_op jit(solution)/shard_map/reduce_scatter | solution.py:384
  1837.6 280.4 %reduce-scatter.22.cloned.1.call-start = ((), (), s32[]{:S(2)}) async-start(), calls=%async_computation.22 | async-start | bytes 18874368 | tf_op jit(solution)/shard_map/reduce_scatter | solution.py:419
  1867.3 370.1 %reduce-scatter.24.cloned.1.call-start = ((), (), s32[]{:S(2)}) async-start(), calls=%async_computation.23 | async-start | bytes 18874368 | tf_op jit(solution)/shard_map/reduce_scatter | solution.py:422
  1902.3 454.4 %reduce-scatter.26.cloned.1.call-start = ((), (), s32[]{:S(2)}) async-start(), calls=%async_computation.24 | async-start | bytes 18874368 | tf_op jit(solution)/shard_map/reduce_scatter | solution.py:425
  1942.4 542.8 %all-reduce.12.cloned.1.call-start = ((), (), s32[]{:S(2)}) async-start(), calls=%async_computation.21 | async-start | bytes 262144 | tf_op jit(solution)/shard_map/psum | solution.py:429
  (203 other events, 3249.9 us)
Sparse Core Ops, SparseCore 0:
  10.2 83.4 all-gather.4
  123.1 53.3 all-gather.6
  179.0 55.9 all-gather.8
  237.0 80.7 all-gather.10
  320.6 153.4 all-reduce.7
  957.5 153.9 all-reduce.9
  1665.6 37.8 reduce-scatter.13
  1707.1 41.2 reduce-scatter.15
  1751.6 41.2 reduce-scatter.17
  1796.4 41.2 reduce-scatter.19
  1840.6 76.7 reduce-scatter.9
  1919.6 77.7 reduce-scatter.11
  2001.0 116.9 reduce-scatter.21
  2121.4 115.9 reduce-scatter.23
  2240.8 115.9 reduce-scatter.25
  2362.7 122.4 all-reduce.11
where the time goes:
time: 2510 us; the launch traced here: 2490 us
  waiting for transfers between devices  1100 us (44%)
  matrix products  552 us (22%)
  other arithmetic  415 us (17%)
  local copies, waits for them, and re-layouts  310 us (12%)
  blocking collectives  71.5 us (3%)
  starting transfers between devices  26.2 us (1%)
    ppermute x32, waiting for transfers between devices, shifted(): return lax.ppermute(block, axis, route)  268 us
    psum x1, waiting for transfers between devices, shards(): lax.psum(second_part.reshape(local_len, seq_count, model_width).astype(jn...  152 us
    psum x1, waiting for transfers between devices, shards(): lax.psum((attn_gain_part, query_gain_part, key_gain_part, ffn_gain_part,...  124 us
    reduce_scatter x1, waiting for transfers between devices, shards(): lax.psum_scatter(jnp.stack(up_grads).astype(jnp.bfloat16), 'sq', scatter_...  115 us
    reduce_scatter x1, waiting for transfers between devices, shards(): lax.psum_scatter(jnp.stack(down_grads).astype(jnp.bfloat16), 'sq', scatte...  115 us
    scatter-add x4, other arithmetic, shards(): second_part = second_part.at[slot_rows].add(input_term * slot_live[:, None])  95.1 us
    scatter-add x4, other arithmetic, shards(): mixture = mixture.at[slot_rows].add(slot_gate[:, None] * expert_out)  86.9 us
    all_gather x1, waiting for transfers between devices, shards(): lax.all_gather(inputs, 'tp', axis=2, tiled=True)  83 us
  transfers between devices with their start and end apart: 48, of which 42 were waited for; matrix products, arithmetic and copies ran while one was open for 25% of the time, Pallas kernels for 0%

commit v1 on v0

v1 whole, which is shorter than its diff:
```python
import functools

import jax
import jax.numpy as jnp
from jax import lax
from jax.experimental import pallas as pl
from jax.experimental.pallas import tpu as pltpu
from jax.sharding import PartitionSpec as P

HD = 128
EPSILON = 1e-05
ROTARY_BASE = 10000.0
NEGATIVE = -1e30
F32 = jnp.float32
BF16 = jnp.bfloat16
VMEM_LIMIT = 56 * 1024 * 1024
CHUNKS = 2
NT = (((1,), (1,)), ((), ()))
TN = (((0,), (0,)), ((), ()))
NN = (((1,), (0,)), ((), ()))


def dot(left, right, dims=NN):
    return lax.dot_general(left, right, dims, preferred_element_type=F32)


def pick(which, cases):
    return lax.select_n(which, *cases) if len(cases) > 1 else cases[0]


def shift(block, axis, distance):
    count = lax.axis_size(axis)
    return lax.ppermute(block, axis, [(i, (i + distance) % count) for i in range(count)])


def swap(block, axis, mask):
    return lax.ppermute(block, axis, [(i, i ^ mask) for i in range(lax.axis_size(axis))])


def gather_chain(block, axis):
    count, place = lax.axis_size(axis), lax.axis_index(axis)
    right, left = [block], [block]
    for t in range(1, count):
        right.append(lax.ppermute(right[-1], axis, [(i, i + 1) for i in range(t - 1, count - 1)]))
        left.append(lax.ppermute(left[-1], axis, [(i + 1, i) for i in range(count - t)]))
    return [
        pick(place, [right[p - f] if p >= f else left[f - p] for p in range(count)])
        for f in range(count)
    ]


def exchange(part_of, axis):
    count, place = lax.axis_size(axis), lax.axis_index(axis)
    got = [part_of(place)]
    for k in range(1, count):
        got.append(shift(part_of((place + k) % count), axis, k))
    return got


def exchange_sum(part_of, axis):
    total = None
    for part in exchange(part_of, axis):
        total = part.astype(F32) if total is None else total + part.astype(F32)
    return total


def exchange_ordered(part_of, axis):
    count, place = lax.axis_size(axis), lax.axis_index(axis)
    got = exchange(part_of, axis)
    return [pick(place, [got[(p - f) % count] for p in range(count)]) for f in range(count)]


def butterfly(value, axis):
    mask = 1
    while mask < lax.axis_size(axis):
        value = value + swap(value, axis, mask)
        mask *= 2
    return value


def block_of(array, index, size, axis):
    return lax.dynamic_slice_in_dim(array, index * size, size, axis)


def relative(array, axis_name, width):
    count, place = lax.axis_size(axis_name), lax.axis_index(axis_name)
    return [block_of(array, place ^ m, width, 1) for m in range(count)]


def reduce_blocks(rel, right):
    count = len(rel)
    width = rel[0].shape[1]
    if count == 1:
        return dot(rel[0], right, TN)
    odd = jnp.concatenate([rel[m] for m in range(1, count, 2)], axis=1)
    even = jnp.concatenate([rel[m] for m in range(0, count, 2)], axis=1)
    received = swap(dot(odd, right, TN).astype(BF16), "sq", 1)
    own = (dot(even, right, TN) + received.astype(F32)).astype(BF16)
    columns = right.shape[1]
    own = own.reshape(count // 2, width, columns)
    half = columns // 2
    results = []
    for part in range(2):
        blocks = own[:, :, part * half : (part + 1) * half]
        steps = [1 << b for b in range((count // 2).bit_length() - 1)]
        if part:
            steps = steps[::-1]
        kept = {m: blocks[m] for m in range(count // 2)}
        for number, step in enumerate(steps):
            give = sorted(m for m in kept if m & step)
            keep = sorted(m for m in kept if not m & step)
            got = swap(jnp.stack([kept[m] for m in give]), "sq", 2 * step)
            last = number == len(steps) - 1
            kept = {
                m: (kept[m].astype(F32) + got[i].astype(F32)).astype(F32 if last else BF16)
                for i, m in enumerate(keep)
            }
        results.append(kept[0])
    return jnp.concatenate(results, axis=1).astype(F32)


def attn_forward_kernel(slots, info, q_ref, *refs):
    kv_refs, (low_ref, full_ref, lse_ref), (top, total, accum) = (
        refs[:slots],
        refs[slots : slots + 3],
        refs[slots + 3 :],
    )
    rank = info[0]
    length = info[1 + pl.program_id(0)]
    queries = q_ref[0]
    size = queries.shape[0]
    top[...] = jnp.full(top.shape, NEGATIVE, F32)
    total[...] = jnp.zeros(total.shape, F32)
    accum[...] = jnp.zeros(accum.shape, F32)
    key_row = lax.broadcasted_iota(jnp.int32, (size, size), 0)
    query_col = lax.broadcasted_iota(jnp.int32, (size, size), 1)
    for slot in range(slots):
        block = rank ^ slot
        start = block * size

        @pl.when((block <= rank) & (start < length))
        def _(slot=slot, start=start):
            scores = dot(kv_refs[slot][0, 0], queries, NT) * HD**-0.5
            allowed = key_row + start < length
            if slot == 0:
                allowed = allowed & (key_row <= query_col)
            scores = jnp.where(allowed, scores, NEGATIVE)
            newest = jnp.maximum(top[...], jnp.max(scores, axis=0, keepdims=True))
            weights = jnp.exp(scores - newest)
            factor = jnp.exp(top[...] - newest)
            top[...] = newest
            total[...] = total[...] * factor + jnp.sum(weights, axis=0, keepdims=True)
            accum[...] = accum[...] * factor + dot(
                kv_refs[slot][1, 0], weights.astype(BF16), TN
            )

    result = (accum[...] / total[...]).T
    full_ref[0] = result
    low_ref[0] = result.astype(BF16)
    lse_ref[0, 0] = top[...] + jnp.log(total[...])


def attn_forward(info, queries, kv_slots):
    seqs, size, columns = queries.shape
    heads = columns // HD
    slots = len(kv_slots)
    row_spec = pl.BlockSpec((1, size, HD), lambda s, h, info: (s, 0, h))
    kv_spec = pl.BlockSpec((2, 1, size, HD), lambda s, h, info: (0, s, 0, h))
    lse_spec = pl.BlockSpec((1, 1, 1, size), lambda s, h, info: (s, h, 0, 0))
    return pl.pallas_call(
        functools.partial(attn_forward_kernel, slots),
        grid_spec=pltpu.PrefetchScalarGridSpec(
            num_scalar_prefetch=1,
            grid=(seqs, heads),
            in_specs=[row_spec] + [kv_spec] * slots,
            out_specs=[row_spec, row_spec, lse_spec],
            scratch_shapes=[
                pltpu.VMEM((1, size), F32),
                pltpu.VMEM((1, size), F32),
                pltpu.VMEM((HD, size), F32),
            ],
        ),
        out_shape=[
            jax.ShapeDtypeStruct(queries.shape, BF16),
            jax.ShapeDtypeStruct(queries.shape, F32),
            jax.ShapeDtypeStruct((seqs, heads, 1, size), F32),
        ],
        compiler_params=pltpu.CompilerParams(vmem_limit_bytes=VMEM_LIMIT),
        cost_estimate=pl.CostEstimate(
            flops=4 * seqs * heads * slots * size * size * HD,
            bytes_accessed=4 * seqs * size * columns * (slots + 2),
            transcendentals=seqs * heads * slots * size * size,
        ),
        name="attn_forward",
    )(info, queries, *kv_slots)


def attn_backward_kernel(slots, info, q_ref, grad_ref, full_ref, lse_ref, *refs):
    kv_refs, (dq_ref, even_ref, odd_ref), (accum,) = (
        refs[:slots],
        refs[slots : slots + 3],
        refs[slots + 3 :],
    )
    rank = info[0]
    length = info[1 + pl.program_id(0)]
    queries, grads = q_ref[0], grad_ref[0]
    size = queries.shape[0]
    lse = lse_ref[0, 0]
    delta = jnp.sum((grads.astype(F32) * full_ref[0]).T, axis=0, keepdims=True)
    accum[...] = jnp.zeros(accum.shape, F32)
    key_row = lax.broadcasted_iota(jnp.int32, (size, size), 0)
    query_col = lax.broadcasted_iota(jnp.int32, (size, size), 1)
    for slot in range(slots):
        block = rank ^ slot
        start = block * size
        out_ref = odd_ref if slot % 2 else even_ref
        live = (block <= rank) & (start < length)

        @pl.when(live)
        def _(slot=slot, start=start, out_ref=out_ref):
            keys, values = kv_refs[slot][0, 0], kv_refs[slot][1, 0]
            scores = dot(keys, queries, NT) * HD**-0.5
            allowed = key_row + start < length
            if slot == 0:
                allowed = allowed & (key_row <= query_col)
            weights = jnp.where(allowed, jnp.exp(scores - lse), 0.0)
            back = dot(values, grads, NT)
            score_grad = (weights * (back - delta)).astype(BF16)
            out_ref[slot // 2, 1, 0] = dot(weights.astype(BF16), grads).astype(BF16)
            out_ref[slot // 2, 0, 0] = (dot(score_grad, queries) * HD**-0.5).astype(BF16)
            accum[...] += dot(score_grad, keys, TN)

        @pl.when(jnp.logical_not(live))
        def _(slot=slot, out_ref=out_ref):
            out_ref[slot // 2, :, 0] = jnp.zeros((2,) + queries.shape, BF16)

    dq_ref[0] = (accum[...] * HD**-0.5).astype(BF16)


def attn_backward(info, queries, grads, full, lse, kv_slots):
    seqs, size, columns = queries.shape
    heads = columns // HD
    slots = len(kv_slots)
    row_spec = pl.BlockSpec((1, size, HD), lambda s, h, info: (s, 0, h))
    kv_spec = pl.BlockSpec((2, 1, size, HD), lambda s, h, info: (0, s, 0, h))
    lse_spec = pl.BlockSpec((1, 1, 1, size), lambda s, h, info: (s, h, 0, 0))
    out_spec = pl.BlockSpec((slots // 2, 2, 1, size, HD), lambda s, h, info: (0, 0, s, 0, h))
    out_shape = jax.ShapeDtypeStruct((slots // 2, 2, seqs, size, columns), BF16)
    return pl.pallas_call(
        functools.partial(attn_backward_kernel, slots),
        grid_spec=pltpu.PrefetchScalarGridSpec(
            num_scalar_prefetch=1,
            grid=(seqs, heads),
            in_specs=[row_spec, row_spec, row_spec, lse_spec] + [kv_spec] * slots,
            out_specs=[row_spec, out_spec, out_spec],
            scratch_shapes=[pltpu.VMEM((size, HD), F32)],
        ),
        out_shape=[jax.ShapeDtypeStruct(queries.shape, BF16), out_shape, out_shape],
        compiler_params=pltpu.CompilerParams(vmem_limit_bytes=VMEM_LIMIT),
        cost_estimate=pl.CostEstimate(
            flops=10 * seqs * heads * slots * size * size * HD,
            bytes_accessed=8 * seqs * size * columns * (slots + 2),
            transcendentals=seqs * heads * slots * size * size,
        ),
        name="attn_backward",
    )(info, queries, grads, full, lse, *kv_slots)


def expert_hidden_kernel(
    tile, x_ref, g_ref, gate_ref, wg_ref, wu_ref, wd_ref, gh_ref, gp_ref, up_ref, gg_ref
):
    expert, block = pl.program_id(0), pl.program_id(1)
    rows = x_ref.shape[0]

    @pl.when((expert == 0) & (block == 0))
    def _():
        gg_ref[...] = jnp.zeros(gg_ref.shape, F32)

    @pl.loop(0, rows // tile)
    def _(i):
        span = pl.ds(pl.multiple_of(i * tile, tile), tile)
        tokens = x_ref[span, :]
        gate_pre = dot(tokens, wg_ref[0])
        up_pre = dot(tokens, wu_ref[0])
        back = dot(g_ref[span, :], wd_ref[0], NT)
        gates = gate_ref[span, :]
        lane = lax.broadcasted_iota(jnp.int32, gates.shape, 1)
        gate = jnp.sum(jnp.where(lane == expert, gates, 0.0), axis=1, keepdims=True)
        sigmoid = 1.0 / (1.0 + jnp.exp(-gate_pre))
        silu = gate_pre * sigmoid
        hidden = silu * up_pre
        inner = jnp.sum(hidden * back, axis=1, keepdims=True)
        gg_ref[span, :] += jnp.where(lane == expert, inner, 0.0)
        gh_ref[span, :] = (gate * hidden).astype(BF16)
        hidden_grad = gate * back
        gp_ref[span, :] = (
            hidden_grad * up_pre * (sigmoid + silu * (1.0 - sigmoid))
        ).astype(BF16)
        up_ref[span, :] = (hidden_grad * silu).astype(BF16)


def expert_hidden(tokens, grads, gates, w_gate, w_up, w_down):
    rows, width = tokens.shape
    experts, _, units = w_gate.shape
    cols = min(256, units)
    tile = min(512, rows)
    whole = pl.BlockSpec((rows, width), lambda e, f: (0, 0), pipeline_mode=pl.Buffered(1))
    small = pl.BlockSpec((rows, experts), lambda e, f: (0, 0))
    wide = pl.BlockSpec((1, width, cols), lambda e, f: (e, 0, f))
    tall = pl.BlockSpec((1, cols, width), lambda e, f: (e, f, 0))
    result = pl.BlockSpec((rows, cols), lambda e, f: (0, e * (units // cols) + f))
    out = jax.ShapeDtypeStruct((rows, experts * units), BF16)
    return pl.pallas_call(
        functools.partial(expert_hidden_kernel, tile),
        grid=(experts, units // cols),
        in_specs=[whole, whole, small, wide, wide, tall],
        out_specs=[result, result, result, small],
        out_shape=[out, out, out, jax.ShapeDtypeStruct((rows, experts), F32)],
        compiler_params=pltpu.CompilerParams(vmem_limit_bytes=VMEM_LIMIT),
        cost_estimate=pl.CostEstimate(
            flops=6 * rows * width * experts * units,
            bytes_accessed=6 * width * experts * units + 6 * rows * experts * units,
            transcendentals=rows * experts * units,
        ),
        name="expert_hidden",
    )(tokens, grads, gates, w_gate, w_up, w_down)


def expert_back_kernel(gp_ref, up_ref, lg_ref, router_ref, wg_ref, wu_ref, out_ref, accum):
    expert = pl.program_id(1)

    @pl.when(expert == 0)
    def _():
        accum[...] = lax.dot_general(
            lg_ref[...],
            router_ref[...].astype(F32),
            NT,
            precision=lax.Precision.HIGHEST,
            preferred_element_type=F32,
        )

    accum[...] += dot(gp_ref[...], wg_ref[0], NT) + dot(up_ref[...], wu_ref[0], NT)

    @pl.when(expert == pl.num_programs(1) - 1)
    def _():
        out_ref[...] = accum[...].astype(BF16)


def expert_back(gate_grads, up_grads, logit_grads, router, w_gate, w_up):
    rows = gate_grads.shape[0]
    experts, width, units = w_gate.shape
    total = router.shape[1]
    cols = min(512, width)
    left = pl.BlockSpec((rows, units), lambda d, e: (0, e))
    weight = pl.BlockSpec((1, cols, units), lambda d, e: (e, d, 0))
    return pl.pallas_call(
        expert_back_kernel,
        grid=(width // cols, experts),
        in_specs=[
            left,
            left,
            pl.BlockSpec((rows, total), lambda d, e: (0, 0)),
            pl.BlockSpec((cols, total), lambda d, e: (d, 0)),
            weight,
            weight,
        ],
        out_specs=pl.BlockSpec((rows, cols), lambda d, e: (0, d)),
        out_shape=jax.ShapeDtypeStruct((rows, width), BF16),
        scratch_shapes=[pltpu.VMEM((rows, cols), F32)],
        compiler_params=pltpu.CompilerParams(vmem_limit_bytes=VMEM_LIMIT),
        cost_estimate=pl.CostEstimate(
            flops=4 * rows * width * experts * units,
            bytes_accessed=4 * width * experts * units + 20 * rows * experts * units,
            transcendentals=0,
        ),
        name="expert_back",
    )(gate_grads, up_grads, logit_grads, router, w_gate, w_up)


def rotary_tables(positions):
    exponent = jnp.arange(HD // 2, dtype=F32) * 2.0 / HD
    frequency = ROTARY_BASE ** (-exponent)
    angles = positions.astype(F32)[:, None] * frequency[None, :]
    cosine = jnp.concatenate([jnp.cos(angles), jnp.cos(angles)], axis=-1)
    sine = jnp.concatenate([jnp.sin(angles), jnp.sin(angles)], axis=-1)
    return cosine, sine


def rotate_forward(values, cosine, sine):
    half = HD // 2
    turned = jnp.concatenate([-values[..., half:], values[..., :half]], axis=-1)
    return values * cosine[None, :, None, :] + turned * sine[None, :, None, :]


def rotate_backward(grads, cosine, sine):
    half = HD // 2
    scaled = grads * sine[None, :, None, :]
    turned = jnp.concatenate([scaled[..., half:], -scaled[..., :half]], axis=-1)
    return grads * cosine[None, :, None, :] + turned


def gather_sq(block):
    count = lax.axis_size("sq")
    slots = [None] * count
    for m in range(0, count, 2):
        slots[m] = block if m == 0 else swap(block, "sq", m)
    for m in range(0, count, 2):
        if count > 1:
            slots[m + 1] = swap(slots[m], "sq", 1)
    return slots


def scatter_sq(even, odd):
    received = swap(odd, "sq", 1)
    total = None
    for k in range(even.shape[0]):
        part = (even[k].astype(F32) + received[k].astype(F32)).astype(BF16)
        part = part if k == 0 else swap(part, "sq", 2 * k)
        total = part.astype(F32) if total is None else total + part.astype(F32)
    return total


def shards(
    inputs,
    lengths,
    routes,
    attn_gain,
    w_query,
    w_key,
    w_value,
    query_gain,
    key_gain,
    w_out,
    ffn_gain,
    router,
    w_gate,
    w_up,
    w_down,
    cotangent,
):
    size, seqs, feat = inputs.shape
    width, head_cols = w_query.shape
    heads = head_cols // HD
    tp_rank, tp_count = lax.axis_index("tp"), lax.axis_size("tp")
    sq_rank, sq_count = lax.axis_index("sq"), lax.axis_size("sq")
    experts = w_gate.shape[0]
    experts_total = router.shape[1]
    all_cols = head_cols * tp_count
    block = width // sq_count
    chunks = CHUNKS
    per = seqs // chunks
    rows_n = per * size
    quarter = rows_n // tp_count
    positions = sq_rank * size + jnp.arange(size, dtype=jnp.int32)
    cosine, sine = rotary_tables(positions)
    group = lambda array: [
        array[:, c * per : (c + 1) * per].transpose(1, 0, 2) for c in range(chunks)
    ]
    inputs_c, cotangent_c, routes_c = group(inputs), group(cotangent), group(routes)
    info_c = [
        jnp.concatenate([sq_rank[None], lengths[c * per : (c + 1) * per]]).astype(jnp.int32)
        for c in range(chunks)
    ]

    slab = w_out.shape[0] // sq_count
    w_out_all = lax.all_gather(
        block_of(w_out, sq_rank, slab, 0), ("tp", "sq"), axis=0, tiled=True
    )

    w_qkv = jnp.concatenate([w_query, w_key, w_value], axis=1)

    def attention_in(c):
        pieces = gather_chain(inputs_c[c].reshape(rows_n, feat), "tp")
        low = jnp.concatenate(pieces, axis=1)
        rows = low.astype(F32)
        inv = lax.rsqrt(jnp.mean(rows * rows, axis=1, keepdims=True) + EPSILON)
        normed = (rows * inv * attn_gain).astype(BF16)
        qkv = dot(normed, w_qkv)
        query_raw, key_raw = qkv[:, :head_cols], qkv[:, head_cols : 2 * head_cols]
        value = qkv[:, 2 * head_cols :].astype(BF16)
        squares = jnp.stack(
            [jnp.sum(query_raw * query_raw, axis=1), jnp.sum(key_raw * key_raw, axis=1)]
        )
        squares = butterfly(squares, "tp")
        inv_qk = lax.rsqrt(squares / all_cols + EPSILON)
        query_hat = query_raw * inv_qk[0][:, None]
        key_hat = key_raw * inv_qk[1][:, None]
        shape = (per, size, heads, HD)
        turn = lambda hat, gain: (
            rotate_forward((hat * gain).reshape(shape), cosine, sine)
            .astype(BF16)
            .reshape(per, size, head_cols)
        )
        queries = turn(query_hat, query_gain)
        keys = turn(key_hat, key_gain)
        pair = jnp.stack([keys, value.reshape(per, size, head_cols)])
        return low, inv, normed, query_raw, key_raw, inv_qk, queries, pair

    ins = [attention_in(c) for c in range(chunks)]
    slots_c = [gather_sq(ins[c][7]) for c in range(chunks)]
    attn_c = [attn_forward(info_c[c], ins[c][6], slots_c[c]) for c in range(chunks)]

    grad_c = [
        jnp.concatenate(gather_chain(cotangent_c[c].reshape(rows_n, feat), "tp"), axis=1)
        for c in range(chunks)
    ]

    def middle_of(c):
        low = ins[c][0]
        attn_all = jnp.concatenate(
            gather_chain(attn_c[c][0].reshape(rows_n, head_cols), "tp"), axis=1
        )
        middle = low.astype(F32) + dot(attn_all, w_out_all)
        inv = lax.rsqrt(jnp.mean(middle * middle, axis=1, keepdims=True) + EPSILON)
        ffn_in = (middle * inv * ffn_gain).astype(BF16)
        probs = jax.nn.softmax(dot(ffn_in, router), axis=1)
        flat_routes = routes_c[c].reshape(rows_n, -1)
        ids = jnp.arange(experts_total, dtype=jnp.int32)
        routed = functools.reduce(
            jnp.logical_or,
            [flat_routes[:, r : r + 1] == ids[None, :] for r in range(flat_routes.shape[1])],
        )
        gates = jnp.where(routed, probs, 0.0)
        own = block_of(gates, tp_rank, experts, 1)
        return attn_all, middle, inv, ffn_in, probs, routed, own

    mids = [middle_of(c) for c in range(chunks)]

    def expert_part(c):
        _, _, _, ffn_in, probs, routed, own = mids[c]
        hidden, gate_grads, up_grads, inner = expert_hidden(
            ffn_in, grad_c[c], own, w_gate, w_up, w_down
        )
        inner = lax.dynamic_update_slice_in_dim(
            jnp.zeros(probs.shape, F32), inner, tp_rank * experts, 1
        )
        prob_grad = jnp.where(routed, inner, 0.0)
        logit_grad = probs * (prob_grad - jnp.sum(probs * prob_grad, axis=1, keepdims=True))
        back = expert_back(gate_grads, up_grads, logit_grad, router, w_gate, w_up)
        return hidden, gate_grads, up_grads, logit_grad, back

    exps = [expert_part(c) for c in range(chunks)]

    def middle_back(c):
        attn_all, middle, inv, _, _, _, _ = mids[c]
        back = exps[c][4]
        ffn_grad = exchange_sum(lambda d: block_of(back, d, quarter, 0), "tp")
        own_middle = block_of(middle, tp_rank, quarter, 0)
        own_inv = block_of(inv, tp_rank, quarter, 0)
        own_grad = block_of(grad_c[c], tp_rank, quarter, 0).astype(F32)
        hat = own_middle * own_inv
        gained = ffn_grad * ffn_gain
        gain_part = jnp.sum(ffn_grad * hat, axis=0)
        middle_grad = own_grad + own_inv * (
            gained - hat * jnp.mean(gained * hat, axis=1, keepdims=True)
        )
        low = middle_grad.astype(BF16)
        attn_grad = dot(low, w_out_all, NT).astype(BF16)
        parts = exchange_ordered(lambda d: block_of(attn_grad, d, head_cols, 1), "tp")
        attn_grad = jnp.concatenate(parts, axis=0).reshape(per, size, head_cols)
        parts = exchange_ordered(lambda d: block_of(low, d, feat, 1), "tp")
        middle_own = jnp.concatenate(parts, axis=0)
        return gain_part, low, attn_grad, middle_own, block_of(attn_all, tp_rank, quarter, 0)

    backs = [middle_back(c) for c in range(chunks)]

    def output_of(c):
        hidden = exps[c][0]
        mixture = dot(hidden, w_down.reshape(-1, width)).astype(BF16)
        total = exchange_sum(lambda d: block_of(mixture, d, feat, 1), "tp")
        own = block_of(mids[c][1], tp_rank, feat, 1)
        return (own + total).astype(BF16).reshape(per, size, feat).transpose(1, 0, 2)

    outputs = [output_of(c) for c in range(chunks)]

    join = lambda parts: parts[0] if len(parts) == 1 else jnp.concatenate(parts, axis=0)
    ffn_all = join([mids[c][3] for c in range(chunks)])
    grad_all = join(grad_c)
    ffn_rel = relative(ffn_all, "sq", block)
    grad_rel = relative(grad_all, "sq", block)
    w_gate_grad = reduce_blocks(ffn_rel, join([exps[c][1] for c in range(chunks)]))
    w_up_grad = reduce_blocks(ffn_rel, join([exps[c][2] for c in range(chunks)]))
    w_down_grad = reduce_blocks(grad_rel, join([exps[c][0] for c in range(chunks)]))
    spread = lambda g: g.reshape(block, experts, -1).transpose(1, 0, 2)
    w_gate_grad, w_up_grad = spread(w_gate_grad), spread(w_up_grad)
    w_down_grad = w_down_grad.T.reshape(experts, -1, block)

    logit_all = join([exps[c][3] for c in range(chunks)])
    router_grad = lax.dot_general(
        logit_all,
        ffn_all.astype(F32),
        TN,
        precision=lax.Precision.HIGHEST,
        preferred_element_type=F32,
    )

    low_rel = relative(join([b[1] for b in backs]), "sq", block)
    out_grad = reduce_blocks(low_rel, join([b[4] for b in backs])).astype(BF16)
    w_out_grad = exchange_sum(lambda d: block_of(out_grad, d, head_cols, 1), "tp").T

    def attention_back(c):
        low, inv, normed, query_raw, key_raw, inv_qk, queries, _ = ins[c]
        _, full, lse = attn_c[c]
        dq, even, odd = attn_backward(info_c[c], queries, backs[c][2], full, lse, slots_c[c])
        dkv = scatter_sq(even, odd).astype(BF16)
        shape = (per, size, heads, HD)
        turn = lambda grad: rotate_backward(
            grad.astype(F32).reshape(shape), cosine, sine
        ).reshape(rows_n, head_cols)
        query_grad, key_grad = turn(dq), turn(dkv[0])
        value_grad = dkv[1].reshape(rows_n, head_cols)
        query_hat = query_raw * inv_qk[0][:, None]
        key_hat = key_raw * inv_qk[1][:, None]
        gained_q, gained_k = query_grad * query_gain, key_grad * key_gain
        stats = jnp.stack(
            [jnp.sum(gained_q * query_hat, axis=1), jnp.sum(gained_k * key_hat, axis=1)]
        )
        stats = butterfly(stats, "tp") / all_cols
        raw_q = (inv_qk[0][:, None] * (gained_q - query_hat * stats[0][:, None])).astype(BF16)
        raw_k = (inv_qk[1][:, None] * (gained_k - key_hat * stats[1][:, None])).astype(BF16)
        gain_q = jnp.sum(query_grad * query_hat, axis=0)
        gain_k = jnp.sum(key_grad * key_hat, axis=0)
        raw = jnp.concatenate([raw_q, raw_k, value_grad], axis=1)
        first = dot(raw, w_qkv, NT)
        hat = low.astype(F32) * inv
        gain_part = jnp.sum(first * hat, axis=0)
        inner = jnp.sum(first * attn_gain * hat, axis=1)
        inner = butterfly(inner, "tp")
        first_low = first.astype(BF16)
        first_own = exchange_sum(lambda d: block_of(first_low, d, feat, 1), "tp")
        hat_own = inputs_c[c].reshape(rows_n, feat).astype(F32) * inv
        gain_own = block_of(attn_gain, tp_rank, feat, 0)
        result = backs[c][3].astype(F32) + inv * (
            gain_own * first_own - hat_own * inner[:, None] / width
        )
        result = result.reshape(per, size, feat).transpose(1, 0, 2)
        return result, raw, gain_q, gain_k, gain_part

    fronts = [attention_back(c) for c in range(chunks)]
    normed_rel = relative(join([ins[c][2] for c in range(chunks)]), "sq", block)
    qkv_grad = reduce_blocks(normed_rel, join([f[1] for f in fronts]))

    tally = lambda parts: functools.reduce(lambda a, b: a + b, parts)
    place = lambda part: lax.dynamic_update_slice_in_dim(
        jnp.zeros((all_cols,), F32), part, tp_rank * head_cols, 0
    )
    early = jnp.concatenate(
        [router_grad, tally([b[0] for b in backs])[None, :]], axis=0
    )
    early = butterfly(butterfly(early, "sq"), "tp")
    late = jnp.stack(
        [
            tally([f[4] for f in fronts]),
            place(tally([f[2] for f in fronts])),
            place(tally([f[3] for f in fronts])),
        ]
    )
    late = butterfly(butterfly(late, "sq"), "tp")
    joined = lambda parts: parts[0] if len(parts) == 1 else jnp.concatenate(parts, axis=1)
    return (
        joined(outputs),
        joined([f[0] for f in fronts]),
        late[0],
        qkv_grad[:, :head_cols],
        qkv_grad[:, head_cols : 2 * head_cols],
        qkv_grad[:, 2 * head_cols :],
        late[1],
        late[2],
        w_out_grad,
        early[experts_total],
        early[:experts_total].T,
        w_gate_grad,
        w_up_grad,
        w_down_grad,
    )


def solution(mesh):
    placed = (
        P("sq", None, "tp"),
        P(),
        P("sq", None, None),
        P(),
        P(None, "tp"),
        P(None, "tp"),
        P(None, "tp"),
        P("tp"),
        P("tp"),
        P("tp", None),
        P(),
        P(),
        P("tp", None, None),
        P("tp", None, None),
        P("tp", None, None),
        P("sq", None, "tp"),
    )
    return jax.shard_map(
        shards,
        mesh=mesh,
        in_specs=placed,
        out_specs=(
            P("sq", None, "tp"),
            P("sq", None, "tp"),
            P(),
            P("sq", "tp"),
            P("sq", "tp"),
            P("sq", "tp"),
            P(),
            P(),
            P("tp", "sq"),
            P(),
            P(),
            P("tp", "sq", None),
            P("tp", "sq", None),
            P("tp", None, "sq"),
        ),
        check_vma=False,
    )
```

time: 2510 us -> 1660 us (0.66)
  waiting for transfers between devices: 1100 us -> 635 us
  matrix products: 552 us -> 193 us
  starting transfers between devices: 26.2 us -> 267 us
  other arithmetic: 415 us -> 192 us
  Pallas kernels: 0 us -> 191 us
  local copies, waits for them, and re-layouts: 310 us -> 150 us
  blocking collectives: 71.5 us -> 0 us
    ppermute x32 -> x138, waiting for transfers between devices: 268 us -> 635 us  [the longest x69 393 us: swap(): lax.ppermute(block, axis, [(i, i ^ mask) for i in range(lax.axis_size(axi...]
    dot_general x93 -> x23, matrix products: 552 us -> 193 us  [the longest x22 191 us: dot(): return lax.dot_general(left, right, dims, preferred_element_type=F32)]
    psum x3 -> x0, waiting for transfers between devices: 357 us -> none  [the longest x1 152 us: shards(): lax.psum(second_part.reshape(local_len, seq_count, model_width).astype(jn...]
    reduce_scatter x9 -> x0, waiting for transfers between devices: 329 us -> none  [the longest x1 115 us: shards(): lax.psum_scatter(jnp.stack(up_grads).astype(jnp.bfloat16), 'sq', scatter_...]
    ppermute x32 -> x138, starting transfers between devices: 23.4 us -> 267 us  [the longest x69 152 us: swap(): lax.ppermute(block, axis, [(i, i ^ mask) for i in range(lax.axis_size(axi...]
    scatter-add x12 -> x0, other arithmetic: 213 us -> none  [the longest x4 95.1 us: shards(): second_part = second_part.at[slot_rows].add(input_term * slot_live[:, None])]
    pallas_call x0 -> x8, Pallas kernels: none -> 191 us  [the longest x2 74.2 us: expert_hidden(): pl.pallas_call(functools.partial(expert_hidden_kernel, tile), grid=(exper...]
    all_gather x4 -> x1, waiting for transfers between devices: 147 us -> 0.02 us  [shards(): lax.all_gather(block_of(w_out, sq_rank, slab, 0), ('tp', 'sq'), axis=0, t...]
  transfers between devices with their start and end apart: 48 -> 139, of which waited for: 42 -> 51; matrix products, arithmetic and copies ran while one was open for 25% -> 29% of each run, Pallas kernels for 0% -> 3%
where the time goes in v1:
time: 1660 us; the launch traced here: 1650 us
  waiting for transfers between devices  635 us (38%)
  starting transfers between devices  267 us (16%)
  matrix products  193 us (12%)
  other arithmetic  192 us (12%)
  Pallas kernels  191 us (12%)
  local copies, waits for them, and re-layouts  150 us (9%)
  between operations  18 us (1%)
    ppermute x69, waiting for transfers between devices, swap(): lax.ppermute(block, axis, [(i, i ^ mask) for i in range(lax.axis_size(axi...  393 us
    dot_general x22, matrix products, dot(): return lax.dot_general(left, right, dims, preferred_element_type=F32)  191 us
    ppermute x69, starting transfers between devices, swap(): lax.ppermute(block, axis, [(i, i ^ mask) for i in range(lax.axis_size(axi...  152 us
    ppermute x33, waiting for transfers between devices, shift(): lax.ppermute(block, axis, [(i, (i + distance) % count) for i in range(cou...  133 us
    ppermute x18, waiting for transfers between devices, gather_chain(): lax.ppermute(left[-1], axis, [(i + 1, i) for i in range(count - t)])  104 us
    pallas_call x2, Pallas kernels, expert_hidden(): pl.pallas_call(functools.partial(expert_hidden_kernel, tile), grid=(exper...  74.2 us
    pallas_call x2, Pallas kernels, expert_back(): pl.pallas_call(expert_back_kernel, grid=(width // cols, experts), in_spec...  71 us
    unnamed x427, local copies, waits for them, and re-layouts  66.5 us
  transfers between devices with their start and end apart: 139, of which 51 were waited for; matrix products, arithmetic and copies ran while one was open for 29% of the time, Pallas kernels for 3%

profile of v1, /device:TPU:0, one launch (start us, length us, event | category | flops | bytes accessed | tf_op | source)
XLA Modules:
  0.0 1645.6 jit_solution(12762527521822242311)
XLA Ops:
  43.6 34.6 %collective-permute-done.34 = bf16[512,512]{1,0:T(8,128)(2,1)} collective-permute-done((bf16[512,512]{1,0:T(8,128)(2,1)}, bf16[512,512]{1,0:T(8,128)(2,1)}, u32[]{:S(2)}, u32[]{:S(2)}) %collective-permute-start.34) | collective-permute-done | bytes 524320 | tf_op jit(solution)/shard_map/ppermute | solution.py:45
  80.5 22.4 %collective-permute-done.4 = bf16[512,512]{1,0:T(8,128)(2,1)S(1)} collective-permute-done((bf16[512,512]{1,0:T(8,128)(2,1)}, bf16[512,512]{1,0:T(8,128)(2,1)S(1)}, u32[]{:S(2)}, u32[]{:S(2)}) %collective-permute-start.4) | collective-permute-done | bytes 524320 | tf_op jit(solution)/shard_map/ppermute | solution.py:45
  110.5 12.7 collective-permute-done.35
  136.0 9.7 collective-permute-done.5
  211.4 17.8 %collective-permute-done.43.refs_6_ = bf16[2,2,256,512]{3,2,1,0:T(8,128)(2,1)} collective-permute-done((bf16[2,2,256,512]{3,2,1,0:T(8,128)(2,1)S(1)}, bf16[2,2,256,512]{3,2,1,0:T(8,128)(2,1)}, u32[]{:S(2)}, u32[]{:S(2)}) %collective-permute-start.43) | collective-permute-done | bytes 1048608 | tf_op jit(solution)/shard_map/ppermute | solution.py:37
  230.9 20.8 %collective-permute-done.41.refs_4_ = bf16[2,2,256,512]{3,2,1,0:T(8,128)(2,1)} collective-permute-done((bf16[2,2,256,512]{3,2,1,0:T(8,128)(2,1)S(1)}, bf16[2,2,256,512]{3,2,1,0:T(8,128)(2,1)}, u32[]{:S(2)}, u32[]{:S(2)}) %collective-permute-start.41) | collective-permute-done | bytes 1048608 | tf_op jit(solution)/shard_map/ppermute | solution.py:37
  256.7 17.4 %collective-permute-done.13.refs_6_ = bf16[2,2,256,512]{3,2,1,0:T(8,128)(2,1)} collective-permute-done((bf16[2,2,256,512]{3,2,1,0:T(8,128)(2,1)}, bf16[2,2,256,512]{3,2,1,0:T(8,128)(2,1)}, u32[]{:S(2)}, u32[]{:S(2)}) %collective-permute-start.13) | collective-permute-done | bytes 1048608 | tf_op jit(solution)/shard_map/ppermute | solution.py:37
  274.2 17.3 %collective-permute-done.11.refs_4_ = bf16[2,2,256,512]{3,2,1,0:T(8,128)(2,1)} collective-permute-done((bf16[2,2,256,512]{3,2,1,0:T(8,128)(2,1)}, bf16[2,2,256,512]{3,2,1,0:T(8,128)(2,1)}, u32[]{:S(2)}, u32[]{:S(2)}) %collective-permute-start.11) | collective-permute-done | bytes 1048608 | tf_op jit(solution)/shard_map/ppermute | solution.py:37
  319.3 10.3 attn_forward.2
  331.6 10.3 attn_forward.3
  368.7 28.0 %maximum_maximum_fusion = bf16[1024,2048]{1,0:T(8,128)(2,1)S(1)} fusion(bf16[512,512]{1,0:T(8,128)(2,1)S(1)} %get-tuple-element.209, bf16[512,512]{1,0:T(8,128)(2,1)S(1)} %get-tuple-element.208, bf16[512,512]{1,0:T(8,128)(2,1)S(1)} %get-tuple-element.207, bf16[512,512]{1,0:T(8,128)(2,1)S(1)} %get-tuple-element.206, ...), kind=kLoop, calls=%fused_computation.63 | loop fusion | flops 33554432 | bytes 8388608 | tf_op jit(solution)/shard_map/concatenate | solution.py:576
  413.4 11.2 collective-permute-done.50
  428.4 9.0 multiply_reduce_fusion.1
  451.1 37.0 %expert_hidden.3 = (bf16[512,4096]{1,0:T(8,128)(2,1)}, bf16[512,4096]{1,0:T(8,128)(2,1)}, bf16[512,4096]{1,0:T(8,128)(2,1)}, f32[512,4]{1,0:T(8,128)}) custom-call(bf16[512,2048]{1,0:T(8,128)(2,1)} %copy-done.4, bf16[512,2048]{1,0:T(8,128)(2,1)} %pad_maximum_fusion.7.g_ref, f32[512,4]{1,0:T(8,128)} %dynamic-slice_select_fusion.gate_ref, ...), custom_call_target="tpu_custom_call" | custom-call | flops 25769803776 | bytes 62914560 | tf_op jit(solution)/shard_map/expert_hidden/pallas_call | solution.py:313
  492.6 37.1 %expert_hidden.2 = (bf16[512,4096]{1,0:T(8,128)(2,1)}, bf16[512,4096]{1,0:T(8,128)(2,1)}, bf16[512,4096]{1,0:T(8,128)(2,1)}, f32[512,4]{1,0:T(8,128)}) custom-call(bf16[512,2048]{1,0:T(8,128)(2,1)} %copy-done.2, bf16[512,2048]{1,0:T(8,128)(2,1)} %pad_maximum_fusion.4.g_ref, f32[512,4]{1,0:T(8,128)} %dynamic-slice_select_fusion.1.gate_ref, ...), custom_call_target="tpu_custom_call" | custom-call | flops 25769803776 | bytes 62914560 | tf_op jit(solution)/shard_map/expert_hidden/pallas_call | solution.py:313
  540.0 35.4 %expert_back.2 = bf16[512,2048]{1,0:T(8,128)(2,1)} custom-call(bf16[512,4096]{1,0:T(8,128)(2,1)} %get-tuple-element.38.gp_ref, bf16[512,4096]{1,0:T(8,128)(2,1)} %get-tuple-element.39.up_ref, f32[512,16]{1,0:T(8,128)} %copy-done.106, bf16[2048,16]{1,0:T(8,128)(2,1)} %copy.94.router_ref, bf16[4,2048,1024]{2,1,0:T(8,128)(2,1)} %wg_ref.7, ...), custom_call_target="tpu_custom_call" | custom-call | flops 17179869184 | bytes 75497472 | tf_op jit(solution)/shard_map/expert_back/pallas_call | solution.py:356
  575.4 35.6 %expert_back.3 = bf16[512,2048]{1,0:T(8,128)(2,1)} custom-call(bf16[512,4096]{1,0:T(8,128)(2,1)} %get-tuple-element.46.gp_ref, bf16[512,4096]{1,0:T(8,128)(2,1)} %get-tuple-element.47.up_ref, f32[512,16]{1,0:T(8,128)} %copy-done.105, bf16[2048,16]{1,0:T(8,128)(2,1)} %copy.94.router_ref, bf16[4,2048,1024]{2,1,0:T(8,128)(2,1)} %wg_ref.7, ...), custom_call_target="tpu_custom_call" | custom-call | flops 17179869184 | bytes 75497472 | tf_op jit(solution)/shard_map/expert_back/pallas_call | solution.py:356
  622.6 12.7 convolution_convert_fusion.5
  635.3 14.3 convolution_convert_fusion.6
  655.7 14.9 convolution_convert_fusion.2
  670.6 15.3 convolution_convert_fusion.1
  693.0 36.4 %collective-permute-done.61 = bf16[128,2048]{1,0:T(8,128)(2,1)S(1)} collective-permute-done((bf16[128,2048]{1,0:T(8,128)(2,1)S(1)}, bf16[128,2048]{1,0:T(8,128)(2,1)S(1)}, u32[]{:S(2)}, u32[]{:S(2)}) %collective-permute-start.61) | collective-permute-done | bytes 524320 | tf_op jit(solution)/shard_map/ppermute | solution.py:33
  748.5 12.8 attn_backward.2
  784.2 12.9 attn_backward.3
  804.6 15.1 convolution_convert_fusion
  820.0 17.9 %collective-permute-start.119 = (f32[17,2048]{1,0:T(8,128)S(1)}, f32[17,2048]{1,0:T(8,128)S(1)}, u32[]{:S(2)}, u32[]{:S(2)}) collective-permute-start(f32[17,2048]{1,0:T(8,128)S(1)} %fusion.165), channel_id=1, source_target_pairs={{0,8},{4,12},{8,0},{12,4},{16,24},{20,28},{24,16},{28,20},{1,9},{5... | collective-permute-start | bytes 417800 | tf_op jit(solution)/shard_map/ppermute | solution.py:37
  872.4 32.8 %collective-permute-start.120 = (f32[17,2048]{1,0:T(8,128)S(1)}, f32[17,2048]{1,0:T(8,128)S(1)}, u32[]{:S(2)}, u32[]{:S(2)}) collective-permute-start(f32[17,2048]{1,0:T(8,128)S(1)} %add.823), channel_id=1, source_target_pairs={{0,16},{4,20},{8,24},{12,28},{16,0},{20,4},{24,8},{28,12},{1,17},{... | collective-permute-start | bytes 417800 | tf_op jit(solution)/shard_map/ppermute | solution.py:37
  905.2 16.9 %collective-permute-start.70 = (bf16[2,2,256,512]{3,2,1,0:T(8,128)(2,1)}, bf16[2,2,256,512]{3,2,1,0:T(8,128)(2,1)}, u32[]{:S(2)}, u32[]{:S(2)}) collective-permute-start(bf16[2,2,256,512]{3,2,1,0:T(8,128)(2,1)} %get-tuple-element.126), channel_id=1, source_target_pairs={{0,8},{4,12},{8,0},{12,4},{16,24},{20,28},{24,16},{28,20},{1,9},{5... | collective-permute-start | bytes 3145736 | tf_op jit(solution)/shard_map/ppermute | solution.py:37
  937.4 25.4 %collective-permute-start.72 = (bf16[2,2,256,512]{3,2,1,0:T(8,128)(2,1)}, bf16[2,2,256,512]{3,2,1,0:T(8,128)(2,1)S(1)}, u32[]{:S(2)}, u32[]{:S(2)}) collective-permute-start(bf16[2,2,256,512]{3,2,1,0:T(8,128)(2,1)} %get-tuple-element.127), channel_id=1, source_target_pairs={{0,24},{4,28},{8,16},{12,20},{16,8},{20,12},{24,0},{28,4},{1,25},{... | collective-permute-start | bytes 3145736 | tf_op jit(solution)/shard_map/ppermute | solution.py:37
  980.7 13.0 collective-permute-done.72
  993.7 18.1 %collective-permute-done.71 = bf16[2,2,256,512]{3,2,1,0:T(8,128)(2,1)} collective-permute-done((bf16[2,2,256,512]{3,2,1,0:T(8,128)(2,1)}, bf16[2,2,256,512]{3,2,1,0:T(8,128)(2,1)}, u32[]{:S(2)}, u32[]{:S(2)}) %collective-permute-start.71) | collective-permute-done | bytes 1048608 | tf_op jit(solution)/shard_map/ppermute | solution.py:37
  1017.3 19.0 %collective-permute-done.92 = bf16[2,2,256,512]{3,2,1,0:T(8,128)(2,1)} collective-permute-done((bf16[2,2,256,512]{3,2,1,0:T(8,128)(2,1)}, bf16[2,2,256,512]{3,2,1,0:T(8,128)(2,1)}, u32[]{:S(2)}, u32[]{:S(2)}) %collective-permute-start.92) | collective-permute-done | bytes 1048608 | tf_op jit(solution)/shard_map/ppermute | solution.py:37
  1036.4 15.4 collective-permute-done.91
  1092.7 10.5 fusion.11
  1127.0 8.8 collective-permute-done.101
  1177.2 9.8 collective-permute-done.77
  1189.5 30.4 %collective-permute-done.76 = bf16[512,512]{1,0:T(8,128)(2,1)S(1)} collective-permute-done((bf16[512,512]{1,0:T(8,128)(2,1)S(1)}, bf16[512,512]{1,0:T(8,128)(2,1)S(1)}, u32[]{:S(2)}, u32[]{:S(2)}) %collective-permute-start.76) | collective-permute-done | bytes 524320 | tf_op jit(solution)/shard_map/ppermute | solution.py:33
  1234.9 19.0 %collective-permute-done.96 = bf16[512,512]{1,0:T(8,128)(2,1)S(1)} collective-permute-done((bf16[512,512]{1,0:T(8,128)(2,1)S(1)}, bf16[512,512]{1,0:T(8,128)(2,1)S(1)}, u32[]{:S(2)}, u32[]{:S(2)}) %collective-permute-start.96) | collective-permute-done | bytes 524320 | tf_op jit(solution)/shard_map/ppermute | solution.py:33
  1262.5 14.3 add_convert_fusion.1
  1277.1 18.8 %add_convert_fusion = bf16[1024,4096]{1,0:T(8,128)(2,1)} fusion(bf16[1024,4096]{1,0:T(8,128)(2,1)} %collective-permute-done.133, bf16[1024,4096]{1,0:T(8,128)(2,1)} %constant_dynamic-update-slice_fusion.9, bf16[1024,256]{1,0:T(8,128)(2,1)S(1)} %copy-done.117, bf16[1024,256]{1,0:T(8,128)(2,1)S(1)} %copy-done.116, bf16[1024,256]{1,0:T(8,128)(2,1)S(1)} %copy-done.115, ...), kind=kOutput, calls=%fused_computation | convolution fusion | flops 8610906112 | bytes 27262976 | tf_op jit(solution)/shard_map/dot_general | solution.py:24
  1306.7 14.6 add_convert_fusion.2
  1321.4 9.1 add_convert_fusion.4
  1356.8 60.1 %collective-permute-done.106 = bf16[2,256,768]{2,1,0:T(8,128)(2,1)} collective-permute-done((bf16[2,256,768]{2,1,0:T(8,128)(2,1)}, bf16[2,256,768]{2,1,0:T(8,128)(2,1)}, u32[]{:S(2)}, u32[]{:S(2)}) %collective-permute-start.106) | collective-permute-done | bytes 786464 | tf_op jit(solution)/shard_map/ppermute | solution.py:37
  1454.6 14.2 collective-permute-done.124
  1470.7 20.3 %collective-permute-done.126 = bf16[2,256,2048]{1,2,0:T(8,128)(2,1)S(1)} collective-permute-done((bf16[2,256,2048]{1,2,0:T(8,128)(2,1)}, bf16[2,256,2048]{1,2,0:T(8,128)(2,1)S(1)}, u32[]{:S(2)}, u32[]{:S(2)}) %collective-permute-start.126) | collective-permute-done | bytes 2097184 | tf_op jit(solution)/shard_map/ppermute | solution.py:37
  1493.4 51.0 %collective-permute-done.107 = bf16[1,256,768]{2,1,0:T(8,128)(2,1)S(1)} collective-permute-done((bf16[1,256,768]{2,1,0:T(8,128)(2,1)S(1)}, bf16[1,256,768]{2,1,0:T(8,128)(2,1)S(1)}, u32[]{:S(2)}, u32[]{:S(2)}) %collective-permute-start.107) | collective-permute-done | bytes 393248 | tf_op jit(solution)/shard_map/ppermute | solution.py:37
  1550.1 39.3 %collective-permute-done.135 = bf16[1,256,2048]{2,1,0:T(8,128)(2,1)S(1)} collective-permute-done((bf16[1,256,2048]{2,1,0:T(8,128)(2,1)S(1)}, bf16[1,256,2048]{2,1,0:T(8,128)(2,1)S(1)}, u32[]{:S(2)}, u32[]{:S(2)}) %collective-permute-start.135) | collective-permute-done | bytes 1048608 | tf_op jit(solution)/shard_map/ppermute | solution.py:37
  1598.7 8.8 collective-permute-done.125
  (926 shorter events, 638.9 us)
Async XLA Ops:
  7.2 421.2 %all-gather.2.cloned.1.call-start = ((), (), s32[]{:S(2)}) async-start(), calls=%async_computation | async-start | bytes 8650752 | tf_op jit(solution)/shard_map/all_gather | solution.py:466
  27.6 99.9 %collective-permute-start.54 = (bf16[512,512]{1,0:T(8,128)(2,1)S(1)}, bf16[512,512]{1,0:T(8,128)(2,1)}, u32[]{:S(2)}, u32[]{:S(2)}) collective-permute-start(bf16[512,512]{1,0:T(8,128)(2,1)S(1)} %bitcast.301), channel_id=1, source_target_pairs={{1,0},{2,1},{3,2},{5,4},{6,5},{7,6},{9,8},{10,9},{11,10},{13,12},{... | collective-permute-start | bytes 1572872 | tf_op jit(solution)/shard_map/ppermute | solution.py:45
  40.8 62.2 %collective-permute-start.4 = (bf16[512,512]{1,0:T(8,128)(2,1)}, bf16[512,512]{1,0:T(8,128)(2,1)S(1)}, u32[]{:S(2)}, u32[]{:S(2)}) collective-permute-start(bf16[512,512]{1,0:T(8,128)(2,1)} %collective-permute-done.3), channel_id=1, source_target_pairs={{1,0},{2,1},{5,4},{6,5},{9,8},{10,9},{13,12},{14,13},{17,16},{18,1... | collective-permute-start | bytes 1572872 | tf_op jit(solution)/shard_map/ppermute | solution.py:45
  42.9 66.3 %collective-permute-start.1 = (bf16[512,512]{1,0:T(8,128)(2,1)}, bf16[512,512]{1,0:T(8,128)(2,1)S(1)}, u32[]{:S(2)}, u32[]{:S(2)}) collective-permute-start(bf16[512,512]{1,0:T(8,128)(2,1)} %collective-permute-done), channel_id=1, source_target_pairs={{1,2},{2,3},{5,6},{6,7},{9,10},{10,11},{13,14},{14,15},{17,18},{18... | collective-permute-start | bytes 1572872 | tf_op jit(solution)/shard_map/ppermute | solution.py:44
  127.6 77.1 %collective-permute-start.21 = (bf16[512,512]{1,0:T(8,128)(2,1)}, bf16[512,512]{1,0:T(8,128)(2,1)}, u32[]{:S(2)}, u32[]{:S(2)}) collective-permute-start(bf16[512,512]{1,0:T(8,128)(2,1)} %bitcast.12), channel_id=1, source_target_pairs={{0,1},{1,2},{2,3},{4,5},{5,6},{6,7},{8,9},{9,10},{10,11},{12,13},{... | collective-permute-start | bytes 1572872 | tf_op jit(solution)/shard_map/ppermute | solution.py:44
  133.1 72.1 %collective-permute-start.55 = (bf16[512,512]{1,0:T(8,128)(2,1)}, bf16[512,512]{1,0:T(8,128)(2,1)}, u32[]{:S(2)}, u32[]{:S(2)}) collective-permute-start(bf16[512,512]{1,0:T(8,128)(2,1)} %collective-permute-done.54), channel_id=1, source_target_pairs={{1,0},{2,1},{5,4},{6,5},{9,8},{10,9},{13,12},{14,13},{17,16},{18,1... | collective-permute-start | bytes 1572872 | tf_op jit(solution)/shard_map/ppermute | solution.py:45
  134.6 71.0 %collective-permute-start.52 = (bf16[512,512]{1,0:T(8,128)(2,1)}, bf16[512,512]{1,0:T(8,128)(2,1)}, u32[]{:S(2)}, u32[]{:S(2)}) collective-permute-start(bf16[512,512]{1,0:T(8,128)(2,1)} %collective-permute-done.51), channel_id=1, source_target_pairs={{1,2},{2,3},{5,6},{6,7},{9,10},{10,11},{13,14},{14,15},{17,18},{18... | collective-permute-start | bytes 1572872 | tf_op jit(solution)/shard_map/ppermute | solution.py:44
  145.7 59.9 %collective-permute-start.25 = (bf16[512,512]{1,0:T(8,128)(2,1)}, bf16[512,512]{1,0:T(8,128)(2,1)}, u32[]{:S(2)}, u32[]{:S(2)}) collective-permute-start(bf16[512,512]{1,0:T(8,128)(2,1)} %collective-permute-done.24), channel_id=1, source_target_pairs={{1,0},{2,1},{5,4},{6,5},{9,8},{10,9},{13,12},{14,13},{17,16},{18,1... | collective-permute-start | bytes 1572872 | tf_op jit(solution)/shard_map/ppermute | solution.py:45
  208.8 65.4 %collective-permute-start.13 = (bf16[2,2,256,512]{3,2,1,0:T(8,128)(2,1)}, bf16[2,2,256,512]{3,2,1,0:T(8,128)(2,1)}, u32[]{:S(2)}, u32[]{:S(2)}) collective-permute-start(bf16[2,2,256,512]{3,2,1,0:T(8,128)(2,1)} %pad_maximum_fusion.16.refs_0_), channel_id=1, source_target_pairs={{0,24},{4,28},{8,16},{12,20},{16,8},{20,12},{24,0},{28,4},{1,25},{... | collective-permute-start | bytes 3145736 | tf_op jit(solution)/shard_map/ppermute | solution.py:37
  229.2 62.3 %collective-permute-start.11 = (bf16[2,2,256,512]{3,2,1,0:T(8,128)(2,1)}, bf16[2,2,256,512]{3,2,1,0:T(8,128)(2,1)}, u32[]{:S(2)}, u32[]{:S(2)}) collective-permute-start(bf16[2,2,256,512]{3,2,1,0:T(8,128)(2,1)} %pad_maximum_fusion.16.refs_0_), channel_id=1, source_target_pairs={{0,16},{4,20},{8,24},{12,28},{16,0},{20,4},{24,8},{28,12},{1,17},{... | collective-permute-start | bytes 3145736 | tf_op jit(solution)/shard_map/ppermute | solution.py:37
  613.5 75.8 %collective-permute-start.80 = (bf16[128,2048]{1,0:T(8,128)(2,1)S(1)}, bf16[128,2048]{1,0:T(8,128)(2,1)S(1)}, u32[]{:S(2)}, u32[]{:S(2)}) collective-permute-start(bf16[128,2048]{1,0:T(8,128)(2,1)S(1)} %get-tuple-element.185), channel_id=1, source_target_pairs={{0,1},{1,2},{2,3},{3,0},{4,5},{5,6},{6,7},{7,4},{8,9},{9,10},{10,1... | collective-permute-start | bytes 1572872 | tf_op jit(solution)/shard_map/ppermute | solution.py:33
  613.8 79.1 %collective-permute-start.82 = (bf16[128,2048]{1,0:T(8,128)(2,1)}, bf16[128,2048]{1,0:T(8,128)(2,1)S(1)}, u32[]{:S(2)}, u32[]{:S(2)}) collective-permute-start(bf16[128,2048]{1,0:T(8,128)(2,1)} %get-tuple-element.186), channel_id=1, source_target_pairs={{0,3},{1,0},{2,1},{3,2},{4,7},{5,4},{6,5},{7,6},{8,11},{9,8},{10,9... | collective-permute-start | bytes 1572872 | tf_op jit(solution)/shard_map/ppermute | solution.py:33
  617.3 75.6 %collective-permute-start.81 = (bf16[128,2048]{1,0:T(8,128)(2,1)S(1)}, bf16[128,2048]{1,0:T(8,128)(2,1)S(1)}, u32[]{:S(2)}, u32[]{:S(2)}) collective-permute-start(bf16[128,2048]{1,0:T(8,128)(2,1)S(1)} %get-tuple-element.187), channel_id=1, source_target_pairs={{0,2},{1,3},{2,0},{3,1},{4,6},{5,7},{6,4},{7,5},{8,10},{9,11},{10,... | collective-permute-start | bytes 1572872 | tf_op jit(solution)/shard_map/ppermute | solution.py:33
  618.6 74.4 %collective-permute-start.60 = (bf16[128,2048]{1,0:T(8,128)(2,1)}, bf16[128,2048]{1,0:T(8,128)(2,1)S(1)}, u32[]{:S(2)}, u32[]{:S(2)}) collective-permute-start(bf16[128,2048]{1,0:T(8,128)(2,1)} %get-tuple-element.179), channel_id=1, source_target_pairs={{0,1},{1,2},{2,3},{3,0},{4,5},{5,6},{6,7},{7,4},{8,9},{9,10},{10,1... | collective-permute-start | bytes 1572872 | tf_op jit(solution)/shard_map/ppermute | solution.py:33
  619.4 73.6 %collective-permute-start.62 = (bf16[128,2048]{1,0:T(8,128)(2,1)}, bf16[128,2048]{1,0:T(8,128)(2,1)S(1)}, u32[]{:S(2)}, u32[]{:S(2)}) collective-permute-start(bf16[128,2048]{1,0:T(8,128)(2,1)} %get-tuple-element.180), channel_id=1, source_target_pairs={{0,3},{1,0},{2,1},{3,2},{4,7},{5,4},{6,5},{7,6},{8,11},{9,8},{10,9... | collective-permute-start | bytes 1572872 | tf_op jit(solution)/shard_map/ppermute | solution.py:33
  693.0 111.6 %collective-permute-start.57 = (bf16[512,512]{1,0:T(8,128)(2,1)}, bf16[512,512]{1,0:T(8,128)(2,1)}, u32[]{:S(2)}, u32[]{:S(2)}) collective-permute-start(bf16[512,512]{1,0:T(8,128)(2,1)} %get-tuple-element.191), channel_id=1, source_target_pairs={{0,1},{1,2},{2,3},{3,0},{4,5},{5,6},{6,7},{7,4},{8,9},{9,10},{10,1... | collective-permute-start | bytes 1572872 | tf_op jit(solution)/shard_map/ppermute | solution.py:33
  761.2 89.2 %collective-permute-start.69 = (bf16[4,2,2,256,512]{4,3,2,1,0:T(8,128)(2,1)}, bf16[4,2,2,256,512]{4,3,2,1,0:T(8,128)(2,1)}, u32[]{:S(2)}, u32[]{:S(2)}) collective-permute-start(bf16[4,2,2,256,512]{4,3,2,1,0:T(8,128)(2,1)} %get-tuple-element.45), channel_id=1, source_target_pairs={{0,4},{4,0},{8,12},{12,8},{16,20},{20,16},{24,28},{28,24},{1,5},{5... | collective-permute-start | bytes 12582920 | tf_op jit(solution)/shard_map/ppermute | solution.py:37
  797.1 165.9 %collective-permute-start.89 = (bf16[4,2,2,256,512]{4,3,2,1,0:T(8,128)(2,1)}, bf16[4,2,2,256,512]{4,3,2,1,0:T(8,128)(2,1)}, u32[]{:S(2)}, u32[]{:S(2)}) collective-permute-start(bf16[4,2,2,256,512]{4,3,2,1,0:T(8,128)(2,1)} %get-tuple-element.53), channel_id=1, source_target_pairs={{0,4},{4,0},{8,12},{12,8},{16,20},{20,16},{24,28},{28,24},{1,5},{5... | collective-permute-start | bytes 12582920 | tf_op jit(solution)/shard_map/ppermute | solution.py:37
  804.5 165.1 %collective-permute-start.110 = (bf16[1024,2048]{1,0:T(8,128)(2,1)}, bf16[1024,2048]{1,0:T(8,128)(2,1)}, u32[]{:S(2)}, u32[]{:S(2)}) collective-permute-start(bf16[1024,2048]{1,0:T(8,128)(2,1)} %convolution_convert_fusion.3), channel_id=1, source_target_pairs={{0,4},{4,0},{8,12},{12,8},{16,20},{20,16},{24,28},{28,24},{1,5},{5... | collective-permute-start | bytes 12582920 | tf_op jit(solution)/shard_map/ppermute | solution.py:37
  850.4 54.8 %collective-permute-start.28 = (bf16[512,512]{1,0:T(8,128)(2,1)S(1)}, bf16[512,512]{1,0:T(8,128)(2,1)S(1)}, u32[]{:S(2)}, u32[]{:S(2)}) collective-permute-start(bf16[512,512]{1,0:T(8,128)(2,1)S(1)} %get-tuple-element.190), channel_id=1, source_target_pairs={{0,2},{1,3},{2,0},{3,1},{4,6},{5,7},{6,4},{7,5},{8,10},{9,11},{10,... | collective-permute-start | bytes 1572872 | tf_op jit(solution)/shard_map/ppermute | solution.py:33
  862.8 61.5 %collective-permute-start.64 = (bf16[128,512]{1,0:T(8,128)(2,1)S(1)}, bf16[128,512]{1,0:T(8,128)(2,1)S(1)}, u32[]{:S(2)}, u32[]{:S(2)}) collective-permute-start(bf16[128,512]{1,0:T(8,128)(2,1)S(1)} %get-tuple-element.282), channel_id=1, source_target_pairs={{0,2},{1,3},{2,0},{3,1},{4,6},{5,7},{6,4},{7,5},{8,10},{9,11},{10,... | collective-permute-start | bytes 393224 | tf_op jit(solution)/shard_map/ppermute | solution.py:33
  872.4 53.9 %collective-permute-start.120 = (f32[17,2048]{1,0:T(8,128)S(1)}, f32[17,2048]{1,0:T(8,128)S(1)}, u32[]{:S(2)}, u32[]{:S(2)}) collective-permute-start(f32[17,2048]{1,0:T(8,128)S(1)} %add.823), channel_id=1, source_target_pairs={{0,16},{4,20},{8,24},{12,28},{16,0},{20,4},{24,8},{28,12},{1,17},{... | collective-permute-start | bytes 417800 | tf_op jit(solution)/shard_map/ppermute | solution.py:37
  905.2 66.4 %collective-permute-start.70 = (bf16[2,2,256,512]{3,2,1,0:T(8,128)(2,1)}, bf16[2,2,256,512]{3,2,1,0:T(8,128)(2,1)}, u32[]{:S(2)}, u32[]{:S(2)}) collective-permute-start(bf16[2,2,256,512]{3,2,1,0:T(8,128)(2,1)} %get-tuple-element.126), channel_id=1, source_target_pairs={{0,8},{4,12},{8,0},{12,4},{16,24},{20,28},{24,16},{28,20},{1,9},{5... | collective-permute-start | bytes 3145736 | tf_op jit(solution)/shard_map/ppermute | solution.py:37
  937.4 56.2 %collective-permute-start.72 = (bf16[2,2,256,512]{3,2,1,0:T(8,128)(2,1)}, bf16[2,2,256,512]{3,2,1,0:T(8,128)(2,1)S(1)}, u32[]{:S(2)}, u32[]{:S(2)}) collective-permute-start(bf16[2,2,256,512]{3,2,1,0:T(8,128)(2,1)} %get-tuple-element.127), channel_id=1, source_target_pairs={{0,24},{4,28},{8,16},{12,20},{16,8},{20,12},{24,0},{28,4},{1,25},{... | collective-permute-start | bytes 3145736 | tf_op jit(solution)/shard_map/ppermute | solution.py:37
  969.6 66.6 %collective-permute-start.92 = (bf16[2,2,256,512]{3,2,1,0:T(8,128)(2,1)}, bf16[2,2,256,512]{3,2,1,0:T(8,128)(2,1)}, u32[]{:S(2)}, u32[]{:S(2)}) collective-permute-start(bf16[2,2,256,512]{3,2,1,0:T(8,128)(2,1)} %get-tuple-element.130), channel_id=1, source_target_pairs={{0,24},{4,28},{8,16},{12,20},{16,8},{20,12},{24,0},{28,4},{1,25},{... | collective-permute-start | bytes 3145736 | tf_op jit(solution)/shard_map/ppermute | solution.py:37
  971.6 80.2 %collective-permute-start.91 = (bf16[2,2,256,512]{3,2,1,0:T(8,128)(2,1)}, bf16[2,2,256,512]{3,2,1,0:T(8,128)(2,1)}, u32[]{:S(2)}, u32[]{:S(2)}) collective-permute-start(bf16[2,2,256,512]{3,2,1,0:T(8,128)(2,1)} %get-tuple-element.131), channel_id=1, source_target_pairs={{0,16},{4,20},{8,24},{12,28},{16,0},{20,4},{24,8},{28,12},{1,17},{... | collective-permute-start | bytes 3145736 | tf_op jit(solution)/shard_map/ppermute | solution.py:37
  993.7 265.4 %collective-permute-start.128 = (bf16[1024,4096]{1,0:T(8,128)(2,1)}, bf16[1024,4096]{1,0:T(8,128)(2,1)}, u32[]{:S(2)}, u32[]{:S(2)}) collective-permute-start(bf16[1024,4096]{1,0:T(8,128)(2,1)} %convolution_convert_fusion.1), channel_id=1, source_target_pairs={{0,4},{4,0},{8,12},{12,8},{16,20},{20,16},{24,28},{28,24},{1,5},{5... | collective-permute-start | bytes 25165832 | tf_op jit(solution)/shard_map/ppermute | solution.py:37
  1011.8 265.1 %collective-permute-start.133 = (bf16[1024,4096]{1,0:T(8,128)(2,1)}, bf16[1024,4096]{1,0:T(8,128)(2,1)}, u32[]{:S(2)}, u32[]{:S(2)}) collective-permute-start(bf16[1024,4096]{1,0:T(8,128)(2,1)} %convolution_convert_fusion), channel_id=1, source_target_pairs={{0,4},{4,0},{8,12},{12,8},{16,20},{20,16},{24,28},{28,24},{1,5},{5... | collective-permute-start | bytes 25165832 | tf_op jit(solution)/shard_map/ppermute | solution.py:37
  1017.3 86.0 %collective-permute-start.84 = (bf16[128,512]{1,0:T(8,128)(2,1)}, bf16[128,512]{1,0:T(8,128)(2,1)}, u32[]{:S(2)}, u32[]{:S(2)}) collective-permute-start(bf16[128,512]{1,0:T(8,128)(2,1)} %get-tuple-element.288), channel_id=1, source_target_pairs={{0,2},{1,3},{2,0},{3,1},{4,6},{5,7},{6,4},{7,5},{8,10},{9,11},{10,... | collective-permute-start | bytes 393224 | tf_op jit(solution)/shard_map/ppermute | solution.py:33
  1036.2 70.9 %collective-permute-start.85 = (bf16[128,512]{1,0:T(8,128)(2,1)}, bf16[128,512]{1,0:T(8,128)(2,1)}, u32[]{:S(2)}, u32[]{:S(2)}) collective-permute-start(bf16[128,512]{1,0:T(8,128)(2,1)} %get-tuple-element.289), channel_id=1, source_target_pairs={{0,3},{1,0},{2,1},{3,2},{4,7},{5,4},{6,5},{7,6},{8,11},{9,8},{10,9... | collective-permute-start | bytes 393224 | tf_op jit(solution)/shard_map/ppermute | solution.py:33
  1160.6 145.6 %collective-permute-start.123 = (bf16[1024,4096]{1,0:T(8,128)(2,1)}, bf16[1024,4096]{1,0:T(8,128)(2,1)}, u32[]{:S(2)}, u32[]{:S(2)}) collective-permute-start(bf16[1024,4096]{1,0:T(8,128)(2,1)} %convolution_convert_fusion.2), channel_id=1, source_target_pairs={{0,4},{4,0},{8,12},{12,8},{16,20},{20,16},{24,28},{28,24},{1,5},{5... | collective-permute-start | bytes 25165832 | tf_op jit(solution)/shard_map/ppermute | solution.py:37
  1234.9 86.5 %collective-permute-start.105 = (bf16[1024,1536]{1,0:T(8,128)(2,1)}, bf16[1024,1536]{1,0:T(8,128)(2,1)}, u32[]{:S(2)}, u32[]{:S(2)}) collective-permute-start(bf16[1024,1536]{1,0:T(8,128)(2,1)} %convolution_convert_fusion.4), channel_id=1, source_target_pairs={{0,4},{4,0},{8,12},{12,8},{16,20},{20,16},{24,28},{28,24},{1,5},{5... | collective-permute-start | bytes 9437192 | tf_op jit(solution)/shard_map/ppermute | solution.py:37
  1253.8 79.8 %collective-permute-start.115 = (bf16[256,512]{0,1:T(8,128)(2,1)}, bf16[256,512]{0,1:T(8,128)(2,1)S(1)}, u32[]{:S(2)}, u32[]{:S(2)}) collective-permute-start(bf16[256,512]{0,1:T(8,128)(2,1)} %get-tuple-element.224), channel_id=1, source_target_pairs={{0,1},{1,2},{2,3},{3,0},{4,5},{5,6},{6,7},{7,4},{8,9},{9,10},{10,1... | collective-permute-start | bytes 786440 | tf_op jit(solution)/shard_map/ppermute | solution.py:33
  1259.1 76.4 %collective-permute-start.116 = (bf16[256,512]{0,1:T(8,128)(2,1)}, bf16[256,512]{0,1:T(8,128)(2,1)}, u32[]{:S(2)}, u32[]{:S(2)}) collective-permute-start(bf16[256,512]{0,1:T(8,128)(2,1)} %get-tuple-element.225), channel_id=1, source_target_pairs={{0,2},{1,3},{2,0},{3,1},{4,6},{5,7},{6,4},{7,5},{8,10},{9,11},{10,... | collective-permute-start | bytes 786440 | tf_op jit(solution)/shard_map/ppermute | solution.py:33
  1276.9 76.9 %collective-permute-start.117 = (bf16[256,512]{0,1:T(8,128)(2,1)}, bf16[256,512]{0,1:T(8,128)(2,1)}, u32[]{:S(2)}, u32[]{:S(2)}) collective-permute-start(bf16[256,512]{0,1:T(8,128)(2,1)} %get-tuple-element.226), channel_id=1, source_target_pairs={{0,3},{1,0},{2,1},{3,2},{4,7},{5,4},{6,5},{7,6},{8,11},{9,8},{10,9... | collective-permute-start | bytes 786440 | tf_op jit(solution)/shard_map/ppermute | solution.py:33
  1306.2 138.7 %collective-permute-start.134 = (bf16[2,256,2048]{2,1,0:T(8,128)(2,1)}, bf16[2,256,2048]{2,1,0:T(8,128)(2,1)}, u32[]{:S(2)}, u32[]{:S(2)}) collective-permute-start(bf16[2,256,2048]{2,1,0:T(8,128)(2,1)} %pad_maximum_fusion.13), channel_id=1, source_target_pairs={{0,8},{4,12},{8,0},{12,4},{16,24},{20,28},{24,16},{28,20},{1,9},{5... | collective-permute-start | bytes 6291464 | tf_op jit(solution)/shard_map/ppermute | solution.py:37
  1333.6 115.7 %collective-permute-start.129 = (bf16[2,256,2048]{1,2,0:T(8,128)(2,1)}, bf16[2,256,2048]{1,2,0:T(8,128)(2,1)}, u32[]{:S(2)}, u32[]{:S(2)}) collective-permute-start(bf16[2,256,2048]{1,2,0:T(8,128)(2,1)} %pad_maximum_fusion.12), channel_id=1, source_target_pairs={{0,8},{4,12},{8,0},{12,4},{16,24},{20,28},{24,16},{28,20},{1,9},{5... | collective-permute-start | bytes 6291464 | tf_op jit(solution)/shard_map/ppermute | solution.py:37
  1335.5 81.5 %collective-permute-start.106 = (bf16[2,256,768]{2,1,0:T(8,128)(2,1)}, bf16[2,256,768]{2,1,0:T(8,128)(2,1)}, u32[]{:S(2)}, u32[]{:S(2)}) collective-permute-start(bf16[2,256,768]{2,1,0:T(8,128)(2,1)} %pad_maximum_fusion.27), channel_id=1, source_target_pairs={{0,8},{4,12},{8,0},{12,4},{16,24},{20,28},{24,16},{28,20},{1,9},{5... | collective-permute-start | bytes 2359304 | tf_op jit(solution)/shard_map/ppermute | solution.py:37
  1350.5 102.4 %collective-permute-start.131 = (bf16[2,256,2048]{1,2,0:T(8,128)(2,1)}, bf16[2,256,2048]{1,2,0:T(8,128)(2,1)}, u32[]{:S(2)}, u32[]{:S(2)}) collective-permute-start(bf16[2,256,2048]{1,2,0:T(8,128)(2,1)} %copy.143), channel_id=1, source_target_pairs={{0,16},{4,20},{8,24},{12,28},{16,0},{20,4},{24,8},{28,12},{1,17},{... | collective-permute-start | bytes 6291464 | tf_op jit(solution)/shard_map/ppermute | solution.py:37
  1353.8 88.4 %collective-permute-start.109 = (bf16[1,256,768]{2,1,0:T(8,128)(2,1)}, bf16[1,256,768]{2,1,0:T(8,128)(2,1)S(1)}, u32[]{:S(2)}, u32[]{:S(2)}) collective-permute-start(bf16[1,256,768]{2,1,0:T(8,128)(2,1)} %add_convert_fusion.39), channel_id=1, source_target_pairs={{0,8},{4,12},{8,0},{12,4},{16,24},{20,28},{24,16},{28,20},{1,9},{5... | collective-permute-start | bytes 1179656 | tf_op jit(solution)/shard_map/ppermute | solution.py:37
  1417.0 51.8 %collective-permute-start.124 = (bf16[2,256,2048]{1,2,0:T(8,128)(2,1)}, bf16[2,256,2048]{1,2,0:T(8,128)(2,1)}, u32[]{:S(2)}, u32[]{:S(2)}) collective-permute-start(bf16[2,256,2048]{1,2,0:T(8,128)(2,1)} %pad_maximum_fusion.11), channel_id=1, source_target_pairs={{0,8},{4,12},{8,0},{12,4},{16,24},{20,28},{24,16},{28,20},{1,9},{5... | collective-permute-start | bytes 6291464 | tf_op jit(solution)/shard_map/ppermute | solution.py:37
  1444.9 103.1 %collective-permute-start.136 = (bf16[2,256,2048]{2,1,0:T(8,128)(2,1)}, bf16[2,256,2048]{2,1,0:T(8,128)(2,1)S(1)}, u32[]{:S(2)}, u32[]{:S(2)}) collective-permute-start(bf16[2,256,2048]{2,1,0:T(8,128)(2,1)} %stack.120), channel_id=1, source_target_pairs={{0,16},{4,20},{8,24},{12,28},{16,0},{20,4},{24,8},{28,12},{1,17},{... | collective-permute-start | bytes 6291464 | tf_op jit(solution)/shard_map/ppermute | solution.py:37
  1449.3 95.1 %collective-permute-start.107 = (bf16[1,256,768]{2,1,0:T(8,128)(2,1)S(1)}, bf16[1,256,768]{2,1,0:T(8,128)(2,1)S(1)}, u32[]{:S(2)}, u32[]{:S(2)}) collective-permute-start(bf16[1,256,768]{2,1,0:T(8,128)(2,1)S(1)} %get-tuple-element.165), channel_id=1, source_target_pairs={{0,16},{4,20},{8,24},{12,28},{16,0},{20,4},{24,8},{28,12},{1,17},{... | collective-permute-start | bytes 1179656 | tf_op jit(solution)/shard_map/ppermute | solution.py:37
  1452.8 142.6 %collective-permute-start.130 = (bf16[1,256,2048]{1,2,0:T(8,128)(2,1)S(1)}, bf16[1,256,2048]{1,2,0:T(8,128)(2,1)S(1)}, u32[]{:S(2)}, u32[]{:S(2)}) collective-permute-start(bf16[1,256,2048]{1,2,0:T(8,128)(2,1)S(1)} %add_convert_fusion.11), channel_id=1, source_target_pairs={{0,16},{4,20},{8,24},{12,28},{16,0},{20,4},{24,8},{28,12},{1,17},{... | collective-permute-start | bytes 3145736 | tf_op jit(solution)/shard_map/ppermute | solution.py:37
  1468.8 128.2 %collective-permute-start.132 = (bf16[1,256,2048]{1,2,0:T(8,128)(2,1)S(1)}, bf16[1,256,2048]{1,2,0:T(8,128)(2,1)S(1)}, u32[]{:S(2)}, u32[]{:S(2)}) collective-permute-start(bf16[1,256,2048]{1,2,0:T(8,128)(2,1)S(1)} %add_convert_fusion.9), channel_id=1, source_target_pairs={{0,8},{4,12},{8,0},{12,4},{16,24},{20,28},{24,16},{28,20},{1,9},{5... | collective-permute-start | bytes 3145736 | tf_op jit(solution)/shard_map/ppermute | solution.py:37
  1491.1 98.3 %collective-permute-start.135 = (bf16[1,256,2048]{2,1,0:T(8,128)(2,1)S(1)}, bf16[1,256,2048]{2,1,0:T(8,128)(2,1)S(1)}, u32[]{:S(2)}, u32[]{:S(2)}) collective-permute-start(bf16[1,256,2048]{2,1,0:T(8,128)(2,1)S(1)} %add_convert_fusion.7), channel_id=1, source_target_pairs={{0,16},{4,20},{8,24},{12,28},{16,0},{20,4},{24,8},{28,12},{1,17},{... | collective-permute-start | bytes 3145736 | tf_op jit(solution)/shard_map/ppermute | solution.py:37
  1544.4 63.1 %collective-permute-start.125 = (bf16[1,256,2048]{1,2,0:T(8,128)(2,1)S(1)}, bf16[1,256,2048]{1,2,0:T(8,128)(2,1)S(1)}, u32[]{:S(2)}, u32[]{:S(2)}) collective-permute-start(bf16[1,256,2048]{1,2,0:T(8,128)(2,1)S(1)} %add_convert_fusion.15), channel_id=1, source_target_pairs={{0,16},{4,20},{8,24},{12,28},{16,0},{20,4},{24,8},{28,12},{1,17},{... | collective-permute-start | bytes 3145736 | tf_op jit(solution)/shard_map/ppermute | solution.py:37
  1548.0 70.1 %collective-permute-start.127 = (bf16[1,256,2048]{1,2,0:T(8,128)(2,1)}, bf16[1,256,2048]{1,2,0:T(8,128)(2,1)}, u32[]{:S(2)}, u32[]{:S(2)}) collective-permute-start(bf16[1,256,2048]{1,2,0:T(8,128)(2,1)} %add_convert_fusion.13), channel_id=1, source_target_pairs={{0,8},{4,12},{8,0},{12,4},{16,24},{20,28},{24,16},{28,20},{1,9},{5... | collective-permute-start | bytes 3145736 | tf_op jit(solution)/shard_map/ppermute | solution.py:37
  (289 other events, 5522.8 us)
Sparse Core Ops, SparseCore 0:
  25.2 92.9 all-gather.1

commit v2 on v1

v2 whole, which is shorter than its diff:
```python
import functools

import jax
import jax.numpy as jnp
from jax import lax
from jax.experimental import pallas as pl
from jax.experimental.pallas import tpu as pltpu
from jax.sharding import PartitionSpec as P

HD = 128
EPSILON = 1e-05
ROTARY_BASE = 10000.0
NEGATIVE = -1e30
F32 = jnp.float32
BF16 = jnp.bfloat16
VMEM_LIMIT = 56 * 1024 * 1024
CHUNKS = 2
NT = (((1,), (1,)), ((), ()))
TN = (((0,), (0,)), ((), ()))
NN = (((1,), (0,)), ((), ()))


def dot(left, right, dims=NN):
    return lax.dot_general(left, right, dims, preferred_element_type=F32)


def after(value, *others):
    return lax.optimization_barrier((value, *others))[0]


def shift(block, axis, distance):
    count = lax.axis_size(axis)
    return lax.ppermute(block, axis, [(i, (i + distance) % count) for i in range(count)])


def swap(block, axis, mask):
    return lax.ppermute(block, axis, [(i, i ^ mask) for i in range(lax.axis_size(axis))])


OUTER, INNER = [(0, 1), (1, 0), (2, 3), (3, 2)], [(0, 0), (1, 2), (2, 1), (3, 3)]


def first_step(block):
    count = lax.axis_size("tp")
    if count == 4:
        return [block, lax.ppermute(block, "tp", OUTER), lax.ppermute(block, "tp", INNER)]
    return [block] + [shift(block, "tp", k) for k in range(1, count)]


def second_step(first, *others):
    if lax.axis_size("tp") != 4:
        return []
    _, a1, b1 = first
    return [
        lax.ppermute(after(b1, a1, *others), "tp", OUTER),
        lax.ppermute(after(a1, b1, *others), "tp", INNER),
    ]


def third_step(first, second, *others):
    count = lax.axis_size("tp")
    if count != 4:
        return first, by_distance(count)
    (block, a1, b1), (a2, b2) = first, second
    a3 = lax.ppermute(after(b2, a2, *others), "tp", OUTER)
    return [block, a1, a2, a3, b1, b2], ((0, 1, 2, 3), (1, 0, 4, 5), (5, 4, 0, 1), (3, 2, 1, 0))


def gather_tp(block, second=(), third=()):
    first = first_step(block)
    return third_step(first, second_step(first, *second), *third)


def by_distance(count):
    return tuple(tuple((z - f) % count for f in range(count)) for z in range(count))


def exchange(pieces):
    return [p if k == 0 else shift(p, "tp", k) for k, p in enumerate(pieces)]


def butterfly(value, axis):
    return butterfly_steps(value, axis)[0]


def butterfly_steps(value, axis):
    mask, received = 1, None
    while mask < lax.axis_size(axis):
        received = swap(value, axis, mask)
        value = value + received
        mask *= 2
    return value, received


def block_of(array, index, size, axis):
    return lax.dynamic_slice_in_dim(array, index * size, size, axis)


def gather_sides(pair):
    if lax.axis_size("sq") == 8:
        return swap(pair, "sq", 2), swap(pair, "sq", 4)
    return [swap(pair, "sq", m) for m in range(2, lax.axis_size("sq"), 2)]


def gather_diagonal(pair, sides):
    trio = swap(jnp.stack([pair, *sides]), "sq", 1)
    if lax.axis_size("sq") == 8:
        near, far = sides
        return trio, swap(far[:1], "sq", 2), swap(near[1:], "sq", 4)
    return (trio,)


def gather_slots(pair, sides, trio, *diagonal):
    slots = []
    for k, side in enumerate([pair, *sides]):
        slots += [side, trio[k]]
    if diagonal:
        slots += [diagonal, swap(jnp.concatenate(diagonal), "sq", 1)]
    return slots


def scatter_cores(odd):
    return swap(odd, "sq", 1)


def scatter_diagonal(even, received):
    return add_blocks([[(even, (3, half)), (received, (3, half))] for half in range(2)])


def send_halves(diagonal):
    return [swap(diagonal[half], "sq", 2 + 2 * half) for half in range(2)]


def scatter_sides(even, received, halves):
    sums = []
    for k in range(1, 3 if halves else even.shape[0]):
        terms = [[(even, (k, half)), (received, (k, half))] for half in range(2)]
        if halves:
            terms[2 - k].append((halves[2 - k], ()))
        sums.append(add_blocks(terms))
    return sums, [swap(array, "sq", 2 * k + 2) for k, array in enumerate(sums)]


def scatter_total(even, received, blocks):
    return add_blocks(
        [
            [(even, (0, half)), (received, (0, half))] + [(block, (half,)) for block in blocks]
            for half in range(2)
        ]
    )


def reduce_cores(info, pairs):
    received = swap(relative_grads(info, 1, pairs, None), "sq", 1)
    own = relative_grads(info, 0, pairs, received)
    return own.reshape(lax.axis_size("sq") // 2, -1, own.shape[1])


def reduce_chips(own):
    half = own.shape[2] // 2
    results = []
    for part in range(2):
        blocks = own[:, :, part * half : (part + 1) * half]
        steps = [1 << b for b in range(own.shape[0].bit_length() - 1)]
        if part:
            steps = steps[::-1]
        kept = {m: blocks[m] for m in range(own.shape[0])}
        for number, step in enumerate(steps):
            give = sorted(m for m in kept if m & step)
            keep = sorted(m for m in kept if not m & step)
            got = swap(jnp.stack([kept[m] for m in give]), "sq", 2 * step)
            last = number == len(steps) - 1
            kept = {
                m: (kept[m].astype(F32) + got[i].astype(F32)).astype(F32 if last else BF16)
                for i, m in enumerate(keep)
            }
        results.append(kept[0])
    return jnp.concatenate(results, axis=1).astype(F32)


COST = 100


def cost(flops, bytes_accessed, transcendentals):
    return pl.CostEstimate(
        flops=flops // COST,
        bytes_accessed=bytes_accessed // COST,
        transcendentals=transcendentals // COST,
    )


def add_kernel(counts, *refs):
    first = 0
    for half, count in enumerate(counts):
        total = None
        for ref in refs[first : first + count]:
            part = ref[(0,) * (len(ref.shape) - 2)].astype(F32)
            total = part if total is None else total + part
        refs[-1][half, 0] = total.astype(BF16)
        first += count


def add_blocks(halves):
    shape = halves[0][0][0].shape[-3:]

    def spec(lead):
        return pl.BlockSpec((1,) * (len(lead) + 1) + shape[1:], lambda s: (*lead, s, 0, 0))

    terms = [term for half in halves for term in half]
    return pl.pallas_call(
        functools.partial(add_kernel, [len(half) for half in halves]),
        grid=(shape[0],),
        in_specs=[spec(lead) for _, lead in terms],
        out_specs=pl.BlockSpec((2, 1) + shape[1:], lambda s: (0, s, 0, 0)),
        out_shape=jax.ShapeDtypeStruct((2, *shape), BF16),
        compiler_params=params(),
        name="add_blocks",
    )(*[array for array, _ in terms])


def params():
    return pltpu.CompilerParams(vmem_limit_bytes=VMEM_LIMIT)


def place_columns(rank, table, sources, out_ref):
    width = sources[0].shape[-1]
    for z in range(len(table)):

        @pl.when(rank == z)
        def _(z=z):
            for f, index in enumerate(table[z]):
                out_ref[:, f * width : (f + 1) * width] = sources[index][...]


def row_sums(values):
    cols = values.shape[1]
    total = values[:, :HD]
    for k in range(1, cols // HD):
        total = total + values[:, k * HD : (k + 1) * HD]
    return jnp.sum(total.T, axis=0, keepdims=True)


def as_columns(row):
    return jnp.broadcast_to(row, (HD, row.shape[1])).T


def front_kernel(table, count, info, *refs):
    sources, refs = refs[:count], refs[count:]
    gain_ref, wq_ref, wk_ref, wv_ref = refs[:4]
    low_ref, normed_ref, inv_ref, query_ref, key_ref, value_ref, square_ref = refs[4:]
    place_columns(info[0], table, sources, low_ref)
    rows = low_ref[...].astype(F32)
    inv = lax.rsqrt(jnp.mean(rows * rows, axis=1, keepdims=True) + EPSILON)
    inv_ref[...] = inv
    normed = (rows * inv * gain_ref[...]).astype(BF16)
    normed_ref[...] = normed
    query, key = dot(normed, wq_ref[...]), dot(normed, wk_ref[...])
    query_ref[...] = query
    key_ref[...] = key
    value_ref[...] = dot(normed, wv_ref[...]).astype(BF16)
    square_ref[0:1, :] = row_sums(query * query)
    square_ref[1:2, :] = row_sums(key * key)


def front(rank, gathered, gain, w_query, w_key, w_value):
    sources, table = gathered
    rows, width = sources[0].shape
    total = width * len(table)
    cols = w_query.shape[1]
    tile = min(256, rows)
    spec = lambda cols: pl.BlockSpec((tile, cols), lambda i, info: (i, 0))
    whole = lambda array: pl.BlockSpec(
        array.shape, lambda i, info: (0, 0), pipeline_mode=pl.Buffered(1)
    )
    out = lambda cols, dtype: jax.ShapeDtypeStruct((rows, cols), dtype)
    return pl.pallas_call(
        functools.partial(front_kernel, table, len(sources)),
        grid_spec=pltpu.PrefetchScalarGridSpec(
            num_scalar_prefetch=1,
            grid=(rows // tile,),
            in_specs=[spec(width)] * len(sources)
            + [pl.BlockSpec((1, total), lambda i, info: (0, 0))]
            + [whole(w_query), whole(w_key), whole(w_value)],
            out_specs=[spec(total), spec(total), spec(1), spec(cols), spec(cols), spec(cols)]
            + [pl.BlockSpec((2, tile), lambda i, info: (0, i))],
        ),
        out_shape=[
            out(total, BF16),
            out(total, BF16),
            out(1, F32),
            out(cols, F32),
            out(cols, F32),
            out(cols, BF16),
            jax.ShapeDtypeStruct((2, rows), F32),
        ],
        compiler_params=params(),
        cost_estimate=cost(
            flops=6 * rows * total * cols,
            bytes_accessed=6 * total * cols + 8 * rows * total,
            transcendentals=0,
        ),
        name="front",
    )(rank, *sources, gain[None, :], w_query, w_key, w_value)


def halves(count):
    lane = lax.broadcasted_iota(jnp.int32, (1, HD), 1)
    return jnp.where(lane < HD // 2, 1.0, -1.0)


def rotate_kernel(
    all_cols, q_ref, k_ref, v_ref, square_ref, qg_ref, kg_ref, cos_ref, sin_ref, out_ref, pair_ref
):
    inv = lax.rsqrt(square_ref[...] / all_cols + EPSILON)
    cosine, sine = cos_ref[...], -halves(HD) * sin_ref[...]
    for number, (raw_ref, gain_ref) in enumerate(((q_ref, qg_ref), (k_ref, kg_ref))):
        scale = as_columns(inv[number : number + 1, :])
        for h in range(raw_ref.shape[1] // HD):
            span = slice(h * HD, (h + 1) * HD)
            normed = raw_ref[:, span] * scale * gain_ref[:, span]
            turned = (normed * cosine + pltpu.roll(normed, HD // 2, 1) * sine).astype(BF16)
            if number == 0:
                out_ref[0, :, span] = turned
            else:
                pair_ref[0, 0, :, span] = turned
    pair_ref[1, 0] = v_ref[...]


def rotate(query, key, value, squares, query_gain, key_gain, cosine, sine, all_cols):
    rows, cols = query.shape
    size = cosine.shape[0]
    spec = pl.BlockSpec((size, cols), lambda s: (s, 0))
    one = pl.BlockSpec((1, cols), lambda s: (0, 0))
    turn = pl.BlockSpec((size, HD), lambda s: (0, 0))
    return pl.pallas_call(
        functools.partial(rotate_kernel, all_cols),
        grid=(rows // size,),
        in_specs=[spec, spec, spec, pl.BlockSpec((2, size), lambda s: (0, s))]
        + [one, one, turn, turn],
        out_specs=[
            pl.BlockSpec((1, size, cols), lambda s: (s, 0, 0)),
            pl.BlockSpec((2, 1, size, cols), lambda s: (0, s, 0, 0)),
        ],
        out_shape=[
            jax.ShapeDtypeStruct((rows // size, size, cols), BF16),
            jax.ShapeDtypeStruct((2, rows // size, size, cols), BF16),
        ],
        compiler_params=params(),
        name="rotate",
    )(query, key, value, squares, query_gain[None, :], key_gain[None, :], cosine, sine)


def back_parts(all_cols, refs):
    dq_ref, dkv_ref, q_ref, k_ref, square_ref, qg_ref, kg_ref, cos_ref, sin_ref = refs
    inv = lax.rsqrt(square_ref[...] / all_cols + EPSILON)
    cosine, sine = cos_ref[...], sin_ref[...]
    sign = halves(HD)
    for number, (raw_ref, gain_ref) in enumerate(((q_ref, qg_ref), (k_ref, kg_ref))):
        scale = as_columns(inv[number : number + 1, :])
        for h in range(raw_ref.shape[1] // HD):
            span = slice(h * HD, (h + 1) * HD)
            grad = (dkv_ref[0, 0, :, span] if number else dq_ref[0, :, span]).astype(F32)
            back = grad * cosine + pltpu.roll(grad * sine, HD // 2, 1) * sign
            yield number, span, back, raw_ref[:, span] * scale, scale, gain_ref[:, span]


def back_stats_kernel(all_cols, *refs):
    stat_ref, gain_ref = refs[9:]

    @pl.when(pl.program_id(0) == 0)
    def _():
        gain_ref[...] = jnp.zeros(gain_ref.shape, F32)

    totals = [None, None]
    for number, span, back, hat, _, gain in back_parts(all_cols, refs[:9]):
        product = back * hat
        gain_ref[number : number + 1, span] += jnp.sum(product, axis=0, keepdims=True)
        product = product * gain
        totals[number] = product if totals[number] is None else totals[number] + product
    for number in range(2):
        stat_ref[number : number + 1, :] = row_sums(totals[number])


def back_specs(size, cols):
    spec = pl.BlockSpec((size, cols), lambda s: (s, 0))
    one = pl.BlockSpec((1, cols), lambda s: (0, 0))
    turn = pl.BlockSpec((size, HD), lambda s: (0, 0))
    row = pl.BlockSpec((2, size), lambda s: (0, s))
    return [
        pl.BlockSpec((1, size, cols), lambda s: (s, 0, 0)),
        pl.BlockSpec((2, 1, size, cols), lambda s: (0, s, 0, 0)),
        spec,
        spec,
        row,
        one,
        one,
        turn,
        turn,
    ]


def back_stats(operands, all_cols):
    rows, cols = operands[2].shape
    size = operands[0].shape[1]
    return pl.pallas_call(
        functools.partial(back_stats_kernel, all_cols),
        grid=(rows // size,),
        in_specs=back_specs(size, cols),
        out_specs=[
            pl.BlockSpec((2, size), lambda s: (0, s)),
            pl.BlockSpec((2, cols), lambda s: (0, 0)),
        ],
        out_shape=[
            jax.ShapeDtypeStruct((2, rows), F32),
            jax.ShapeDtypeStruct((2, cols), F32),
        ],
        compiler_params=params(),
        name="back_stats",
    )(*operands)


def back_first_kernel(all_cols, count, info, *refs):
    stat_ref, low_ref, inv_ref, gain_ref, wq_ref, wk_ref, wv_ref = refs[9:16]
    raw_ref, part_ref = refs[16:18]
    first_refs, buffer = refs[18 : 18 + count], refs[18 + count]
    size = buffer.shape[0]
    rows = pl.ds(pl.multiple_of(pl.program_id(0) * size, size), size)
    cols = wq_ref.shape[1]
    stats = stat_ref[...] / all_cols
    for number, span, back, hat, scale, gain in back_parts(all_cols, refs[:9]):
        mean = as_columns(stats[number : number + 1, :])
        raw = scale * (back * gain - hat * mean)
        raw_ref[:, number * cols + span.start : number * cols + span.stop] = raw.astype(BF16)
    raw_ref[:, 2 * cols :] = refs[1][1, 0]
    first = (
        dot(raw_ref[:, :cols], wq_ref[...], NT)
        + dot(raw_ref[:, cols : 2 * cols], wk_ref[...], NT)
        + dot(raw_ref[:, 2 * cols :], wv_ref[...], NT)
    )
    buffer[...] = first.astype(BF16)
    feat = first_refs[0].shape[1]
    for k in range(count):
        target = lax.rem(info[1] + k, count)
        span = pl.ds(pl.multiple_of(target * feat, feat), feat)
        first_refs[k][rows, :] = buffer[:, span]

    @pl.when(pl.program_id(0) == 0)
    def _():
        part_ref[...] = jnp.zeros(part_ref.shape, F32)

    product = first * (low_ref[...].astype(F32) * inv_ref[...])
    part_ref[...] += jnp.sum(product, axis=0, keepdims=True)
    rest = row_sums(product * gain_ref[...])
    line = lax.broadcasted_iota(jnp.int32, (EXTRA, size), 0)
    terms = jnp.zeros((EXTRA, size), F32)
    for term in range(2):
        part = rest.astype(BF16).astype(F32)
        rest = rest - part
        terms = jnp.where(line == 2 * pl.program_id(0) + term, part, terms)
    for ref in first_refs:
        place = ref.shape[0] - EXTRA

        @pl.when(pl.program_id(0) == 0)
        def _(ref=ref, place=place):
            ref[place:, :] = jnp.zeros((EXTRA, feat), BF16)

        ref[place:, :size] += terms.astype(BF16)


EXTRA = 16


def back_first(info, operands, stats, low, inv, gain, w_query, w_key, w_value, all_cols, count):
    rows, cols = operands[2].shape
    size = operands[0].shape[1]
    total = low.shape[1]
    lift = lambda spec: pl.BlockSpec(spec.block_shape, lambda s, info: spec.index_map(s))
    spec = lambda cols: pl.BlockSpec((size, cols), lambda s, info: (s, 0))
    row = lambda count: pl.BlockSpec((count, size), lambda s, info: (0, s))
    whole = lambda array: pl.BlockSpec(
        array.shape, lambda s, info: (0, 0), pipeline_mode=pl.Buffered(1)
    )
    one = pl.BlockSpec((1, total), lambda s, info: (0, 0))
    height = rows + EXTRA
    raw, part, *pieces = pl.pallas_call(
        functools.partial(back_first_kernel, all_cols, count),
        grid_spec=pltpu.PrefetchScalarGridSpec(
            num_scalar_prefetch=1,
            grid=(rows // size,),
            in_specs=[lift(s) for s in back_specs(size, cols)]
            + [row(2), spec(total), spec(1), one]
            + [whole(w_query), whole(w_key), whole(w_value)],
            out_specs=[spec(3 * cols), one]
            + [pl.BlockSpec((height, total // count), lambda s, info: (0, 0))] * count,
            scratch_shapes=[pltpu.VMEM((size, total), BF16)],
        ),
        out_shape=[
            jax.ShapeDtypeStruct((rows, 3 * cols), BF16),
            jax.ShapeDtypeStruct((1, total), F32),
        ]
        + [jax.ShapeDtypeStruct((height, total // count), BF16)] * count,
        compiler_params=params(),
        cost_estimate=cost(
            flops=6 * rows * total * cols,
            bytes_accessed=6 * total * cols + 8 * rows * total,
            transcendentals=0,
        ),
        name="back_first",
    )(info, *operands, stats, low, inv, gain[None, :], w_query, w_key, w_value)
    return raw, pieces, part[0]


def joined_kernel(table, count, info, *refs):
    place_columns(info[0], table, refs[:count], refs[count])


def joined_rows(rank, gathered):
    sources, table = gathered
    rows, width = sources[0].shape
    total = width * len(table)
    tile = min(256, rows)
    spec = lambda cols: pl.BlockSpec((tile, cols), lambda i, info: (i, 0))
    return pl.pallas_call(
        functools.partial(joined_kernel, table, len(sources)),
        grid_spec=pltpu.PrefetchScalarGridSpec(
            num_scalar_prefetch=1,
            grid=(rows // tile,),
            in_specs=[spec(width)] * len(sources),
            out_specs=spec(total),
        ),
        out_shape=jax.ShapeDtypeStruct((rows, total), BF16),
        compiler_params=params(),
        name="joined_rows",
    )(rank, *sources)


def relative_grads_kernel(counts, info, *refs):
    more = refs[2 * sum(counts) : -1]
    first, start = 0, 0
    for count in counts:
        lefts, rights = refs[first : first + count], refs[first + count : first + 2 * count]
        first += 2 * count
        total = dot(lefts[0][...], rights[0][...], TN)
        for left, right in zip(lefts[1:], rights[1:]):
            total += dot(left[...], right[...], TN)
        span = slice(start, start + total.shape[1])
        start = span.stop
        for ref in more:
            total += ref[:, span].astype(F32)
        refs[-1][:, span] = total.astype(BF16)


def relative_grads(info, parity, pairs, more):
    blocks = lax.axis_size("sq")
    height = pairs[0][0][0][0].shape[1] // blocks
    specs, operands, width = [], [], 0
    for lefts, rights in pairs:
        width += rights[0].shape[1]
        for (_, chunk), right in zip(lefts, rights):
            specs.append(
                pl.BlockSpec(
                    (right.shape[0], height),
                    lambda m, info, chunk=chunk: (
                        chunk,
                        jnp.bitwise_xor(info[0], 2 * m + parity),
                    ),
                )
            )
        specs += [
            pl.BlockSpec(right.shape, lambda m, info: (0, 0), pipeline_mode=pl.Buffered(1))
            for right in rights
        ]
        operands += [left for left, _ in lefts] + list(rights)
    out = pl.BlockSpec((height, width), lambda m, info: (m, 0))
    if more is not None:
        specs.append(out)
        operands.append(more)
    return pl.pallas_call(
        functools.partial(relative_grads_kernel, [len(lefts) for lefts, _ in pairs]),
        grid_spec=pltpu.PrefetchScalarGridSpec(
            num_scalar_prefetch=1, grid=(blocks // 2,), in_specs=specs, out_specs=out
        ),
        out_shape=jax.ShapeDtypeStruct((height * blocks // 2, width), BF16),
        compiler_params=params(),
        name="relative_grads",
    )(info, *operands)


def middle_kernel(table, count, info, *refs):
    sources = refs[:count]
    low_ref, w_ref, gain_ref, router_ref, routes_ref = refs[count : count + 5]
    attn_ref, middle_ref, inv_ref, ffn_ref, prob_ref, routed_ref = refs[count + 5 :]
    place_columns(info[0], table, sources, attn_ref)
    middle = low_ref[...].astype(F32) + dot(attn_ref[...], w_ref[...])
    middle_ref[...] = middle
    inv = lax.rsqrt(jnp.mean(middle * middle, axis=1, keepdims=True) + EPSILON)
    inv_ref[...] = inv
    ffn_in = (middle * inv * gain_ref[...]).astype(BF16)
    ffn_ref[...] = ffn_in
    logits = dot(ffn_in, router_ref[...])
    powers = jnp.exp(logits - jnp.max(logits, axis=1, keepdims=True))
    prob_ref[...] = powers / jnp.sum(powers, axis=1, keepdims=True)
    routes = routes_ref[...]
    ids = lax.broadcasted_iota(jnp.int32, logits.shape, 1)
    routed = jnp.zeros(logits.shape, F32)
    for r in range(routes.shape[1]):
        routed = jnp.where(routes[:, r : r + 1] == ids, 1.0, routed)
    routed_ref[...] = routed


def middle_rows(rank, gathered, low, w_out, gain, router, routes):
    sources, table = gathered
    rows, width = sources[0].shape
    total = low.shape[1]
    experts = router.shape[1]
    tile = min(256, rows)
    spec = lambda cols: pl.BlockSpec((tile, cols), lambda i, info: (i, 0))
    whole = lambda array: pl.BlockSpec(
        array.shape, lambda i, info: (0, 0), pipeline_mode=pl.Buffered(1)
    )
    out = lambda cols, dtype: jax.ShapeDtypeStruct((rows, cols), dtype)
    return pl.pallas_call(
        functools.partial(middle_kernel, table, len(sources)),
        grid_spec=pltpu.PrefetchScalarGridSpec(
            num_scalar_prefetch=1,
            grid=(rows // tile,),
            in_specs=[spec(width)] * len(sources)
            + [spec(total), whole(w_out), pl.BlockSpec((1, total), lambda i, info: (0, 0))]
            + [whole(router), spec(routes.shape[1])],
            out_specs=[
                spec(width * len(table)),
                spec(total),
                spec(1),
                spec(total),
                spec(experts),
                spec(experts),
            ],
        ),
        out_shape=[
            out(width * len(table), BF16),
            out(total, F32),
            out(1, F32),
            out(total, BF16),
            out(experts, F32),
            out(experts, F32),
        ],
        compiler_params=params(),
        cost_estimate=cost(
            flops=2 * rows * total * total,
            bytes_accessed=2 * total * total + 12 * rows * total,
            transcendentals=0,
        ),
        name="middle_rows",
    )(rank, *sources, low, w_out, gain[None, :], router, routes)


def weight_grad_kernel(count, parts, *refs):
    height = refs[count].shape[0]
    left = lambda i: refs[i][...] if parts == 1 else refs[0][i * height : (i + 1) * height, :]
    total = dot(left(0), refs[count][...], TN)
    for i in range(1, len(refs) - 1 - count):
        total += dot(left(i), refs[count + i][...], TN)
    refs[-1][...] = total.astype(BF16)


def weight_grad(lefts, rights):
    rows, height = rights[0].shape[0], lefts[0].shape[1]
    width = rights[0].shape[1]
    parts = lefts[0].shape[0] // rows
    tall = min(2048, height)
    cols = min(512, width)
    return pl.pallas_call(
        functools.partial(weight_grad_kernel, len(lefts), parts),
        grid=(width // cols, height // tall),
        in_specs=[pl.BlockSpec((rows * parts, tall), lambda j, i: (0, i))] * len(lefts)
        + [pl.BlockSpec((rows, cols), lambda j, i: (0, j))] * len(rights),
        out_specs=pl.BlockSpec((tall, cols), lambda j, i: (i, j)),
        out_shape=jax.ShapeDtypeStruct((height, width), BF16),
        compiler_params=params(),
        cost_estimate=cost(
            flops=2 * rows * len(rights) * height * width,
            bytes_accessed=2 * (rows * len(rights) * (height + width) + height * width),
            transcendentals=0,
        ),
        name="weight_grad",
    )(*lefts, *rights)


def slot_operands(kv_slots):
    arrays, places = [], []
    for slot in kv_slots:
        if isinstance(slot, tuple):
            places.append(((len(arrays), 0), (len(arrays) + 1, 0)))
            arrays += list(slot)
        else:
            places.append(((len(arrays), 0), (len(arrays), 1)))
            arrays.append(slot)
    size = arrays[0].shape[2]
    specs = [
        pl.BlockSpec((a.shape[0], 1, size, HD), lambda s, h, info: (0, s, 0, h)) for a in arrays
    ]
    return arrays, specs, places


def attn_forward_kernel(places, count, info, q_ref, *refs):
    kv_refs, (low_ref, full_ref, lse_ref, top, total, accum) = refs[:count], refs[count:]
    rank = info[0]
    length = info[2 + pl.program_id(0)]
    queries = q_ref[0]
    size = queries.shape[0]
    top[...] = jnp.full(top.shape, NEGATIVE, F32)
    total[...] = jnp.zeros(total.shape, F32)
    accum[...] = jnp.zeros(accum.shape, F32)
    key_row = lax.broadcasted_iota(jnp.int32, (size, size), 0)
    query_col = lax.broadcasted_iota(jnp.int32, (size, size), 1)
    for slot, ((ka, ki), (va, vi)) in enumerate(places):
        block = rank ^ slot
        start = block * size

        @pl.when((block <= rank) & (start < length))
        def _(slot=slot, start=start, ka=ka, ki=ki, va=va, vi=vi):
            scores = dot(kv_refs[ka][ki, 0], queries, NT) * HD**-0.5
            allowed = key_row + start < length
            if slot == 0:
                allowed = allowed & (key_row <= query_col)
            scores = jnp.where(allowed, scores, NEGATIVE)
            newest = jnp.maximum(top[...], jnp.max(scores, axis=0, keepdims=True))
            weights = jnp.exp(scores - newest)
            factor = jnp.exp(top[...] - newest)
            top[...] = newest
            total[...] = total[...] * factor + jnp.sum(weights, axis=0, keepdims=True)
            accum[...] = accum[...] * factor + dot(kv_refs[va][vi, 0], weights.astype(BF16), TN)

    result = (accum[...] / total[...]).T
    full_ref[0] = result
    low_ref[0] = result.astype(BF16)
    lse_ref[0, 0] = top[...] + jnp.log(total[...])


def attn_forward(info, queries, kv_slots):
    seqs, size, columns = queries.shape
    heads = columns // HD
    slots = len(kv_slots)
    arrays, specs, places = slot_operands(kv_slots)
    row_spec = pl.BlockSpec((1, size, HD), lambda s, h, info: (s, 0, h))
    lse_spec = pl.BlockSpec((1, 1, 1, size), lambda s, h, info: (s, h, 0, 0))
    return pl.pallas_call(
        functools.partial(attn_forward_kernel, places, len(arrays)),
        grid_spec=pltpu.PrefetchScalarGridSpec(
            num_scalar_prefetch=1,
            grid=(seqs, heads),
            in_specs=[row_spec] + specs,
            out_specs=[row_spec, row_spec, lse_spec],
            scratch_shapes=[
                pltpu.VMEM((1, size), F32),
                pltpu.VMEM((1, size), F32),
                pltpu.VMEM((HD, size), F32),
            ],
        ),
        out_shape=[
            jax.ShapeDtypeStruct(queries.shape, BF16),
            jax.ShapeDtypeStruct(queries.shape, F32),
            jax.ShapeDtypeStruct((seqs, heads, 1, size), F32),
        ],
        compiler_params=params(),
        cost_estimate=cost(
            flops=8 * seqs * heads * slots * size * size * HD,
            bytes_accessed=4 * seqs * size * columns * (slots + 2),
            transcendentals=seqs * heads * slots * size * size,
        ),
        name="attn_forward",
    )(info, queries, *arrays)


def attn_backward_kernel(places, count, tp_count, info, q_ref, full_ref, lse_ref, *refs):
    grad_refs, refs = refs[:tp_count], refs[tp_count:]
    kv_refs, (dq_ref, even_ref, odd_ref, accum, grad_buf) = refs[:count], refs[count:]
    rank = info[0]
    length = info[2 + pl.program_id(0)]
    queries = q_ref[0]
    size = queries.shape[0]
    piece = size * pl.num_programs(0) // tp_count
    for i in range(size // piece):
        sender = pl.program_id(0) * (size // piece) + i
        distance = lax.rem(info[1] - sender + tp_count, tp_count)
        for k in range(tp_count):

            @pl.when(distance == k)
            def _(i=i, k=k):
                grad_buf[i * piece : (i + 1) * piece, :] = grad_refs[k][...]

    grads = grad_buf[...]
    lse = lse_ref[0, 0]
    delta = jnp.sum((grads.astype(F32) * full_ref[0]).T, axis=0, keepdims=True)
    accum[...] = jnp.zeros(accum.shape, F32)
    key_row = lax.broadcasted_iota(jnp.int32, (size, size), 0)
    query_col = lax.broadcasted_iota(jnp.int32, (size, size), 1)
    for slot, ((ka, ki), (va, vi)) in enumerate(places):
        block = rank ^ slot
        start = block * size
        out_ref = odd_ref if slot % 2 else even_ref
        live = (block <= rank) & (start < length)

        @pl.when(live)
        def _(slot=slot, start=start, out_ref=out_ref, ka=ka, ki=ki, va=va, vi=vi):
            keys, values = kv_refs[ka][ki, 0], kv_refs[va][vi, 0]
            scores = dot(keys, queries, NT) * HD**-0.5
            allowed = key_row + start < length
            if slot == 0:
                allowed = allowed & (key_row <= query_col)
            weights = jnp.where(allowed, jnp.exp(scores - lse), 0.0)
            back = dot(values, grads, NT)
            score_grad = (weights * (back - delta)).astype(BF16)
            out_ref[slot // 2, 1, 0] = dot(weights.astype(BF16), grads).astype(BF16)
            out_ref[slot // 2, 0, 0] = (dot(score_grad, queries) * HD**-0.5).astype(BF16)
            accum[...] += dot(score_grad, keys, TN)

        @pl.when(jnp.logical_not(live))
        def _(slot=slot, out_ref=out_ref):
            out_ref[slot // 2, :, 0] = jnp.zeros((2,) + queries.shape, BF16)

    dq_ref[0] = (accum[...] * HD**-0.5).astype(BF16)


def attn_backward(info, queries, grad_pieces, full, lse, kv_slots):
    seqs, size, columns = queries.shape
    heads = columns // HD
    slots = len(kv_slots)
    arrays, specs, places = slot_operands(kv_slots)
    piece = size * seqs // len(grad_pieces)
    last = grad_pieces[0].shape[0] // piece - 1
    row_spec = pl.BlockSpec((1, size, HD), lambda s, h, info: (s, 0, h))
    piece_spec = pl.BlockSpec((piece, HD), lambda s, h, info: (last, h))
    lse_spec = pl.BlockSpec((1, 1, 1, size), lambda s, h, info: (s, h, 0, 0))
    out_spec = pl.BlockSpec((slots // 2, 2, 1, size, HD), lambda s, h, info: (0, 0, s, 0, h))
    out_shape = jax.ShapeDtypeStruct((slots // 2, 2, seqs, size, columns), BF16)
    return pl.pallas_call(
        functools.partial(attn_backward_kernel, places, len(arrays), len(grad_pieces)),
        grid_spec=pltpu.PrefetchScalarGridSpec(
            num_scalar_prefetch=1,
            grid=(seqs, heads),
            in_specs=[row_spec, row_spec, lse_spec] + [piece_spec] * len(grad_pieces) + specs,
            out_specs=[row_spec, out_spec, out_spec],
            scratch_shapes=[pltpu.VMEM((size, HD), F32), pltpu.VMEM((size, HD), BF16)],
        ),
        out_shape=[jax.ShapeDtypeStruct(queries.shape, BF16), out_shape, out_shape],
        compiler_params=params(),
        cost_estimate=cost(
            flops=20 * seqs * heads * slots * size * size * HD,
            bytes_accessed=8 * seqs * size * columns * (slots + 2),
            transcendentals=seqs * heads * slots * size * size,
        ),
        name="attn_backward",
    )(info, queries, full, lse, *grad_pieces, *arrays)


def expert_hidden_kernel(
    tile,
    info,
    x_ref,
    g_ref,
    prob_ref,
    routed_ref,
    wg_ref,
    wu_ref,
    wd_ref,
    gh_ref,
    gp_ref,
    up_ref,
    gg_ref,
):
    expert, block = pl.program_id(0), pl.program_id(1)
    rows = x_ref.shape[0]

    @pl.when((expert == 0) & (block == 0))
    def _():
        gg_ref[...] = jnp.zeros(gg_ref.shape, F32)

    for i in range(rows // tile):
        span = slice(i * tile, (i + 1) * tile)
        tokens = x_ref[span, :]
        gate_pre = dot(tokens, wg_ref[0])
        up_pre = dot(tokens, wu_ref[0])
        back = dot(g_ref[span, :], wd_ref[0], NT)
        probs = prob_ref[span, :]
        lane = lax.broadcasted_iota(jnp.int32, probs.shape, 1)
        chosen = (lane == info[1] * pl.num_programs(0) + expert) & (routed_ref[span, :] > 0.5)
        gate = jnp.sum(jnp.where(chosen, probs, 0.0), axis=1, keepdims=True)
        sigmoid = 1.0 / (1.0 + jnp.exp(-gate_pre))
        silu = gate_pre * sigmoid
        hidden = silu * up_pre
        inner = jnp.sum(hidden * back, axis=1, keepdims=True)
        gg_ref[span, :] += jnp.where(chosen, inner, 0.0)
        gh_ref[span, :] = (gate * hidden).astype(BF16)
        hidden_grad = gate * back
        gp_ref[span, :] = (
            hidden_grad * up_pre * (sigmoid + silu * (1.0 - sigmoid))
        ).astype(BF16)
        up_ref[span, :] = (hidden_grad * silu).astype(BF16)


def expert_hidden(info, tokens, grads, probs, routed, w_gate, w_up, w_down, chunk):
    rows, width = tokens.shape
    experts, _, units = w_gate.shape
    cols = min(512, units)
    tile = min(512, rows)
    whole = pl.BlockSpec((rows, width), lambda e, f, info: (0, 0), pipeline_mode=pl.Buffered(1))
    part = pl.BlockSpec((rows, width), lambda e, f, info: (chunk, 0), pipeline_mode=pl.Buffered(1))
    small = pl.BlockSpec(probs.shape, lambda e, f, info: (0, 0))
    wide = pl.BlockSpec((1, width, cols), lambda e, f, info: (e, 0, f))
    tall = pl.BlockSpec((1, cols, width), lambda e, f, info: (e, f, 0))
    result = pl.BlockSpec((rows, cols), lambda e, f, info: (0, e * (units // cols) + f))
    out = jax.ShapeDtypeStruct((rows, experts * units), BF16)
    return pl.pallas_call(
        functools.partial(expert_hidden_kernel, tile),
        grid_spec=pltpu.PrefetchScalarGridSpec(
            num_scalar_prefetch=1,
            grid=(experts, units // cols),
            in_specs=[whole, part, small, small, wide, wide, tall],
            out_specs=[result, result, result, small],
        ),
        out_shape=[out, out, out, jax.ShapeDtypeStruct(probs.shape, F32)],
        compiler_params=params(),
        cost_estimate=cost(
            flops=6 * rows * width * experts * units,
            bytes_accessed=6 * width * experts * units + 6 * rows * experts * units,
            transcendentals=rows * experts * units,
        ),
        name="expert_hidden",
    )(info, tokens, grads, probs, routed, w_gate, w_up, w_down)


def expert_back_kernel(
    count, info, gp_ref, up_ref, gg_ref, prob_ref, router_ref, x_ref, wg_ref, wu_ref, *refs
):
    out_refs, lg_ref, rg_ref, accum = refs[:count], refs[count], refs[count + 1], refs[count + 2]
    expert, block = pl.program_id(0), pl.program_id(1)
    cols = wg_ref.shape[1]
    span = pl.ds(pl.multiple_of(block * cols, cols), cols)

    @pl.when((expert == 0) & (block == 0))
    def _():
        probs, inner = prob_ref[...], gg_ref[...]
        lg_ref[...] = probs * (inner - jnp.sum(probs * inner, axis=1, keepdims=True))

    @pl.when(expert == 0)
    def _():
        accum[:, span] = lax.dot_general(
            lg_ref[...],
            router_ref[...].astype(F32),
            NT,
            precision=lax.Precision.HIGHEST,
            preferred_element_type=F32,
        )

    accum[:, span] += dot(gp_ref[...], wg_ref[0], NT) + dot(up_ref[...], wu_ref[0], NT)

    @pl.when(expert == 0)
    def _():
        rest = lg_ref[...]
        total = jnp.zeros((rest.shape[1], cols), F32)
        for _ in range(3):
            part = rest.astype(BF16)
            rest = rest - part.astype(F32)
            total += dot(part, x_ref[...], TN)
        rg_ref[...] = total

    @pl.when(expert == pl.num_programs(0) - 1)
    def _():
        height = out_refs[0].shape[0]
        for k in range(count):
            target = lax.rem(info[1] + k, count)
            rows = pl.ds(pl.multiple_of(target * height, height), height)
            out_refs[k][:, span] = accum[rows, span].astype(BF16)


def expert_back(info, gate_grads, up_grads, inner, probs, router, tokens, w_gate, w_up, count):
    rows = gate_grads.shape[0]
    experts, width, units = w_gate.shape
    total = router.shape[1]
    cols = min(1024, width)
    left = pl.BlockSpec((rows, units), lambda e, d, info: (0, e))
    small = pl.BlockSpec((rows, total), lambda e, d, info: (0, 0))
    weight = pl.BlockSpec((1, cols, units), lambda e, d, info: (e, d, 0))
    piece = pl.BlockSpec((rows // count, width), lambda e, d, info: (0, 0))
    last = width // cols - 1
    *pieces, _, router_grad = pl.pallas_call(
        functools.partial(expert_back_kernel, count),
        grid_spec=pltpu.PrefetchScalarGridSpec(
            num_scalar_prefetch=1,
            grid=(experts, width // cols),
            in_specs=[
                left,
                left,
                small,
                small,
                pl.BlockSpec((cols, total), lambda e, d, info: (d, 0)),
                pl.BlockSpec((rows, cols), lambda e, d, info: (0, jnp.where(e == 0, d, last))),
                weight,
                weight,
            ],
            out_specs=[piece] * count
            + [
                small,
                pl.BlockSpec((total, cols), lambda e, d, info: (0, jnp.where(e == 0, d, last))),
            ],
            scratch_shapes=[pltpu.VMEM((rows, width), F32)],
        ),
        out_shape=[jax.ShapeDtypeStruct((rows // count, width), BF16)] * count
        + [jax.ShapeDtypeStruct((rows, total), F32), jax.ShapeDtypeStruct((total, width), F32)],
        compiler_params=params(),
        cost_estimate=cost(
            flops=4 * rows * width * experts * units,
            bytes_accessed=4 * width * experts * units + 6 * rows * experts * units,
            transcendentals=0,
        ),
        name="expert_back",
    )(info, gate_grads, up_grads, inner, probs, router, tokens, w_gate, w_up)
    return pieces, router_grad


def mixture_kernel(count, info, hidden_ref, w_ref, *refs):
    head_refs, out_refs = refs[:count], refs[count:]
    rows = hidden_ref.shape[0]
    result = dot(hidden_ref[...], w_ref[...]).astype(BF16)
    for k in range(count):

        @pl.when(pl.program_id(0) == k)
        def _(k=k):
            out_refs[k][:rows] = result
            out_refs[k][rows:] = head_refs[k][...]


def mixture(info, hidden, w_down, heads, count):
    rows, units = hidden.shape
    width = w_down.shape[-1]
    feat = width // count
    height = heads[0].shape[0]
    piece = pl.BlockSpec((rows + height, feat), lambda k, info: (0, 0))
    row = pl.BlockSpec((height, feat), lambda k, info: (0, 0))
    return pl.pallas_call(
        functools.partial(mixture_kernel, count),
        grid_spec=pltpu.PrefetchScalarGridSpec(
            num_scalar_prefetch=1,
            grid=(count,),
            in_specs=[
                pl.BlockSpec((rows, units), lambda k, info: (0, 0), pipeline_mode=pl.Buffered(1)),
                pl.BlockSpec((units, feat), lambda k, info: (0, lax.rem(info[1] + k, count))),
            ]
            + [row] * count,
            out_specs=[piece] * count,
        ),
        out_shape=[jax.ShapeDtypeStruct((rows + height, feat), BF16)] * count,
        compiler_params=params(),
        cost_estimate=cost(
            flops=2 * rows * units * width,
            bytes_accessed=2 * (rows * units + units * width + rows * width),
            transcendentals=0,
        ),
        name="mixture",
    )(info, hidden, w_down.reshape(units, width), *heads)


def middle_back_kernel(count, info, *refs):
    piece_refs, refs = refs[:count], refs[count:]
    middle_ref, inv_ref, grad_ref, gain_ref, w_ref = refs[:5]
    part_ref, low_ref, *out_refs = refs[5:]
    ffn_grad = piece_refs[0][...].astype(F32)
    for k in range(1, count):
        ffn_grad = ffn_grad + piece_refs[k][...].astype(F32)
    inv = inv_ref[...]
    hat = middle_ref[...] * inv
    part_ref[...] = jnp.sum(ffn_grad * hat, axis=0, keepdims=True)
    gained = ffn_grad * gain_ref[...]
    mean = jnp.mean(gained * hat, axis=1, keepdims=True)
    low = (grad_ref[...].astype(F32) + inv * (gained - hat * mean)).astype(BF16)
    low_ref[...] = low
    cols = out_refs[0].shape[1]
    for k in range(count):
        target = lax.rem(info[1] + k, count)
        rows = pl.ds(pl.multiple_of(target * cols, cols), cols)
        out_refs[k][...] = dot(low, w_ref[rows, :], NT).astype(BF16)


def middle_back(info, pieces, middle, inv, grads, gain, w_out, chunk):
    count = len(pieces)
    height, width = pieces[0].shape
    cols = w_out.shape[0] // count
    whole = lambda array: pl.BlockSpec(array.shape, lambda i, info: (0, 0))
    own = lambda cols: pl.BlockSpec((height, cols), lambda i, info: (info[1], 0))
    part = pl.BlockSpec((height, width), lambda i, info: (chunk * count + info[1], 0))
    first = lambda rows, cols: pl.BlockSpec((rows, cols), lambda i, info: (0, 0))
    out = lambda rows, cols, dtype: jax.ShapeDtypeStruct((rows, cols), dtype)
    part, low, *rest = pl.pallas_call(
        functools.partial(middle_back_kernel, count),
        grid_spec=pltpu.PrefetchScalarGridSpec(
            num_scalar_prefetch=1,
            grid=(1,),
            in_specs=[first(height, width)] * count
            + [own(width), own(1), part, first(1, width), whole(w_out)],
            out_specs=[first(1, width), first(height, width)] + [first(height, cols)] * count,
        ),
        out_shape=[out(1, width, F32), out(height, width, BF16)]
        + [out(height, cols, BF16)] * count,
        compiler_params=params(),
        cost_estimate=cost(
            flops=2 * height * width * width, bytes_accessed=2 * width * width, transcendentals=0
        ),
        name="middle_back",
    )(info, *pieces, middle, inv, grads, gain[None, :], w_out)
    return part[0], low, rest


def finish_kernel(count, info, *refs):
    row_ref, first_refs = refs[0], refs[1 : 1 + count]
    x_ref, inv_ref, gain_ref, out_ref = refs[1 + count :]
    size, width = out_ref.shape[0], count * x_ref.shape[1]
    rows = pl.ds(pl.multiple_of(pl.program_id(0) * size, size), size)
    place = first_refs[0].shape[0] - EXTRA
    first, terms = None, None
    for ref in first_refs:
        part, extra = ref[rows, :].astype(F32), ref[place:, :size].astype(F32)
        first = part if first is None else first + part
        terms = extra if terms is None else terms + extra
    line = lax.broadcasted_iota(jnp.int32, terms.shape, 0)
    own = jnp.where(line // 2 == pl.program_id(0), terms, 0.0)
    inner = as_columns(jnp.sum(own, axis=0, keepdims=True) / width)[:, :1]
    inv = inv_ref[...]
    hat = x_ref[...].astype(F32) * inv
    out_ref[...] = row_ref[...].astype(F32) + inv * (gain_ref[...] * first - hat * inner)


def finish(info, all_rows, first_pieces, x, inv, gain, chunk, seqs):
    count = len(first_pieces)
    rows, feat = x.shape
    size = rows // seqs
    one = lambda array: pl.BlockSpec(array.shape, lambda i, info: (0, 0))
    own = lambda cols: pl.BlockSpec((size, cols), lambda i, info: (i, 0))
    return pl.pallas_call(
        functools.partial(finish_kernel, count),
        grid_spec=pltpu.PrefetchScalarGridSpec(
            num_scalar_prefetch=1,
            grid=(seqs,),
            in_specs=[
                pl.BlockSpec((size, feat), lambda i, info: (chunk * seqs + i, info[1]))
            ]
            + [one(a) for a in first_pieces]
            + [own(feat), own(1), pl.BlockSpec((1, feat), lambda i, info: (0, info[1]))],
            out_specs=own(feat),
        ),
        out_shape=jax.ShapeDtypeStruct((rows, feat), F32),
        compiler_params=params(),
        name="finish",
    )(info, all_rows, *first_pieces, x, inv, gain[None, :])


def ordered_kernel(count, info, *refs):
    height = refs[0].shape[0]
    for z in range(count):

        @pl.when(info[0] == z)
        def _(z=z):
            for c in range(len(refs) // count):
                for f in range(count):
                    row = (c * count + f) * height
                    refs[-1][row : row + height, :] = refs[c * count + (z - f) % count][...]


def ordered_rows(rank, chunks):
    pieces = [piece for chunk in chunks for piece in chunk]
    height, width = pieces[0].shape
    cols = min(512, width)
    spec = lambda rows: pl.BlockSpec((rows, cols), lambda i, info: (0, i))
    return pl.pallas_call(
        functools.partial(ordered_kernel, len(chunks[0])),
        grid_spec=pltpu.PrefetchScalarGridSpec(
            num_scalar_prefetch=1,
            grid=(width // cols,),
            in_specs=[spec(height)] * len(pieces),
            out_specs=spec(height * len(pieces)),
        ),
        out_shape=jax.ShapeDtypeStruct((height * len(pieces), width), BF16),
        compiler_params=params(),
        name="ordered_rows",
    )(rank, *pieces)


def rotary_tables(positions):
    exponent = jnp.arange(HD // 2, dtype=F32) * 2.0 / HD
    frequency = ROTARY_BASE ** (-exponent)
    angles = positions.astype(F32)[:, None] * frequency[None, :]
    cosine = jnp.concatenate([jnp.cos(angles), jnp.cos(angles)], axis=-1)
    sine = jnp.concatenate([jnp.sin(angles), jnp.sin(angles)], axis=-1)
    return cosine, sine


def shards(
    inputs,
    lengths,
    routes,
    attn_gain,
    w_query,
    w_key,
    w_value,
    query_gain,
    key_gain,
    w_out,
    ffn_gain,
    router,
    w_gate,
    w_up,
    w_down,
    cotangent,
):
    size, seqs, feat = inputs.shape
    width, head_cols = w_query.shape
    heads = head_cols // HD
    tp_rank, tp_count = lax.axis_index("tp"), lax.axis_size("tp")
    sq_rank, sq_count = lax.axis_index("sq"), lax.axis_size("sq")
    experts = w_gate.shape[0]
    experts_total = router.shape[1]
    all_cols = head_cols * tp_count
    block = width // sq_count
    chunks = CHUNKS
    per = seqs // chunks
    rows_n = per * size
    quarter = rows_n // tp_count
    positions = sq_rank * size + jnp.arange(size, dtype=jnp.int32)
    cosine, sine = rotary_tables(positions)
    group = lambda array: [
        array[:, c * per : (c + 1) * per].transpose(1, 0, 2).reshape(rows_n, -1)
        for c in range(chunks)
    ]
    inputs_c, routes_c = group(inputs), group(routes)
    cotangent_rows = cotangent.transpose(1, 0, 2).reshape(seqs * size, feat)
    info_c = [
        jnp.concatenate(
            [sq_rank[None], tp_rank[None], lengths[c * per : (c + 1) * per]]
        ).astype(jnp.int32)
        for c in range(chunks)
    ]
    rank = tp_rank[None].astype(jnp.int32)
    def attention_in(c, gathered, *others):
        low, normed, inv, query_raw, key_raw, value, squares = front(
            after(rank, *others) if others else rank, gathered, attn_gain, w_query, w_key, w_value
        )
        with jax.named_scope(f"squares{c}"):
            got = exchange([squares] * tp_count)
        return low, normed, inv, query_raw, key_raw, sum(got), value, got[1:]

    def rotated(c, *others):
        query_raw, key_raw, squares, value = ins[c][3:7]
        squares = after(squares, *others) if others else squares
        return rotate(
            query_raw, key_raw, value, squares, query_gain, key_gain, cosine, sine, all_cols
        )

    def gather_heads(c, ready, *others):
        with jax.named_scope(f"heads{c}"):
            own = attn_c[c][0].reshape(rows_n, head_cols)
            return gather_tp(after(own, *ready) if ready else own, *others)

    early_parts = lambda gathered: (gathered[0][1], gathered[0][-2])

    ins, turned, slots_c, attn_c, heads_c, mids, exps = [], [], [], [], [], [], []
    with jax.named_scope("inputs0"):
        x0 = gather_tp(inputs_c[0])
    with jax.named_scope("inputs1"):
        x1_first = first_step(after(inputs_c[1], x0[0][3]))
    ins.append(attention_in(0, x0))
    turned.append(rotated(0, *x1_first[1:]))
    with jax.named_scope("inputs1"):
        x1_second = second_step(x1_first, ins[0][1])
        x1 = third_step(x1_first, x1_second, turned[0][1])
    with jax.named_scope("pairs0"):
        near0 = gather_sides(turned[0][1])
    ins.append(attention_in(1, x1))
    slab = w_out.shape[0] // sq_count
    w_slab = after(block_of(w_out, sq_rank, slab, 0), *ins[1][7])
    w_out_all = lax.all_gather(w_slab, ("tp", "sq"), axis=0, tiled=True)
    with jax.named_scope("cotangent"):
        grads_first = first_step(after(cotangent_rows, *ins[1][7]))
    with jax.named_scope("pairs0"):
        diag0 = gather_diagonal(turned[0][1], [after(side, x1[0][3]) for side in near0])
    turned.append(rotated(1, *diag0, *grads_first[1:]))
    with jax.named_scope("cotangent"):
        grads_second = second_step(grads_first, turned[1][1])
    with jax.named_scope("pairs0"):
        slots_c.append(gather_slots(turned[0][1], near0, *diag0))
    with jax.named_scope("pairs1"):
        near1 = gather_sides(turned[1][1])
    attn_c.append(attn_forward(after(info_c[0], turned[1][1]), turned[0][0], slots_c[0]))
    heads_c.append(gather_heads(0, grads_second))
    with jax.named_scope("pairs1"):
        near1 = [after(side, attn_c[0][2]) for side in near1]
        diag1 = gather_diagonal(turned[1][1], near1)
        slots_c.append(gather_slots(turned[1][1], near1, *diag1))
    with jax.named_scope("cotangent"):
        grads_third = third_step(grads_first, grads_second)
    attn_c.append(
        attn_forward(
            after(info_c[1], *early_parts(heads_c[0])), turned[1][0], slots_c[1]
        )
    )
    grad_all = joined_rows(rank, grads_third)

    def middle_of(c, *others):
        return middle_rows(
            after(rank, *others), heads_c[c], ins[c][0], w_out_all, ffn_gain, router, routes_c[c]
        )

    def hidden_of(c, *others):
        _, _, _, ffn_in, probs, routed = mids[c]
        return expert_hidden(
            after(info_c[c], *others), ffn_in, grad_all, probs, routed, w_gate, w_up, w_down, c
        )

    def back_of(c, *others):
        _, gate_grads, up_grads, inner = exps[c]
        return expert_back(
            after(info_c[c], *others),
            gate_grads,
            up_grads,
            inner,
            mids[c][4],
            router,
            mids[c][3],
            w_gate,
            w_up,
            tp_count,
        )

    def ffn_exchange(c, pieces):
        with jax.named_scope(f"ffn_grad{c}"):
            return exchange(pieces)

    def middle_grad_of(c, pieces, *others):
        return middle_back(
            after(info_c[c], *others), pieces, mids[c][1], mids[c][2], grad_all, ffn_gain, w_out_all, c
        )

    def mixture_of(c, *others):
        pieces = mixture(
            after(info_c[c], *others), exps[c][0], w_down, backs[c][2], tp_count
        )
        with jax.named_scope(f"mixture{c}"):
            return exchange(pieces)

    def output_of(c, pieces):
        total = block_of(mids[c][1], tp_rank, feat, 1)
        for piece in pieces:
            total = total + piece[:rows_n].astype(F32)
        return total.astype(BF16).reshape(per, size, feat).transpose(1, 0, 2)

    def attention_back(c, *others):
        return attn_backward(
            after(info_c[c], *others), turned[c][0], sent[c], *attn_c[c][1:], slots_c[c]
        )

    def cores_of(c):
        with jax.named_scope(f"pair_cores{c}"):
            return scatter_cores(dqs[c][2])

    def diagonal_of(c, received):
        if sq_count != 8:
            return None, []
        with jax.named_scope(f"pair_diagonal{c}"):
            diagonal = scatter_diagonal(dqs[c][1], received)
            return diagonal, send_halves(diagonal)

    def sides_of(c, received, diagonal):
        with jax.named_scope(f"pair_sides{c}"):
            return scatter_sides(dqs[c][1], received, diagonal)

    def stats_of(c, received, blocks):
        query_raw, key_raw, squares = ins[c][3:6]
        operands = (
            dqs[c][0],
            scatter_total(dqs[c][1], received, blocks),
            query_raw,
            key_raw,
            squares,
            query_gain[None, :],
            key_gain[None, :],
            cosine,
            sine,
        )
        stats, gain_qk = back_stats(operands, all_cols)
        with jax.named_scope(f"stats{c}"):
            stats = sum(exchange([stats] * tp_count))
        return operands, stats, gain_qk

    def first_of(c, operands, stats, *others):
        low, _, inv = ins[c][:3]
        raw, pieces, part = back_first(
            after(info_c[c], *others),
            operands,
            stats,
            low,
            inv,
            attn_gain,
            w_query,
            w_key,
            w_value,
            all_cols,
            tp_count,
        )
        with jax.named_scope(f"first{c}"):
            pieces = exchange(pieces)
        return raw, pieces, part

    scatter = lambda g: lax.psum_scatter(g, "sq", scatter_dimension=0, tiled=True)
    spread = lambda g: g.astype(F32).reshape(block, experts, -1).transpose(1, 0, 2)

    backs, dqs = [], []
    mids.append(middle_of(0, attn_c[1][2], *grads_second))
    exps.append(hidden_of(0))
    heads_c.append(gather_heads(1, (), (mids[0][3],), (exps[0][3],)))
    back0, router0 = back_of(0)
    sent0 = ffn_exchange(0, back0)
    mids.append(middle_of(1, back0[0]))
    exps.append(hidden_of(1))
    ffn_list = [m[3] for m in mids]
    w_down_part = weight_grad([grad_all], [e[0] for e in exps])
    backs.append(middle_grad_of(0, sent0, w_down_part))
    sent = [mixture_of(0, backs[0][1])]
    back1, router1 = back_of(1, sent[0][0])
    sent1 = ffn_exchange(1, back1)
    w_up_part = weight_grad(ffn_list, [exps[0][2], after(exps[1][2], back1[0])])
    w_gate_part = weight_grad(
        ffn_list, [exps[0][1], after(exps[1][1], w_up_part, *sent[0][1:])]
    )
    backs.append(middle_grad_of(1, sent1, w_gate_part))
    sent.append(mixture_of(1, backs[1][1]))
    dqs.append(attention_back(0, sent[1][0]))
    cores0 = cores_of(0)
    summed0, diagonal0 = diagonal_of(0, cores0)
    sums0, sides0 = sides_of(0, cores0, diagonal0)
    with jax.named_scope("low_rows0"):
        low0 = exchange([after(backs[0][1], *sent[1][1:])] * tp_count)
    dqs.append(attention_back(1, *sums0))
    cores1 = cores_of(1)
    operands0, stats0, gain0 = stats_of(0, after(cores0, dqs[1][0]), sides0)
    with jax.named_scope("low_rows1"):
        low1 = exchange([after(backs[1][1], *low0[1:])] * tp_count)
    low_all = ordered_rows(rank, [low0, low1])
    raw0, first0, part0 = first_of(0, operands0, stats0, cores1, *low0[1:])
    summed1, diagonal1 = diagonal_of(1, cores1)
    sums1, sides1 = sides_of(1, cores1, diagonal1)

    outputs = [output_of(c, sent[c]) for c in range(2)]
    operands1, stats1, gain1 = stats_of(1, cores1, sides1)
    raw1, first1, part1 = first_of(1, operands1, stats1, low_all, *first0[1:])
    w_down_rows = scatter(after(w_down_part, backs[0][1]))
    w_up_rows = scatter(after(w_up_part, backs[1][1]))
    w_gate_rows = scatter(after(w_gate_part, backs[1][1]))
    w_down_grad = w_down_rows.astype(F32).T.reshape(experts, -1, block)
    w_up_grad, w_gate_grad = spread(w_up_rows), spread(w_gate_rows)
    heads_own = [attn_c[c][0].reshape(rows_n, head_cols) for c in range(2)]
    with jax.named_scope("weights"):
        own = reduce_cores(
            info_c[0],
            [
                ([(i[1], 0) for i in ins], [raw0, raw1]),
                ([(low_all, 0), (low_all, 1)], heads_own),
            ],
        )
        qkv_grad = reduce_chips(own)
    finals = [
        finish(after(info_c[c], own), low_all, pieces, inputs_c[c], ins[c][2], attn_gain, c, per)
        for c, pieces in enumerate((first0, first1))
    ]
    w_out_grad = qkv_grad[:, 3 * head_cols :].T
    small = jnp.concatenate(
        [
            router0 + router1,
            (backs[0][0] + backs[1][0])[None, :],
            (part0 + after(part1, finals[1]))[None, :],
            lax.dynamic_update_slice_in_dim(
                jnp.zeros((2, all_cols), F32), gain0 + gain1, tp_rank * head_cols, 1
            ),
        ],
        axis=0,
    )
    with jax.named_scope("small"):
        small = butterfly(butterfly(small, "sq"), "tp")
    early, late = small[: experts_total + 1], small[experts_total + 1 :]
    return (
        jnp.concatenate(outputs, axis=1),
        jnp.concatenate(finals, axis=0).reshape(seqs, size, feat).transpose(1, 0, 2),
        late[0],
        qkv_grad[:, :head_cols],
        qkv_grad[:, head_cols : 2 * head_cols],
        qkv_grad[:, 2 * head_cols : 3 * head_cols],
        late[1],
        late[2],
        w_out_grad,
        early[experts_total],
        early[:experts_total].T,
        w_gate_grad,
        w_up_grad,
        w_down_grad,
    )


def solution(mesh):
    placed = (
        P("sq", None, "tp"),
        P(),
        P("sq", None, None),
        P(),
        P(None, "tp"),
        P(None, "tp"),
        P(None, "tp"),
        P("tp"),
        P("tp"),
        P("tp", None),
        P(),
        P(),
        P("tp", None, None),
        P("tp", None, None),
        P("tp", None, None),
        P("sq", None, "tp"),
    )
    return jax.shard_map(
        shards,
        mesh=mesh,
        in_specs=placed,
        out_specs=(
            P("sq", None, "tp"),
            P("sq", None, "tp"),
            P(),
            P("sq", "tp"),
            P("sq", "tp"),
            P("sq", "tp"),
            P(),
            P(),
            P("tp", "sq"),
            P(),
            P(),
            P("tp", "sq", None),
            P("tp", "sq", None),
            P("tp", None, "sq"),
        ),
        check_vma=False,
    )
```

time: 1660 us -> 1130 us (0.68)
  waiting for transfers between devices: 635 us -> 327 us
  Pallas kernels: 191 us -> 447 us
  matrix products: 193 us -> 0 us
  other arithmetic: 192 us -> 28.6 us
  local copies, waits for them, and re-layouts: 150 us -> 54.9 us
  starting transfers between devices: 267 us -> 248 us
    ppermute x69 -> x32, waiting for transfers between devices: 393 us -> 109 us  [swap(): lax.ppermute(block, axis, [(i, i ^ mask) for i in range(lax.axis_size(axi...]
    pallas_call x8 -> x39, Pallas kernels: 191 us -> 447 us  [the longest x2 73.8 us: expert_hidden(): pl.pallas_call(functools.partial(expert_hidden_kernel, tile), grid_spec=p...]
    dot_general x23 -> x0, matrix products: 193 us -> none  [the longest x22 191 us: dot(): return lax.dot_general(left, right, dims, preferred_element_type=F32)]
    concatenate x28 -> x7, other arithmetic: 59.2 us -> 3.72 us  [the longest x1 2.05 us: shards(): jnp.concatenate(outputs, axis=1)]
    ppermute x69 -> x32, starting transfers between devices: 152 us -> 96.7 us  [swap(): lax.ppermute(block, axis, [(i, i ^ mask) for i in range(lax.axis_size(axi...]
    ppermute x33 -> x36, starting transfers between devices: 47.9 us -> 97.3 us  [shift(): lax.ppermute(block, axis, [(i, (i + distance) % count) for i in range(cou...]
    convert_element_type x22 -> x4, other arithmetic: 47.5 us -> 6.44 us  [the longest x2 3.24 us: output_of(): return total.astype(BF16).reshape(per, size, feat).transpose(1, 0, 2)]
    unnamed x427 -> x202, local copies, waits for them, and re-layouts: 66.5 us -> 27.5 us
  transfers between devices with their start and end apart: 139 -> 97, of which waited for: 51 -> 36; matrix products, arithmetic and copies ran while one was open for 29% -> 5% of each run, Pallas kernels for 3% -> 38%
where the time goes in v2:
time: 1130 us; the launch traced here: 1120 us
  Pallas kernels  447 us (40%)
  waiting for transfers between devices  327 us (29%)
  starting transfers between devices  248 us (22%)
  local copies, waits for them, and re-layouts  54.9 us (5%)
  other arithmetic  28.6 us (3%)
  between operations  15.6 us (1%)
    ppermute x32, waiting for transfers between devices, swap(): lax.ppermute(block, axis, [(i, i ^ mask) for i in range(lax.axis_size(axi...  109 us
    ppermute x36, waiting for transfers between devices, shift(): lax.ppermute(block, axis, [(i, (i + distance) % count) for i in range(cou...  107 us
    ppermute x36, starting transfers between devices, shift(): lax.ppermute(block, axis, [(i, (i + distance) % count) for i in range(cou...  97.3 us
    ppermute x32, starting transfers between devices, swap(): lax.ppermute(block, axis, [(i, i ^ mask) for i in range(lax.axis_size(axi...  96.7 us
    pallas_call x2, Pallas kernels, expert_hidden(): pl.pallas_call(functools.partial(expert_hidden_kernel, tile), grid_spec=p...  73.8 us
    pallas_call x3, Pallas kernels, weight_grad(): pl.pallas_call(functools.partial(weight_grad_kernel, len(lefts), parts),...  70.2 us
    pallas_call x2, Pallas kernels, expert_back(): pl.pallas_call(functools.partial(expert_back_kernel, count), grid_spec=pl...  64.2 us
    ppermute x5, waiting for transfers between devices, second_step(): lax.ppermute(after(b1, a1, *others), 'tp', OUTER)  40.7 us
  transfers between devices with their start and end apart: 97, of which 36 were waited for; matrix products, arithmetic and copies ran while one was open for 5% of the time, Pallas kernels for 38%

profile of v2, /device:TPU:0, one launch (start us, length us, event | category | flops | bytes accessed | tf_op | source)
XLA Modules:
  0.0 1120.0 jit_solution(5680940131403300784)
XLA Ops:
  16.5 11.6 %collective-permute-done.refs_1_ = bf16[512,512]{1,0:T(8,128)(2,1)S(1)} collective-permute-done((bf16[512,512]{1,0:T(8,128)(2,1)S(1)}, bf16[512,512]{1,0:T(8,128)(2,1)S(1)}, u32[]{:S(2)}, u32[]{:S(2)}) %collective-permute-start) | collective-permute-done | bytes 524320 | tf_op jit(solution)/shard_map/inputs0/ppermute | solution.py:46
  32.3 10.5 collective-permute-done.3.refs_2_
  44.7 9.8 collective-permute-done.4.refs_3_
  59.4 8.5 front.2
  89.1 9.5 collective-permute-done.12.refs_3_
  98.6 8.5 front.3
  117.4 13.7 %collective-permute-done.17.refs_4_.refs_8_ = bf16[2,2,256,512]{3,2,1,0:T(8,128)(2,1)S(1)} collective-permute-done((bf16[2,2,256,512]{3,2,1,0:T(8,128)(2,1)S(1)}, bf16[2,2,256,512]{3,2,1,0:T(8,128)(2,1)S(1)}, u32[]{:S(2)}, u32[]{:S(2)}) %collective-permute-start.17) | collective-permute-done | bytes 1048608 | tf_op jit(solution)/shard_map/pairs0/ppermute | solution.py:37
  140.3 18.1 %collective-permute-done.19.refs_6_.refs_10_ = bf16[1,2,256,512]{3,2,1,0:T(8,128)(2,1)S(1)} collective-permute-done((bf16[1,2,256,512]{3,2,1,0:T(8,128)(2,1)S(1)}, bf16[1,2,256,512]{3,2,1,0:T(8,128)(2,1)S(1)}, u32[]{:S(2)}, u32[]{:S(2)}) %collective-permute-start.19) | collective-permute-done | bytes 524320 | tf_op jit(solution)/shard_map/pairs0/ppermute | solution.py:37
  159.3 12.4 %collective-permute-done.21.refs_1_ = bf16[1024,512]{1,0:T(8,128)(2,1)S(1)} collective-permute-done((bf16[1024,512]{1,0:T(8,128)(2,1)S(1)}, bf16[1024,512]{1,0:T(8,128)(2,1)S(1)}, u32[]{:S(2)}, u32[]{:S(2)}) %collective-permute-start.21) | collective-permute-done | bytes 1048608 | tf_op jit(solution)/shard_map/cotangent/ppermute | solution.py:46
  183.7 10.4 attn_forward.2
  194.1 16.6 %collective-permute-done.29.refs_4_.refs_8_ = bf16[2,2,256,512]{3,2,1,0:T(8,128)(2,1)S(1)} collective-permute-done((bf16[2,2,256,512]{3,2,1,0:T(8,128)(2,1)}, bf16[2,2,256,512]{3,2,1,0:T(8,128)(2,1)S(1)}, u32[]{:S(2)}, u32[]{:S(2)}) %collective-permute-start.29) | collective-permute-done | bytes 1048608 | tf_op jit(solution)/shard_map/pairs1/ppermute | solution.py:37
  216.6 20.2 %collective-permute-done.24.refs_2_ = bf16[1024,512]{1,0:T(8,128)(2,1)S(1)} collective-permute-done((bf16[1024,512]{1,0:T(8,128)(2,1)S(1)}, bf16[1024,512]{1,0:T(8,128)(2,1)S(1)}, u32[]{:S(2)}, u32[]{:S(2)}) %collective-permute-start.24) | collective-permute-done | bytes 1048608 | tf_op jit(solution)/shard_map/cotangent/ppermute | solution.py:55
  245.2 10.9 collective-permute-done.26.refs_1_
  261.0 10.0 collective-permute-done.34.refs_2_
  275.6 10.3 attn_forward.3
  290.3 14.5 %collective-permute-done.36.refs_3_ = bf16[512,512]{1,0:T(8,128)(2,1)} collective-permute-done((bf16[512,512]{1,0:T(8,128)(2,1)}, bf16[512,512]{1,0:T(8,128)(2,1)}, u32[]{:S(2)}, u32[]{:S(2)}) %collective-permute-start.36) | collective-permute-done | bytes 524320 | tf_op jit(solution)/shard_map/heads0/ppermute | solution.py:65
  304.8 12.2 %middle_rows.2 = (bf16[512,2048]{1,0:T(8,128)(2,1)}, f32[512,2048]{1,0:T(8,128)}, f32[512,1]{1,0:T(8,128)}, bf16[512,2048]{1,0:T(8,128)(2,1)}, f32[512,16]{1,0:T(8,128)}, /*index=5*/f32[512,16]{1,0:T(8,128)}) custom-call(s32[1]{0:T(128)} %bitcast.info, bf16[512,512]{1,0:T(8,128)(2,1)} %bitcast.109, bf16[512,512]{1,0:T(8,128)(2,1)} %copy-done.62, ...), custom_call_target="tpu_custom_call" | custom-call | flops 42949672 | bytes 209715 | tf_op jit(solution)/shard_map/middle_rows/pallas_call | solution.py:622
  325.8 36.9 %expert_hidden.2 = (bf16[512,4096]{1,0:T(8,128)(2,1)}, bf16[512,4096]{1,0:T(8,128)(2,1)}, bf16[512,4096]{1,0:T(8,128)(2,1)}, f32[512,16]{1,0:T(8,128)}) custom-call(s32[4]{0:T(128)} %pad_add_fusion.2.info, bf16[512,2048]{1,0:T(8,128)(2,1)} %get-tuple-element.200.x_ref.refs_0_, bf16[1024,2048]{1,0:T(8,128)(2,1)} %joined_rows.1.g_ref.refs_0_.refs_6_, ...), custom_call_target="tpu_custom_call" | custom-call | flops 257698032 | bytes 629145 | tf_op jit(solution)/shard_map/expert_hidden/pallas_call | solution.py:914
  364.6 31.1 %expert_back.2 = (bf16[128,2048]{1,0:T(8,128)(2,1)}, bf16[128,2048]{1,0:T(8,128)(2,1)}, bf16[128,2048]{1,0:T(8,128)(2,1)}, bf16[128,2048]{1,0:T(8,128)(2,1)}, f32[512,16]{1,0:T(8,128)}, /*index=5*/f32[16,2048]{1,0:T(8,128)}) custom-call(s32[4]{0:T(128)} %pad_add_fusion.2.info, bf16[512,4096]{1,0:T(8,128)(2,1)} %get-tuple-element.204.gp_ref.refs_2_, ...), custom_call_target="tpu_custom_call" | custom-call | flops 171798688 | bytes 461373 | tf_op jit(solution)/shard_map/expert_back/pallas_call | solution.py:987
  401.7 12.2 %middle_rows.3 = (bf16[512,2048]{1,0:T(8,128)(2,1)}, f32[512,2048]{1,0:T(8,128)}, f32[512,1]{1,0:T(8,128)}, bf16[512,2048]{1,0:T(8,128)(2,1)}, f32[512,16]{1,0:T(8,128)}, /*index=5*/f32[512,16]{1,0:T(8,128)}) custom-call(s32[1]{0:T(128)} %bitcast.info, bf16[512,512]{1,0:T(8,128)(2,1)} %bitcast.116, bf16[512,512]{1,0:T(8,128)(2,1)} %copy-done.60, ...), custom_call_target="tpu_custom_call" | custom-call | flops 42949672 | bytes 209715 | tf_op jit(solution)/shard_map/middle_rows/pallas_call | solution.py:622
  414.0 36.9 %expert_hidden.3 = (bf16[512,4096]{1,0:T(8,128)(2,1)}, bf16[512,4096]{1,0:T(8,128)(2,1)}, bf16[512,4096]{1,0:T(8,128)(2,1)}, f32[512,16]{1,0:T(8,128)}) custom-call(s32[4]{0:T(128)} %pad_add_fusion.info, bf16[512,2048]{1,0:T(8,128)(2,1)} %get-tuple-element.214.x_ref.refs_1_, bf16[1024,2048]{1,0:T(8,128)(2,1)} %joined_rows.1.g_ref.refs_0_.refs_6_, ...), custom_call_target="tpu_custom_call" | custom-call | flops 257698032 | bytes 629145 | tf_op jit(solution)/shard_map/expert_hidden/pallas_call | solution.py:914
  450.9 23.2 %weight_grad.3 = bf16[2048,4096]{1,0:T(8,128)(2,1)} custom-call(bf16[1024,2048]{1,0:T(8,128)(2,1)} %joined_rows.1.g_ref.refs_0_.refs_6_, bf16[512,4096]{1,0:T(8,128)(2,1)} %get-tuple-element.203.refs_1_.hidden_ref, bf16[512,4096]{1,0:T(8,128)(2,1)} %get-tuple-element.217.refs_2_.hidden_ref), custom_call_target="tpu_custom_call" | custom-call | flops 171798688 | bytes 293601 | tf_op jit(solution)/shard_map/weight_grad/pallas_call | solution.py:672
  475.2 9.3 middle_back.2
  484.6 16.2 %mixture.2 = (bf16[640,512]{1,0:T(8,128)(2,1)}, bf16[640,512]{1,0:T(8,128)(2,1)}, bf16[640,512]{1,0:T(8,128)(2,1)}, bf16[640,512]{1,0:T(8,128)(2,1)}) custom-call(s32[4]{0:T(128)} %pad_add_fusion.2.info, bf16[512,4096]{1,0:T(8,128)(2,1)} %get-tuple-element.203.refs_1_.hidden_ref, bf16[4096,2048]{1,0:T(8,128)(2,1)} %bitcast.94, ...), custom_call_target="tpu_custom_call" | custom-call | flops 85899344 | bytes 230686 | tf_op jit(solution)/shard_map/mixture/pallas_call | solution.py:1041
  505.2 33.1 %expert_back.3 = (bf16[128,2048]{1,0:T(8,128)(2,1)}, bf16[128,2048]{1,0:T(8,128)(2,1)}, bf16[128,2048]{1,0:T(8,128)(2,1)}, bf16[128,2048]{1,0:T(8,128)(2,1)}, f32[512,16]{1,0:T(8,128)}, /*index=5*/f32[16,2048]{1,0:T(8,128)}) custom-call(s32[4]{0:T(128)} %pad_add_fusion.info, bf16[512,4096]{1,0:T(8,128)(2,1)} %get-tuple-element.240.gp_ref.refs_3_, ...), custom_call_target="tpu_custom_call" | custom-call | flops 171798688 | bytes 461373 | tf_op jit(solution)/shard_map/expert_back/pallas_call | solution.py:987
  543.5 23.3 %weight_grad.4 = bf16[2048,4096]{1,0:T(8,128)(2,1)} custom-call(bf16[512,2048]{1,0:T(8,128)(2,1)} %get-tuple-element.200.x_ref.refs_0_, bf16[512,2048]{1,0:T(8,128)(2,1)} %get-tuple-element.214.x_ref.refs_1_, bf16[512,4096]{1,0:T(8,128)(2,1)} %get-tuple-element.205.up_ref.refs_2_, bf16[512,4096]{1,0:T(8,128)(2,1)} %get-tuple-element.239.up_ref.refs_3_), custom_call_target="tpu_custom_call" | custom-call | flops 171798688 | bytes 293601 | tf_op jit(solution)/shard_map/weight_grad/pallas_call | solution.py:672
  566.8 23.8 %weight_grad.5 = bf16[2048,4096]{1,0:T(8,128)(2,1)} custom-call(bf16[512,2048]{1,0:T(8,128)(2,1)} %get-tuple-element.200.x_ref.refs_0_, bf16[512,2048]{1,0:T(8,128)(2,1)} %get-tuple-element.214.x_ref.refs_1_, bf16[512,4096]{1,0:T(8,128)(2,1)} %get-tuple-element.204.gp_ref.refs_2_, bf16[512,4096]{1,0:T(8,128)(2,1)} %get-tuple-element.240.gp_ref.refs_3_), custom_call_target="tpu_custom_call" | custom-call | flops 171798688 | bytes 293601 | tf_op jit(solution)/shard_map/weight_grad/pallas_call | solution.py:672
  591.6 9.4 middle_back.3
  601.6 15.5 %mixture.3 = (bf16[640,512]{1,0:T(8,128)(2,1)}, bf16[640,512]{1,0:T(8,128)(2,1)}, bf16[640,512]{1,0:T(8,128)(2,1)}, bf16[640,512]{1,0:T(8,128)(2,1)}) custom-call(s32[4]{0:T(128)} %pad_add_fusion.info, bf16[512,4096]{1,0:T(8,128)(2,1)} %get-tuple-element.217.refs_2_.hidden_ref, bf16[4096,2048]{1,0:T(8,128)(2,1)} %bitcast.95, ...), custom_call_target="tpu_custom_call" | custom-call | flops 85899344 | bytes 230686 | tf_op jit(solution)/shard_map/mixture/pallas_call | solution.py:1041
  617.1 13.5 %attn_backward.2 = (bf16[2,256,512]{2,1,0:T(8,128)(2,1)}, bf16[4,2,2,256,512]{4,3,2,1,0:T(8,128)(2,1)}, bf16[4,2,2,256,512]{4,3,2,1,0:T(8,128)(2,1)}) custom-call(s32[4]{0:T(128)} %pad_add_fusion.2.info, bf16[2,256,512]{2,1,0:T(8,128)(2,1)} %get-tuple-element.181.q_ref, f32[2,256,512]{2,1,0:T(8,128)} %get-tuple-element.258.full_ref, ...), custom_call_target="tpu_custom_call" | custom-call | flops 107374184 | bytes 209715 | tf_op jit(solution)/shard_map/attn_backward/pallas_call | solution.py:837
  630.6 17.7 %collective-permute-start.52 = (bf16[640,512]{1,0:T(8,128)(2,1)}, bf16[640,512]{1,0:T(8,128)(2,1)S(1)}, u32[]{:S(2)}, u32[]{:S(2)}) collective-permute-start(bf16[640,512]{1,0:T(8,128)(2,1)} %get-tuple-element.253), channel_id=1, source_target_pairs={{0,1},{1,2},{2,3},{3,0},{4,5},{5,6},{6,7},{7,4},{8,9},{9,10},{10,1... | collective-permute-start | bytes 1966088 | tf_op jit(solution)/shard_map/mixture1/ppermute | solution.py:33
  661.4 12.7 %collective-permute-start.56 = (bf16[2,256,512]{2,1,0:T(8,128)(2,1)S(1)}, bf16[2,256,512]{2,1,0:T(8,128)(2,1)S(1)}, u32[]{:S(2)}, u32[]{:S(2)}) collective-permute-start(bf16[2,256,512]{2,1,0:T(8,128)(2,1)S(1)} %get-tuple-element.331), channel_id=1, source_target_pairs={{0,16},{4,20},{8,24},{12,28},{16,0},{20,4},{24,8},{28,12},{1,17},{... | collective-permute-start | bytes 1572872 | tf_op jit(solution)/shard_map/pair_diagonal0/ppermute | solution.py:37
  674.1 10.9 collective-permute-done.57.refs_2_
  688.4 9.3 collective-permute-done.56.refs_4_
  702.7 13.4 %attn_backward.3 = (bf16[2,256,512]{2,1,0:T(8,128)(2,1)}, bf16[4,2,2,256,512]{4,3,2,1,0:T(8,128)(2,1)}, bf16[4,2,2,256,512]{4,3,2,1,0:T(8,128)(2,1)}) custom-call(s32[4]{0:T(128)} %pad_add_fusion.info, bf16[2,256,512]{2,1,0:T(8,128)(2,1)} %get-tuple-element.187.q_ref, f32[2,256,512]{2,1,0:T(8,128)} %get-tuple-element.262.full_ref, ...), custom_call_target="tpu_custom_call" | custom-call | flops 107374184 | bytes 209715 | tf_op jit(solution)/shard_map/attn_backward/pallas_call | solution.py:837
  731.0 21.4 %collective-permute-start.73 = (bf16[2,256,512]{2,1,0:T(8,128)(2,1)S(1)}, bf16[2,256,512]{2,1,0:T(8,128)(2,1)S(1)}, u32[]{:S(2)}, u32[]{:S(2)}) collective-permute-start(bf16[2,256,512]{2,1,0:T(8,128)(2,1)S(1)} %get-tuple-element.329), channel_id=1, source_target_pairs={{0,16},{4,20},{8,24},{12,28},{16,0},{20,4},{24,8},{28,12},{1,17},{... | collective-permute-start | bytes 1572872 | tf_op jit(solution)/shard_map/pair_diagonal1/ppermute | solution.py:37
  752.3 14.1 %collective-permute-start.75 = (bf16[2,256,512]{2,1,0:T(8,128)(2,1)S(1)}, bf16[2,256,512]{2,1,0:T(8,128)(2,1)S(1)}, u32[]{:S(2)}, u32[]{:S(2)}) collective-permute-start(bf16[2,256,512]{2,1,0:T(8,128)(2,1)S(1)} %get-tuple-element.328), channel_id=1, source_target_pairs={{0,8},{4,12},{8,0},{12,4},{16,24},{20,28},{24,16},{28,20},{1,9},{5... | collective-permute-start | bytes 1572872 | tf_op jit(solution)/shard_map/pair_diagonal1/ppermute | solution.py:37
  779.2 10.9 collective-permute-start.74
  792.7 15.5 %collective-permute-done.60.refs_2_ = bf16[128,2048]{1,0:T(8,128)(2,1)S(1)} collective-permute-done((bf16[128,2048]{1,0:T(8,128)(2,1)}, bf16[128,2048]{1,0:T(8,128)(2,1)S(1)}, u32[]{:S(2)}, u32[]{:S(2)}) %collective-permute-start.60) | collective-permute-done | bytes 524320 | tf_op jit(solution)/shard_map/low_rows0/ppermute | solution.py:33
  819.4 11.0 collective-permute-start.66
  843.1 11.9 %back_first.2 = (bf16[512,1536]{1,0:T(8,128)(2,1)}, f32[1,2048]{1,0:T(1,128)}, bf16[528,512]{1,0:T(8,128)(2,1)}, bf16[528,512]{1,0:T(8,128)(2,1)}, bf16[528,512]{1,0:T(8,128)(2,1)}, /*index=5*/bf16[528,512]{1,0:T(8,128)(2,1)}) custom-call(s32[4]{0:T(128)} %pad_add_fusion.2.info, bf16[2,256,512]{2,1,0:T(8,128)(2,1)} %get-tuple-element.266.refs_0_, ...), custom_call_target="tpu_custom_call" | custom-call | flops 32212254 | bytes 146800 | tf_op jit(solution)/shard_map/back_first/pallas_call | solution.py:485
  876.2 58.0 %collective-permute-done.68.refs_6_ = bf16[128,2048]{1,0:T(8,128)(2,1)S(1)} collective-permute-done((bf16[128,2048]{1,0:T(8,128)(2,1)S(1)}, bf16[128,2048]{1,0:T(8,128)(2,1)S(1)}, u32[]{:S(2)}, u32[]{:S(2)}) %collective-permute-start.68) | collective-permute-done | bytes 524320 | tf_op jit(solution)/shard_map/low_rows1/ppermute | solution.py:33
  942.0 11.6 %back_first.3 = (bf16[512,1536]{1,0:T(8,128)(2,1)}, f32[1,2048]{1,0:T(1,128)}, bf16[528,512]{1,0:T(8,128)(2,1)}, bf16[528,512]{1,0:T(8,128)(2,1)}, bf16[528,512]{1,0:T(8,128)(2,1)}, /*index=5*/bf16[528,512]{1,0:T(8,128)(2,1)}) custom-call(s32[4]{0:T(128)} %pad_add_fusion.info, bf16[2,256,512]{2,1,0:T(8,128)(2,1)} %get-tuple-element.267.refs_0_, ...), custom_call_target="tpu_custom_call" | custom-call | flops 32212254 | bytes 146800 | tf_op jit(solution)/shard_map/back_first/pallas_call | solution.py:485
  953.7 9.9 relative_grads.2
  971.1 10.6 relative_grads.3
  981.7 21.9 %collective-permute-done.82.refs_3_ = bf16[528,512]{1,0:T(8,128)(2,1)S(1)} collective-permute-done((bf16[528,512]{1,0:T(8,128)(2,1)S(1)}, bf16[528,512]{1,0:T(8,128)(2,1)S(1)}, u32[]{:S(2)}, u32[]{:S(2)}) %collective-permute-start.82) | collective-permute-done | bytes 540704 | tf_op jit(solution)/shard_map/first1/ppermute | solution.py:33
  1031.5 12.0 %collective-permute-start.87 = (f32[20,2048]{1,0:T(8,128)S(1)}, f32[20,2048]{1,0:T(8,128)S(1)}, u32[]{:S(2)}, u32[]{:S(2)}) collective-permute-start(f32[20,2048]{1,0:T(8,128)S(1)} %add.164), channel_id=1, source_target_pairs={{0,1},{1,0},{2,3},{3,2},{4,5},{5,4},{6,7},{7,6},{8,9},{9,8},{10,11... | collective-permute-start | bytes 491528 | tf_op jit(solution)/shard_map/small/ppermute | solution.py:37
  1061.8 18.7 %collective-permute-done.89 = bf16[2,256,1024]{2,1,0:T(8,128)(2,1)S(1)} collective-permute-done((bf16[2,256,1024]{2,1,0:T(8,128)(2,1)S(1)}, bf16[2,256,1024]{2,1,0:T(8,128)(2,1)S(1)}, u32[]{:S(2)}, u32[]{:S(2)}) %collective-permute-start.89) | collective-permute-done | bytes 1048608 | tf_op jit(solution)/shard_map/weights/ppermute | solution.py:37
  (456 shorter events, 321.1 us)
Async XLA Ops:
  7.2 297.6 %all-gather.2.cloned.1.call-start = ((), (), s32[]{:S(2)}) async-start(), calls=%async_computation.3 | async-start | bytes 8650752 | tf_op jit(solution)/shard_map/all_gather | solution.py:1280
  114.3 980.3 %reduce-scatter.8.cloned.1.call-start = ((), (), s32[]{:S(2)}) async-start(), calls=%async_computation.6 | async-start | bytes 18874368 | tf_op jit(solution)/shard_map/reduce_scatter | solution.py:1412
  132.9 38.7 %collective-permute-start.18 = (bf16[3,2,2,256,512]{4,3,2,1,0:T(8,128)(2,1)S(1)}, bf16[3,2,2,256,512]{4,3,2,1,0:T(8,128)(2,1)}, u32[]{:S(2)}, u32[]{:S(2)}) collective-permute-start(bf16[3,2,2,256,512]{4,3,2,1,0:T(8,128)(2,1)S(1)} %pad_maximum_fusion), channel_id=1, source_target_pairs={{0,4},{4,0},{8,12},{12,8},{16,20},{20,16},{24,28},{28,24},{1,5},{5... | collective-permute-start | bytes 9437192 | tf_op jit(solution)/shard_map/pairs0/ppermute | solution.py:37
  135.6 36.1 %collective-permute-start.21 = (bf16[1024,512]{1,0:T(8,128)(2,1)S(1)}, bf16[1024,512]{1,0:T(8,128)(2,1)S(1)}, u32[]{:S(2)}, u32[]{:S(2)}) collective-permute-start(bf16[1024,512]{1,0:T(8,128)(2,1)S(1)} %bitcast.131), channel_id=1, source_target_pairs={{0,1},{1,0},{2,3},{3,2},{4,5},{5,4},{6,7},{7,6},{8,9},{9,8},{10,11... | collective-permute-start | bytes 3145736 | tf_op jit(solution)/shard_map/cotangent/ppermute | solution.py:46
  175.9 34.8 %collective-permute-start.29 = (bf16[2,2,256,512]{3,2,1,0:T(8,128)(2,1)}, bf16[2,2,256,512]{3,2,1,0:T(8,128)(2,1)S(1)}, u32[]{:S(2)}, u32[]{:S(2)}) collective-permute-start(bf16[2,2,256,512]{3,2,1,0:T(8,128)(2,1)} %get-tuple-element.179.refs_0_.refs_4_), channel_id=1, source_target_pairs={{0,16},{4,20},{8,24},{12,28},{16,0},{20,4},{24,8},{28,12},{1,17},{... | collective-permute-start | bytes 3145736 | tf_op jit(solution)/shard_map/pairs1/ppermute | solution.py:37
  177.0 33.7 %collective-permute-start.28 = (bf16[2,2,256,512]{3,2,1,0:T(8,128)(2,1)}, bf16[2,2,256,512]{3,2,1,0:T(8,128)(2,1)S(1)}, u32[]{:S(2)}, u32[]{:S(2)}) collective-permute-start(bf16[2,2,256,512]{3,2,1,0:T(8,128)(2,1)} %get-tuple-element.179.refs_0_.refs_4_), channel_id=1, source_target_pairs={{0,8},{4,12},{8,0},{12,4},{16,24},{20,28},{24,16},{28,20},{1,9},{5... | collective-permute-start | bytes 3145736 | tf_op jit(solution)/shard_map/pairs1/ppermute | solution.py:37
  211.2 61.6 %collective-permute-start.30 = (bf16[3,2,2,256,512]{4,3,2,1,0:T(8,128)(2,1)S(1)}, bf16[3,2,2,256,512]{4,3,2,1,0:T(8,128)(2,1)S(1)}, u32[]{:S(2)}, u32[]{:S(2)}) collective-permute-start(bf16[3,2,2,256,512]{4,3,2,1,0:T(8,128)(2,1)S(1)} %pad_maximum_fusion.1), channel_id=1, source_target_pairs={{0,4},{4,0},{8,12},{12,8},{16,20},{20,16},{24,28},{28,24},{1,5},{5... | collective-permute-start | bytes 9437192 | tf_op jit(solution)/shard_map/pairs1/ppermute | solution.py:37
  214.5 30.5 %collective-permute-start.31 = (bf16[1,2,256,512]{3,2,1,0:T(8,128)(2,1)S(1)}, bf16[1,2,256,512]{3,2,1,0:T(8,128)(2,1)S(1)}, u32[]{:S(2)}, u32[]{:S(2)}) collective-permute-start(bf16[1,2,256,512]{3,2,1,0:T(8,128)(2,1)S(1)} %slice.173), channel_id=1, source_target_pairs={{0,8},{4,12},{8,0},{12,4},{16,24},{20,28},{24,16},{28,20},{1,9},{5... | collective-permute-start | bytes 1572872 | tf_op jit(solution)/shard_map/pairs1/ppermute | solution.py:37
  245.1 29.4 %collective-permute-start.33 = (bf16[2,2,256,512]{3,2,1,0:T(8,128)(2,1)S(1)}, bf16[2,2,256,512]{3,2,1,0:T(8,128)(2,1)S(1)}, u32[]{:S(2)}, u32[]{:S(2)}) collective-permute-start(bf16[2,2,256,512]{3,2,1,0:T(8,128)(2,1)S(1)} %pad_maximum_fusion.4), channel_id=1, source_target_pairs={{0,4},{4,0},{8,12},{12,8},{16,20},{20,16},{24,28},{28,24},{1,5},{5... | collective-permute-start | bytes 3145736 | tf_op jit(solution)/shard_map/pairs1/ppermute | solution.py:37
  259.9 59.8 %collective-permute-start.37 = (bf16[1024,512]{1,0:T(8,128)(2,1)}, bf16[1024,512]{1,0:T(8,128)(2,1)S(1)}, u32[]{:S(2)}, u32[]{:S(2)}) collective-permute-start(bf16[1024,512]{1,0:T(8,128)(2,1)} %collective-permute-done.25.refs_5_), channel_id=1, source_target_pairs={{0,1},{1,0},{2,3},{3,2},{4,5},{5,4},{6,7},{7,6},{8,9},{9,8},{10,11... | collective-permute-start | bytes 3145736 | tf_op jit(solution)/shard_map/cotangent/ppermute | solution.py:65
  271.0 33.8 %collective-permute-start.36 = (bf16[512,512]{1,0:T(8,128)(2,1)}, bf16[512,512]{1,0:T(8,128)(2,1)}, u32[]{:S(2)}, u32[]{:S(2)}) collective-permute-start(bf16[512,512]{1,0:T(8,128)(2,1)} %collective-permute-done.35.refs_5_), channel_id=1, source_target_pairs={{0,1},{1,0},{2,3},{3,2},{4,5},{5,4},{6,7},{7,6},{8,9},{9,8},{10,11... | collective-permute-start | bytes 1572872 | tf_op jit(solution)/shard_map/heads0/ppermute | solution.py:65
  285.9 31.2 %collective-permute-start.39 = (bf16[512,512]{1,0:T(8,128)(2,1)}, bf16[512,512]{1,0:T(8,128)(2,1)S(1)}, u32[]{:S(2)}, u32[]{:S(2)}) collective-permute-start(bf16[512,512]{1,0:T(8,128)(2,1)} %bitcast.114), channel_id=1, source_target_pairs={{0,0},{1,2},{2,1},{3,3},{4,4},{5,6},{6,5},{7,7},{8,8},{9,10},{10,9... | collective-permute-start | bytes 1572872 | tf_op jit(solution)/shard_map/heads1/ppermute | solution.py:46
  287.6 29.5 %collective-permute-start.38 = (bf16[512,512]{1,0:T(8,128)(2,1)}, bf16[512,512]{1,0:T(8,128)(2,1)S(1)}, u32[]{:S(2)}, u32[]{:S(2)}) collective-permute-start(bf16[512,512]{1,0:T(8,128)(2,1)} %bitcast.115), channel_id=1, source_target_pairs={{0,1},{1,0},{2,3},{3,2},{4,5},{5,4},{6,7},{7,6},{8,9},{9,8},{10,11... | collective-permute-start | bytes 1572872 | tf_op jit(solution)/shard_map/heads1/ppermute | solution.py:46
  317.1 45.7 %collective-permute-start.40 = (bf16[512,512]{1,0:T(8,128)(2,1)S(1)}, bf16[512,512]{1,0:T(8,128)(2,1)S(1)}, u32[]{:S(2)}, u32[]{:S(2)}) collective-permute-start(bf16[512,512]{1,0:T(8,128)(2,1)S(1)} %collective-permute-done.39.refs_4_), channel_id=1, source_target_pairs={{0,1},{1,0},{2,3},{3,2},{4,5},{5,4},{6,7},{7,6},{8,9},{9,8},{10,11... | collective-permute-start | bytes 1572872 | tf_op jit(solution)/shard_map/heads1/ppermute | solution.py:55
  318.9 43.9 %collective-permute-start.41 = (bf16[512,512]{1,0:T(8,128)(2,1)S(1)}, bf16[512,512]{1,0:T(8,128)(2,1)S(1)}, u32[]{:S(2)}, u32[]{:S(2)}) collective-permute-start(bf16[512,512]{1,0:T(8,128)(2,1)S(1)} %collective-permute-done.38.refs_1_), channel_id=1, source_target_pairs={{0,0},{1,2},{2,1},{3,3},{4,4},{5,6},{6,5},{7,7},{8,8},{9,10},{10,9... | collective-permute-start | bytes 1572872 | tf_op jit(solution)/shard_map/heads1/ppermute | solution.py:56
  362.8 38.2 %collective-permute-start.42 = (bf16[512,512]{1,0:T(8,128)(2,1)S(1)}, bf16[512,512]{1,0:T(8,128)(2,1)S(1)}, u32[]{:S(2)}, u32[]{:S(2)}) collective-permute-start(bf16[512,512]{1,0:T(8,128)(2,1)S(1)} %collective-permute-done.41.refs_5_), channel_id=1, source_target_pairs={{0,1},{1,0},{2,3},{3,2},{4,5},{5,4},{6,7},{7,6},{8,9},{9,8},{10,11... | collective-permute-start | bytes 1572872 | tf_op jit(solution)/shard_map/heads1/ppermute | solution.py:65
  395.8 78.3 %collective-permute-start.43 = (bf16[128,2048]{1,0:T(8,128)(2,1)}, bf16[128,2048]{1,0:T(8,128)(2,1)S(1)}, u32[]{:S(2)}, u32[]{:S(2)}) collective-permute-start(bf16[128,2048]{1,0:T(8,128)(2,1)} %get-tuple-element.219), channel_id=1, source_target_pairs={{0,1},{1,2},{2,3},{3,0},{4,5},{5,6},{6,7},{7,4},{8,9},{9,10},{10,1... | collective-permute-start | bytes 1572872 | tf_op jit(solution)/shard_map/ffn_grad0/ppermute | solution.py:33
  396.1 78.0 %collective-permute-start.44 = (bf16[128,2048]{1,0:T(8,128)(2,1)}, bf16[128,2048]{1,0:T(8,128)(2,1)S(1)}, u32[]{:S(2)}, u32[]{:S(2)}) collective-permute-start(bf16[128,2048]{1,0:T(8,128)(2,1)} %get-tuple-element.220), channel_id=1, source_target_pairs={{0,2},{1,3},{2,0},{3,1},{4,6},{5,7},{6,4},{7,5},{8,10},{9,11},{10,... | collective-permute-start | bytes 1572872 | tf_op jit(solution)/shard_map/ffn_grad0/ppermute | solution.py:33
  399.0 75.1 %collective-permute-start.45 = (bf16[128,2048]{1,0:T(8,128)(2,1)}, bf16[128,2048]{1,0:T(8,128)(2,1)S(1)}, u32[]{:S(2)}, u32[]{:S(2)}) collective-permute-start(bf16[128,2048]{1,0:T(8,128)(2,1)} %get-tuple-element.221), channel_id=1, source_target_pairs={{0,3},{1,0},{2,1},{3,2},{4,7},{5,4},{6,5},{7,6},{8,11},{9,8},{10,9... | collective-permute-start | bytes 1572872 | tf_op jit(solution)/shard_map/ffn_grad0/ppermute | solution.py:33
  484.5 619.7 %reduce-scatter.6.cloned.1.call-start = ((), (), s32[]{:S(2)}) async-start(), calls=%async_computation.5 | async-start | bytes 18874368 | tf_op jit(solution)/shard_map/reduce_scatter | solution.py:1412
  500.8 39.9 %collective-permute-start.46 = (bf16[640,512]{1,0:T(8,128)(2,1)}, bf16[640,512]{1,0:T(8,128)(2,1)S(1)}, u32[]{:S(2)}, u32[]{:S(2)}) collective-permute-start(bf16[640,512]{1,0:T(8,128)(2,1)} %get-tuple-element.230), channel_id=1, source_target_pairs={{0,1},{1,2},{2,3},{3,0},{4,5},{5,6},{6,7},{7,4},{8,9},{9,10},{10,1... | collective-permute-start | bytes 1966088 | tf_op jit(solution)/shard_map/mixture0/ppermute | solution.py:33
  501.5 65.2 %collective-permute-start.47 = (bf16[640,512]{1,0:T(8,128)(2,1)}, bf16[640,512]{1,0:T(8,128)(2,1)S(1)}, u32[]{:S(2)}, u32[]{:S(2)}) collective-permute-start(bf16[640,512]{1,0:T(8,128)(2,1)} %get-tuple-element.231), channel_id=1, source_target_pairs={{0,2},{1,3},{2,0},{3,1},{4,6},{5,7},{6,4},{7,5},{8,10},{9,11},{10,... | collective-permute-start | bytes 1966088 | tf_op jit(solution)/shard_map/mixture0/ppermute | solution.py:33
  501.9 64.9 %collective-permute-start.48 = (bf16[640,512]{1,0:T(8,128)(2,1)}, bf16[640,512]{1,0:T(8,128)(2,1)S(1)}, u32[]{:S(2)}, u32[]{:S(2)}) collective-permute-start(bf16[640,512]{1,0:T(8,128)(2,1)} %get-tuple-element.232), channel_id=1, source_target_pairs={{0,3},{1,0},{2,1},{3,2},{4,7},{5,4},{6,5},{7,6},{8,11},{9,8},{10,9... | collective-permute-start | bytes 1966088 | tf_op jit(solution)/shard_map/mixture0/ppermute | solution.py:33
  538.3 52.3 %collective-permute-start.49 = (bf16[128,2048]{1,0:T(8,128)(2,1)}, bf16[128,2048]{1,0:T(8,128)(2,1)S(1)}, u32[]{:S(2)}, u32[]{:S(2)}) collective-permute-start(bf16[128,2048]{1,0:T(8,128)(2,1)} %get-tuple-element.242), channel_id=1, source_target_pairs={{0,1},{1,2},{2,3},{3,0},{4,5},{5,6},{6,7},{7,4},{8,9},{9,10},{10,1... | collective-permute-start | bytes 1572872 | tf_op jit(solution)/shard_map/ffn_grad1/ppermute | solution.py:33
  539.4 51.2 %collective-permute-start.50 = (bf16[128,2048]{1,0:T(8,128)(2,1)}, bf16[128,2048]{1,0:T(8,128)(2,1)S(1)}, u32[]{:S(2)}, u32[]{:S(2)}) collective-permute-start(bf16[128,2048]{1,0:T(8,128)(2,1)} %get-tuple-element.243), channel_id=1, source_target_pairs={{0,2},{1,3},{2,0},{3,1},{4,6},{5,7},{6,4},{7,5},{8,10},{9,11},{10,... | collective-permute-start | bytes 1572872 | tf_op jit(solution)/shard_map/ffn_grad1/ppermute | solution.py:33
  540.6 50.0 %collective-permute-start.51 = (bf16[128,2048]{1,0:T(8,128)(2,1)}, bf16[128,2048]{1,0:T(8,128)(2,1)}, u32[]{:S(2)}, u32[]{:S(2)}) collective-permute-start(bf16[128,2048]{1,0:T(8,128)(2,1)} %get-tuple-element.244), channel_id=1, source_target_pairs={{0,3},{1,0},{2,1},{3,2},{4,7},{5,4},{6,5},{7,6},{8,11},{9,8},{10,9... | collective-permute-start | bytes 1572872 | tf_op jit(solution)/shard_map/ffn_grad1/ppermute | solution.py:33
  601.0 507.6 %reduce-scatter.4.cloned.1.call-start = ((), (), s32[]{:S(2)}) async-start(), calls=%async_computation.4 | async-start | bytes 18874368 | tf_op jit(solution)/shard_map/reduce_scatter | solution.py:1412
  630.6 70.7 %collective-permute-start.52 = (bf16[640,512]{1,0:T(8,128)(2,1)}, bf16[640,512]{1,0:T(8,128)(2,1)S(1)}, u32[]{:S(2)}, u32[]{:S(2)}) collective-permute-start(bf16[640,512]{1,0:T(8,128)(2,1)} %get-tuple-element.253), channel_id=1, source_target_pairs={{0,1},{1,2},{2,3},{3,0},{4,5},{5,6},{6,7},{7,4},{8,9},{9,10},{10,1... | collective-permute-start | bytes 1966088 | tf_op jit(solution)/shard_map/mixture1/ppermute | solution.py:33
  648.3 53.0 %collective-permute-start.53 = (bf16[640,512]{1,0:T(8,128)(2,1)}, bf16[640,512]{1,0:T(8,128)(2,1)S(1)}, u32[]{:S(2)}, u32[]{:S(2)}) collective-permute-start(bf16[640,512]{1,0:T(8,128)(2,1)} %get-tuple-element.254), channel_id=1, source_target_pairs={{0,2},{1,3},{2,0},{3,1},{4,6},{5,7},{6,4},{7,5},{8,10},{9,11},{10,... | collective-permute-start | bytes 1966088 | tf_op jit(solution)/shard_map/mixture1/ppermute | solution.py:33
  651.4 49.9 %collective-permute-start.54 = (bf16[640,512]{1,0:T(8,128)(2,1)}, bf16[640,512]{1,0:T(8,128)(2,1)S(1)}, u32[]{:S(2)}, u32[]{:S(2)}) collective-permute-start(bf16[640,512]{1,0:T(8,128)(2,1)} %get-tuple-element.255), channel_id=1, source_target_pairs={{0,3},{1,0},{2,1},{3,2},{4,7},{5,4},{6,5},{7,6},{8,11},{9,8},{10,9... | collective-permute-start | bytes 1966088 | tf_op jit(solution)/shard_map/mixture1/ppermute | solution.py:33
  661.4 36.2 %collective-permute-start.56 = (bf16[2,256,512]{2,1,0:T(8,128)(2,1)S(1)}, bf16[2,256,512]{2,1,0:T(8,128)(2,1)S(1)}, u32[]{:S(2)}, u32[]{:S(2)}) collective-permute-start(bf16[2,256,512]{2,1,0:T(8,128)(2,1)S(1)} %get-tuple-element.331), channel_id=1, source_target_pairs={{0,16},{4,20},{8,24},{12,28},{16,0},{20,4},{24,8},{28,12},{1,17},{... | collective-permute-start | bytes 1572872 | tf_op jit(solution)/shard_map/pair_diagonal0/ppermute | solution.py:37
  717.2 56.5 %collective-permute-start.61 = (bf16[128,2048]{1,0:T(8,128)(2,1)}, bf16[128,2048]{1,0:T(8,128)(2,1)S(1)}, u32[]{:S(2)}, u32[]{:S(2)}) collective-permute-start(bf16[128,2048]{1,0:T(8,128)(2,1)} %get-tuple-element.264.refs_0_), channel_id=1, source_target_pairs={{0,3},{1,0},{2,1},{3,2},{4,7},{5,4},{6,5},{7,6},{8,11},{9,8},{10,9... | collective-permute-start | bytes 1572872 | tf_op jit(solution)/shard_map/low_rows0/ppermute | solution.py:33
  731.0 43.0 %collective-permute-start.73 = (bf16[2,256,512]{2,1,0:T(8,128)(2,1)S(1)}, bf16[2,256,512]{2,1,0:T(8,128)(2,1)S(1)}, u32[]{:S(2)}, u32[]{:S(2)}) collective-permute-start(bf16[2,256,512]{2,1,0:T(8,128)(2,1)S(1)} %get-tuple-element.329), channel_id=1, source_target_pairs={{0,16},{4,20},{8,24},{12,28},{16,0},{20,4},{24,8},{28,12},{1,17},{... | collective-permute-start | bytes 1572872 | tf_op jit(solution)/shard_map/pair_diagonal1/ppermute | solution.py:37
  766.4 41.9 %collective-permute-start.60 = (bf16[128,2048]{1,0:T(8,128)(2,1)}, bf16[128,2048]{1,0:T(8,128)(2,1)S(1)}, u32[]{:S(2)}, u32[]{:S(2)}) collective-permute-start(bf16[128,2048]{1,0:T(8,128)(2,1)} %get-tuple-element.264.refs_0_), channel_id=1, source_target_pairs={{0,2},{1,3},{2,0},{3,1},{4,6},{5,7},{6,4},{7,5},{8,10},{9,11},{10,... | collective-permute-start | bytes 1572872 | tf_op jit(solution)/shard_map/low_rows0/ppermute | solution.py:33
  773.7 36.9 %collective-permute-start.62 = (bf16[2,2,256,512]{3,2,1,0:T(8,128)(2,1)}, bf16[2,2,256,512]{3,2,1,0:T(8,128)(2,1)S(1)}, u32[]{:S(2)}, u32[]{:S(2)}) collective-permute-start(bf16[2,2,256,512]{3,2,1,0:T(8,128)(2,1)} %add_blocks.9), channel_id=1, source_target_pairs={{0,8},{4,12},{8,0},{12,4},{16,24},{20,28},{24,16},{28,20},{1,9},{5... | collective-permute-start | bytes 3145736 | tf_op jit(solution)/shard_map/pair_sides0/ppermute | solution.py:37
  773.8 36.9 %collective-permute-start.63 = (bf16[2,2,256,512]{3,2,1,0:T(8,128)(2,1)S(1)}, bf16[2,2,256,512]{3,2,1,0:T(8,128)(2,1)S(1)}, u32[]{:S(2)}, u32[]{:S(2)}) collective-permute-start(bf16[2,2,256,512]{3,2,1,0:T(8,128)(2,1)S(1)} %copy-done.41), channel_id=1, source_target_pairs={{0,16},{4,20},{8,24},{12,28},{16,0},{20,4},{24,8},{28,12},{1,17},{... | collective-permute-start | bytes 3145736 | tf_op jit(solution)/shard_map/pair_sides0/ppermute | solution.py:37
  774.0 34.7 %collective-permute-start.59 = (bf16[128,2048]{1,0:T(8,128)(2,1)}, bf16[128,2048]{1,0:T(8,128)(2,1)S(1)}, u32[]{:S(2)}, u32[]{:S(2)}) collective-permute-start(bf16[128,2048]{1,0:T(8,128)(2,1)} %get-tuple-element.264.refs_0_), channel_id=1, source_target_pairs={{0,1},{1,2},{2,3},{3,0},{4,5},{5,6},{6,7},{7,4},{8,9},{9,10},{10,1... | collective-permute-start | bytes 1572872 | tf_op jit(solution)/shard_map/low_rows0/ppermute | solution.py:33
  779.2 79.8 %collective-permute-start.74 = (bf16[2,2,256,512]{3,2,1,0:T(8,128)(2,1)}, bf16[2,2,256,512]{3,2,1,0:T(8,128)(2,1)S(1)}, u32[]{:S(2)}, u32[]{:S(2)}) collective-permute-start(bf16[2,2,256,512]{3,2,1,0:T(8,128)(2,1)} %add_blocks.13), channel_id=1, source_target_pairs={{0,8},{4,12},{8,0},{12,4},{16,24},{20,28},{24,16},{28,20},{1,9},{5... | collective-permute-start | bytes 3145736 | tf_op jit(solution)/shard_map/pair_sides1/ppermute | solution.py:37
  808.3 58.3 %collective-permute-start.76 = (bf16[2,2,256,512]{3,2,1,0:T(8,128)(2,1)}, bf16[2,2,256,512]{3,2,1,0:T(8,128)(2,1)S(1)}, u32[]{:S(2)}, u32[]{:S(2)}) collective-permute-start(bf16[2,2,256,512]{3,2,1,0:T(8,128)(2,1)} %add_blocks.14), channel_id=1, source_target_pairs={{0,16},{4,20},{8,24},{12,28},{16,0},{20,4},{24,8},{28,12},{1,17},{... | collective-permute-start | bytes 3145736 | tf_op jit(solution)/shard_map/pair_sides1/ppermute | solution.py:37
  808.6 46.6 %collective-permute-start.69 = (bf16[128,2048]{1,0:T(8,128)(2,1)S(1)}, bf16[128,2048]{1,0:T(8,128)(2,1)S(1)}, u32[]{:S(2)}, u32[]{:S(2)}) collective-permute-start(bf16[128,2048]{1,0:T(8,128)(2,1)S(1)} %copy-done.54), channel_id=1, source_target_pairs={{0,3},{1,0},{2,1},{3,2},{4,7},{5,4},{6,5},{7,6},{8,11},{9,8},{10,9... | collective-permute-start | bytes 1572872 | tf_op jit(solution)/shard_map/low_rows1/ppermute | solution.py:33
  855.0 79.3 %collective-permute-start.70 = (bf16[528,512]{1,0:T(8,128)(2,1)}, bf16[528,512]{1,0:T(8,128)(2,1)S(1)}, u32[]{:S(2)}, u32[]{:S(2)}) collective-permute-start(bf16[528,512]{1,0:T(8,128)(2,1)} %get-tuple-element.273), channel_id=1, source_target_pairs={{0,1},{1,2},{2,3},{3,0},{4,5},{5,6},{6,7},{7,4},{8,9},{9,10},{10,1... | collective-permute-start | bytes 1622024 | tf_op jit(solution)/shard_map/first0/ppermute | solution.py:33
  855.1 86.1 %collective-permute-start.71 = (bf16[528,512]{1,0:T(8,128)(2,1)}, bf16[528,512]{1,0:T(8,128)(2,1)S(1)}, u32[]{:S(2)}, u32[]{:S(2)}) collective-permute-start(bf16[528,512]{1,0:T(8,128)(2,1)} %get-tuple-element.274), channel_id=1, source_target_pairs={{0,2},{1,3},{2,0},{3,1},{4,6},{5,7},{6,4},{7,5},{8,10},{9,11},{10,... | collective-permute-start | bytes 1622024 | tf_op jit(solution)/shard_map/first0/ppermute | solution.py:33
  855.2 86.0 %collective-permute-start.72 = (bf16[528,512]{1,0:T(8,128)(2,1)}, bf16[528,512]{1,0:T(8,128)(2,1)S(1)}, u32[]{:S(2)}, u32[]{:S(2)}) collective-permute-start(bf16[528,512]{1,0:T(8,128)(2,1)} %get-tuple-element.275), channel_id=1, source_target_pairs={{0,3},{1,0},{2,1},{3,2},{4,7},{5,4},{6,5},{7,6},{8,11},{9,8},{10,9... | collective-permute-start | bytes 1622024 | tf_op jit(solution)/shard_map/first0/ppermute | solution.py:33
  858.9 75.3 %collective-permute-start.68 = (bf16[128,2048]{1,0:T(8,128)(2,1)S(1)}, bf16[128,2048]{1,0:T(8,128)(2,1)S(1)}, u32[]{:S(2)}, u32[]{:S(2)}) collective-permute-start(bf16[128,2048]{1,0:T(8,128)(2,1)S(1)} %copy-done.54), channel_id=1, source_target_pairs={{0,2},{1,3},{2,0},{3,1},{4,6},{5,7},{6,4},{7,5},{8,10},{9,11},{10,... | collective-permute-start | bytes 1572872 | tf_op jit(solution)/shard_map/low_rows1/ppermute | solution.py:33
  866.6 67.7 %collective-permute-start.67 = (bf16[128,2048]{1,0:T(8,128)(2,1)S(1)}, bf16[128,2048]{1,0:T(8,128)(2,1)S(1)}, u32[]{:S(2)}, u32[]{:S(2)}) collective-permute-start(bf16[128,2048]{1,0:T(8,128)(2,1)S(1)} %copy-done.54), channel_id=1, source_target_pairs={{0,1},{1,2},{2,3},{3,0},{4,5},{5,6},{6,7},{7,4},{8,9},{9,10},{10,1... | collective-permute-start | bytes 1572872 | tf_op jit(solution)/shard_map/low_rows1/ppermute | solution.py:33
  965.1 38.5 %collective-permute-start.82 = (bf16[528,512]{1,0:T(8,128)(2,1)S(1)}, bf16[528,512]{1,0:T(8,128)(2,1)S(1)}, u32[]{:S(2)}, u32[]{:S(2)}) collective-permute-start(bf16[528,512]{1,0:T(8,128)(2,1)S(1)} %copy-done.97), channel_id=1, source_target_pairs={{0,2},{1,3},{2,0},{3,1},{4,6},{5,7},{6,4},{7,5},{8,10},{9,11},{10,... | collective-permute-start | bytes 1622024 | tf_op jit(solution)/shard_map/first1/ppermute | solution.py:33
  966.7 36.9 %collective-permute-start.83 = (bf16[528,512]{1,0:T(8,128)(2,1)S(1)}, bf16[528,512]{1,0:T(8,128)(2,1)S(1)}, u32[]{:S(2)}, u32[]{:S(2)}) collective-permute-start(bf16[528,512]{1,0:T(8,128)(2,1)S(1)} %copy-done.96), channel_id=1, source_target_pairs={{0,3},{1,0},{2,1},{3,2},{4,7},{5,4},{6,5},{7,6},{8,11},{9,8},{10,9... | collective-permute-start | bytes 1622024 | tf_op jit(solution)/shard_map/first1/ppermute | solution.py:33
  1024.9 33.9 %collective-permute-start.91 = (bf16[2,256,1024]{1,2,0:T(8,128)(2,1)}, bf16[2,256,1024]{1,2,0:T(8,128)(2,1)}, u32[]{:S(2)}, u32[]{:S(2)}) collective-permute-start(bf16[2,256,1024]{1,2,0:T(8,128)(2,1)} %copy.51), channel_id=1, source_target_pairs={{0,16},{4,20},{8,24},{12,28},{16,0},{20,4},{24,8},{28,12},{1,17},{... | collective-permute-start | bytes 3145736 | tf_op jit(solution)/shard_map/weights/ppermute | solution.py:37
  (147 other events, 2106.7 us)
Sparse Core Ops, SparseCore 0:
  114.4 96.7 all-gather.1
  484.7 117.9 reduce-scatter.7
  606.2 143.8 reduce-scatter.5
  753.5 152.8 reduce-scatter.3

commit v3 on v2

--- a/solution.py
+++ b/solution.py
@@ -158,7 +158,7 @@
 
 def reduce_chips(own):
     half = own.shape[2] // 2
-    results = []
+    results, came = [], []
     for part in range(2):
         blocks = own[:, :, part * half : (part + 1) * half]
         steps = [1 << b for b in range(own.shape[0].bit_length() - 1)]
@@ -169,13 +169,15 @@
             give = sorted(m for m in kept if m & step)
             keep = sorted(m for m in kept if not m & step)
             got = swap(jnp.stack([kept[m] for m in give]), "sq", 2 * step)
+            if number == 0:
+                came.append(got)
             last = number == len(steps) - 1
             kept = {
                 m: (kept[m].astype(F32) + got[i].astype(F32)).astype(F32 if last else BF16)
                 for i, m in enumerate(keep)
             }
         results.append(kept[0])
-    return jnp.concatenate(results, axis=1).astype(F32)
+    return jnp.concatenate(results, axis=1).astype(F32), came
 
 
 COST = 100
@@ -1020,23 +1022,24 @@
 
 
 def mixture_kernel(count, info, hidden_ref, w_ref, *refs):
-    head_refs, out_refs = refs[:count], refs[count:]
-    rows = hidden_ref.shape[0]
+    head_refs, own_refs, out_refs = refs[:count], refs[count : 2 * count], refs[2 * count :]
+    rows, height = hidden_ref.shape[0], own_refs[0].shape[0]
     result = dot(hidden_ref[...], w_ref[...]).astype(BF16)
     for k in range(count):
 
         @pl.when(pl.program_id(0) == k)
         def _(k=k):
             out_refs[k][:rows] = result
-            out_refs[k][rows:] = head_refs[k][...]
-
-
-def mixture(info, hidden, w_down, heads, count):
+            out_refs[k][rows : rows + height] = own_refs[k][...]
+            out_refs[k][rows + height :] = head_refs[k][...]
+
+
+def mixture(info, hidden, w_down, heads, own, count):
     rows, units = hidden.shape
     width = w_down.shape[-1]
     feat = width // count
     height = heads[0].shape[0]
-    piece = pl.BlockSpec((rows + height, feat), lambda k, info: (0, 0))
+    piece = pl.BlockSpec((rows + 2 * height, feat), lambda k, info: (0, 0))
     row = pl.BlockSpec((height, feat), lambda k, info: (0, 0))
     return pl.pallas_call(
         functools.partial(mixture_kernel, count),
@@ -1047,10 +1050,10 @@
                 pl.BlockSpec((rows, units), lambda k, info: (0, 0), pipeline_mode=pl.Buffered(1)),
                 pl.BlockSpec((units, feat), lambda k, info: (0, lax.rem(info[1] + k, count))),
             ]
-            + [row] * count,
+            + [row] * (2 * count),
             out_specs=[piece] * count,
         ),
-        out_shape=[jax.ShapeDtypeStruct((rows + height, feat), BF16)] * count,
+        out_shape=[jax.ShapeDtypeStruct((rows + 2 * height, feat), BF16)] * count,
         compiler_params=params(),
         cost_estimate=cost(
             flops=2 * rows * units * width,
@@ -1058,13 +1061,13 @@
             transcendentals=0,
         ),
         name="mixture",
-    )(info, hidden, w_down.reshape(units, width), *heads)
+    )(info, hidden, w_down.reshape(units, width), *heads, *own)
 
 
 def middle_back_kernel(count, info, *refs):
     piece_refs, refs = refs[:count], refs[count:]
     middle_ref, inv_ref, grad_ref, gain_ref, w_ref = refs[:5]
-    part_ref, low_ref, *out_refs = refs[5:]
+    part_ref, low_ref, out_refs, own_refs = refs[5], refs[6], refs[7 : 7 + count], refs[7 + count :]
     ffn_grad = piece_refs[0][...].astype(F32)
     for k in range(1, count):
         ffn_grad = ffn_grad + piece_refs[k][...].astype(F32)
@@ -1075,9 +1078,10 @@
     mean = jnp.mean(gained * hat, axis=1, keepdims=True)
     low = (grad_ref[...].astype(F32) + inv * (gained - hat * mean)).astype(BF16)
     low_ref[...] = low
-    cols = out_refs[0].shape[1]
+    cols, feat = out_refs[0].shape[1], own_refs[0].shape[1]
     for k in range(count):
         target = lax.rem(info[1] + k, count)
+        own_refs[k][...] = low_ref[:, pl.ds(pl.multiple_of(target * feat, feat), feat)]
         rows = pl.ds(pl.multiple_of(target * cols, cols), cols)
         out_refs[k][...] = dot(low, w_ref[rows, :], NT).astype(BF16)
 
@@ -1098,22 +1102,35 @@
             grid=(1,),
             in_specs=[first(height, width)] * count
             + [own(width), own(1), part, first(1, width), whole(w_out)],
-            out_specs=[first(1, width), first(height, width)] + [first(height, cols)] * count,
+            out_specs=[first(1, width), first(height, width)]
+            + [first(height, cols)] * count
+            + [first(height, width // count)] * count,
         ),
         out_shape=[out(1, width, F32), out(height, width, BF16)]
-        + [out(height, cols, BF16)] * count,
+        + [out(height, cols, BF16)] * count
+        + [out(height, width // count, BF16)] * count,
         compiler_params=params(),
         cost_estimate=cost(
             flops=2 * height * width * width, bytes_accessed=2 * width * width, transcendentals=0
         ),
         name="middle_back",
     )(info, *pieces, middle, inv, grads, gain[None, :], w_out)
-    return part[0], low, rest
+    return part[0], low, rest[:count], rest[count:]
 
 
 def finish_kernel(count, info, *refs):
-    row_ref, first_refs = refs[0], refs[1 : 1 + count]
-    x_ref, inv_ref, gain_ref, out_ref = refs[1 + count :]
+    sent_refs, first_refs = refs[:count], refs[count : 2 * count]
+    x_ref, inv_ref, gain_ref, out_ref = refs[2 * count :]
+    height = sent_refs[0].shape[0]
+    pieces = out_ref.shape[0] // height
+    for i in range(pieces):
+        distance = lax.rem(info[1] - pl.program_id(0) * pieces - i + 2 * count, count)
+        for k in range(count):
+
+            @pl.when(distance == k)
+            def _(i=i, k=k):
+                out_ref[i * height : (i + 1) * height, :] = sent_refs[k][...].astype(F32)
+
     size, width = out_ref.shape[0], count * x_ref.shape[1]
     rows = pl.ds(pl.multiple_of(pl.program_id(0) * size, size), size)
     place = first_refs[0].shape[0] - EXTRA
@@ -1127,10 +1144,10 @@
     inner = as_columns(jnp.sum(own, axis=0, keepdims=True) / width)[:, :1]
     inv = inv_ref[...]
     hat = x_ref[...].astype(F32) * inv
-    out_ref[...] = row_ref[...].astype(F32) + inv * (gain_ref[...] * first - hat * inner)
-
-
-def finish(info, all_rows, first_pieces, x, inv, gain, chunk, seqs):
+    out_ref[...] += inv * (gain_ref[...] * first - hat * inner)
+
+
+def finish(info, sent_pieces, first_pieces, x, inv, gain, seqs):
     count = len(first_pieces)
     rows, feat = x.shape
     size = rows // seqs
@@ -1141,9 +1158,7 @@
         grid_spec=pltpu.PrefetchScalarGridSpec(
             num_scalar_prefetch=1,
             grid=(seqs,),
-            in_specs=[
-                pl.BlockSpec((size, feat), lambda i, info: (chunk * seqs + i, info[1]))
-            ]
+            in_specs=[pl.BlockSpec((rows // count, feat), lambda i, info: (count, 0))] * count
             + [one(a) for a in first_pieces]
             + [own(feat), own(1), pl.BlockSpec((1, feat), lambda i, info: (0, info[1]))],
             out_specs=own(feat),
@@ -1151,38 +1166,27 @@
         out_shape=jax.ShapeDtypeStruct((rows, feat), F32),
         compiler_params=params(),
         name="finish",
-    )(info, all_rows, *first_pieces, x, inv, gain[None, :])
-
-
-def ordered_kernel(count, info, *refs):
-    height = refs[0].shape[0]
-    for z in range(count):
-
-        @pl.when(info[0] == z)
-        def _(z=z):
-            for c in range(len(refs) // count):
-                for f in range(count):
-                    row = (c * count + f) * height
-                    refs[-1][row : row + height, :] = refs[c * count + (z - f) % count][...]
-
-
-def ordered_rows(rank, chunks):
-    pieces = [piece for chunk in chunks for piece in chunk]
-    height, width = pieces[0].shape
-    cols = min(512, width)
-    spec = lambda rows: pl.BlockSpec((rows, cols), lambda i, info: (0, i))
+    )(info, *sent_pieces, *first_pieces, x, inv, gain[None, :])
+
+
+def spread_kernel(turned, in_ref, out_ref):
+    block = in_ref[...].astype(F32)
+    out_ref[0] = block.T if turned else block
+
+
+def spread(rows, experts, turned):
+    height, width = rows.shape
+    units = width // experts
+    shape = (units, height) if turned else (height, units)
     return pl.pallas_call(
-        functools.partial(ordered_kernel, len(chunks[0])),
-        grid_spec=pltpu.PrefetchScalarGridSpec(
-            num_scalar_prefetch=1,
-            grid=(width // cols,),
-            in_specs=[spec(height)] * len(pieces),
-            out_specs=spec(height * len(pieces)),
-        ),
-        out_shape=jax.ShapeDtypeStruct((height * len(pieces), width), BF16),
-        compiler_params=params(),
-        name="ordered_rows",
-    )(rank, *pieces)
+        functools.partial(spread_kernel, turned),
+        grid=(experts,),
+        in_specs=[pl.BlockSpec((height, units), lambda e: (0, e))],
+        out_specs=pl.BlockSpec((1, *shape), lambda e: (e, 0, 0)),
+        out_shape=jax.ShapeDtypeStruct((experts, *shape), F32),
+        compiler_params=params(),
+        name="spread",
+    )(rows)
 
 
 def rotary_tables(positions):
@@ -1341,7 +1345,7 @@
 
     def mixture_of(c, *others):
         pieces = mixture(
-            after(info_c[c], *others), exps[c][0], w_down, backs[c][2], tp_count
+            after(info_c[c], *others), exps[c][0], w_down, backs[c][2], backs[c][3], tp_count
         )
         with jax.named_scope(f"mixture{c}"):
             return exchange(pieces)
@@ -1410,7 +1414,6 @@
         return raw, pieces, part
 
     scatter = lambda g: lax.psum_scatter(g, "sq", scatter_dimension=0, tiled=True)
-    spread = lambda g: g.astype(F32).reshape(block, experts, -1).transpose(1, 0, 2)
 
     backs, dqs = [], []
     mids.append(middle_of(0, attn_c[1][2], *grads_second))
@@ -1427,50 +1430,54 @@
     back1, router1 = back_of(1, sent[0][0])
     sent1 = ffn_exchange(1, back1)
     w_up_part = weight_grad(ffn_list, [exps[0][2], after(exps[1][2], back1[0])])
-    w_gate_part = weight_grad(
-        ffn_list, [exps[0][1], after(exps[1][1], w_up_part, *sent[0][1:])]
-    )
-    backs.append(middle_grad_of(1, sent1, w_gate_part))
+    dqs.append(attention_back(0, w_up_part))
+    backs.append(middle_grad_of(1, sent1, dqs[0][0]))
     sent.append(mixture_of(1, backs[1][1]))
-    dqs.append(attention_back(0, sent[1][0]))
+    w_gate_part = weight_grad(ffn_list, [exps[0][1], after(exps[1][1], sent[1][0])])
     cores0 = cores_of(0)
     summed0, diagonal0 = diagonal_of(0, cores0)
     sums0, sides0 = sides_of(0, cores0, diagonal0)
-    with jax.named_scope("low_rows0"):
-        low0 = exchange([after(backs[0][1], *sent[1][1:])] * tp_count)
-    dqs.append(attention_back(1, *sums0))
+    attn_own = [block_of(m[0], tp_rank, quarter, 0) for m in mids]
+    w_out_part = weight_grad([backs[0][1], after(backs[1][1], w_gate_part)], attn_own)
+    dqs.append(attention_back(1, w_out_part, *diagonal0, *sums0))
     cores1 = cores_of(1)
     operands0, stats0, gain0 = stats_of(0, after(cores0, dqs[1][0]), sides0)
-    with jax.named_scope("low_rows1"):
-        low1 = exchange([after(backs[1][1], *low0[1:])] * tp_count)
-    low_all = ordered_rows(rank, [low0, low1])
-    raw0, first0, part0 = first_of(0, operands0, stats0, cores1, *low0[1:])
-    summed1, diagonal1 = diagonal_of(1, cores1)
+    summed1, diagonal1 = diagonal_of(1, after(cores1, gain0))
+    raw0, first0, part0 = first_of(
+        0, operands0, stats0, *([cores1] if summed1 is None else [summed1])
+    )
     sums1, sides1 = sides_of(1, cores1, diagonal1)
 
     outputs = [output_of(c, sent[c]) for c in range(2)]
     operands1, stats1, gain1 = stats_of(1, cores1, sides1)
-    raw1, first1, part1 = first_of(1, operands1, stats1, low_all, *first0[1:])
+    raw1, first1, part1 = first_of(1, operands1, stats1, *first0[1:])
     w_down_rows = scatter(after(w_down_part, backs[0][1]))
-    w_up_rows = scatter(after(w_up_part, backs[1][1]))
-    w_gate_rows = scatter(after(w_gate_part, backs[1][1]))
-    w_down_grad = w_down_rows.astype(F32).T.reshape(experts, -1, block)
-    w_up_grad, w_gate_grad = spread(w_up_rows), spread(w_gate_rows)
-    heads_own = [attn_c[c][0].reshape(rows_n, head_cols) for c in range(2)]
+    w_up_rows = scatter(after(w_up_part, backs[1][1], w_down_rows))
+    w_out_rows = scatter(after(w_out_part, w_up_rows, raw0))
+    w_gate_rows = scatter(after(w_gate_part, w_out_rows, raw1))
+    w_down_grad = spread(w_down_rows, experts, True)
+    w_up_grad = spread(w_up_rows, experts, False)
+    w_gate_grad = spread(w_gate_rows, experts, False)
     with jax.named_scope("weights"):
-        own = reduce_cores(
-            info_c[0],
-            [
-                ([(i[1], 0) for i in ins], [raw0, raw1]),
-                ([(low_all, 0), (low_all, 1)], heads_own),
-            ],
+        own = reduce_cores(info_c[0], [([(i[1], 0) for i in ins], [raw0, raw1])])
+        qkv_grad, came = reduce_chips(own)
+    with jax.named_scope("out_weight"):
+        out_pieces = exchange(
+            [block_of(w_out_rows, (tp_rank + k) % tp_count, head_cols, 1) for k in range(tp_count)]
         )
-        qkv_grad = reduce_chips(own)
+        w_out_grad = sum(p.astype(F32) for p in out_pieces).T
     finals = [
-        finish(after(info_c[c], own), low_all, pieces, inputs_c[c], ins[c][2], attn_gain, c, per)
+        finish(
+            after(info_c[c], own),
+            sent[c],
+            pieces,
+            inputs_c[c],
+            ins[c][2],
+            attn_gain,
+            per,
+        )
         for c, pieces in enumerate((first0, first1))
     ]
-    w_out_grad = qkv_grad[:, 3 * head_cols :].T
     small = jnp.concatenate(
         [
             router0 + router1,

time: 1130 us -> 1110 us (0.982); the launches traced: 1120 us -> 1090 us
  starting transfers between devices: 248 us -> 167 us
  waiting for transfers between devices: 327 us -> 377 us
  Pallas kernels: 447 us -> 461 us
    ppermute x32, waiting for transfers between devices: 109 us -> 198 us  [swap(): lax.ppermute(block, axis, [(i, i ^ mask) for i in range(lax.axis_size(axi...]
    ppermute x36 -> x33, starting transfers between devices: 97.3 us -> 49.9 us  [shift(): lax.ppermute(block, axis, [(i, (i + distance) % count) for i in range(cou...]
    ppermute x36 -> x33, waiting for transfers between devices: 107 us -> 69.1 us  [shift(): lax.ppermute(block, axis, [(i, (i + distance) % count) for i in range(cou...]
    ppermute x32, starting transfers between devices: 96.7 us -> 62.7 us  [swap(): lax.ppermute(block, axis, [(i, i ^ mask) for i in range(lax.axis_size(axi...]
    pallas_call x3 -> x4, Pallas kernels: 70.2 us -> 77.9 us  [weight_grad(): pl.pallas_call(functools.partial(weight_grad_kernel, len(lefts), parts),...]
    unnamed x202 -> x184, local copies, waits for them, and re-layouts: 27.5 us -> 24.6 us
  transfers between devices with their start and end apart: 97 -> 95, of which waited for: 36 -> 40; matrix products, arithmetic and copies ran while one was open for 5% -> 4% of each run, Pallas kernels for 38% -> 40%
where the time goes in v3:
time: 1110 us; the launch traced here: 1090 us
  Pallas kernels  461 us (42%)
  waiting for transfers between devices  377 us (34%)
  starting transfers between devices  167 us (15%)
  local copies, waits for them, and re-layouts  48 us (4%)
  other arithmetic  19.8 us (2%)
  between operations  15.4 us (1%)
    ppermute x32, waiting for transfers between devices, swap(): lax.ppermute(block, axis, [(i, i ^ mask) for i in range(lax.axis_size(axi...  198 us
    pallas_call x4, Pallas kernels, weight_grad(): pl.pallas_call(functools.partial(weight_grad_kernel, len(lefts), parts),...  77.9 us
    pallas_call x2, Pallas kernels, expert_hidden(): pl.pallas_call(functools.partial(expert_hidden_kernel, tile), grid_spec=p...  73.9 us
    ppermute x33, waiting for transfers between devices, shift(): lax.ppermute(block, axis, [(i, (i + distance) % count) for i in range(cou...  69.1 us
    pallas_call x2, Pallas kernels, expert_back(): pl.pallas_call(functools.partial(expert_back_kernel, count), grid_spec=pl...  63.6 us
    ppermute x32, starting transfers between devices, swap(): lax.ppermute(block, axis, [(i, i ^ mask) for i in range(lax.axis_size(axi...  62.7 us
    ppermute x33, starting transfers between devices, shift(): lax.ppermute(block, axis, [(i, (i + distance) % count) for i in range(cou...  49.9 us
    ppermute x5, waiting for transfers between devices, second_step(): lax.ppermute(after(b1, a1, *others), 'tp', OUTER)  40.7 us
  transfers between devices with their start and end apart: 95, of which 40 were waited for; matrix products, arithmetic and copies ran while one was open for 4% of the time, Pallas kernels for 40%

profile of v3, /device:TPU:0, one launch (start us, length us, event | category | flops | bytes accessed | tf_op | source)
XLA Modules:
  0.0 1087.5 jit_solution(4169081494129841210)
XLA Ops:
  16.5 11.6 %collective-permute-done.refs_1_ = bf16[512,512]{1,0:T(8,128)(2,1)S(1)} collective-permute-done((bf16[512,512]{1,0:T(8,128)(2,1)S(1)}, bf16[512,512]{1,0:T(8,128)(2,1)S(1)}, u32[]{:S(2)}, u32[]{:S(2)}) %collective-permute-start) | collective-permute-done | bytes 524320 | tf_op jit(solution)/shard_map/inputs0/ppermute | solution.py:46
  32.3 10.5 collective-permute-done.3.refs_2_
  44.7 9.8 collective-permute-done.4.refs_3_
  59.4 8.5 front.2
  89.1 9.5 collective-permute-done.12.refs_3_
  98.6 8.5 front.3
  117.4 13.7 %collective-permute-done.17.refs_4_.refs_8_ = bf16[2,2,256,512]{3,2,1,0:T(8,128)(2,1)S(1)} collective-permute-done((bf16[2,2,256,512]{3,2,1,0:T(8,128)(2,1)S(1)}, bf16[2,2,256,512]{3,2,1,0:T(8,128)(2,1)S(1)}, u32[]{:S(2)}, u32[]{:S(2)}) %collective-permute-start.17) | collective-permute-done | bytes 1048608 | tf_op jit(solution)/shard_map/pairs0/ppermute | solution.py:37
  140.0 18.0 %collective-permute-done.19.refs_6_.refs_10_ = bf16[1,2,256,512]{3,2,1,0:T(8,128)(2,1)S(1)} collective-permute-done((bf16[1,2,256,512]{3,2,1,0:T(8,128)(2,1)S(1)}, bf16[1,2,256,512]{3,2,1,0:T(8,128)(2,1)S(1)}, u32[]{:S(2)}, u32[]{:S(2)}) %collective-permute-start.19) | collective-permute-done | bytes 524320 | tf_op jit(solution)/shard_map/pairs0/ppermute | solution.py:37
  159.0 12.4 %collective-permute-done.21.refs_1_ = bf16[1024,512]{1,0:T(8,128)(2,1)S(1)} collective-permute-done((bf16[1024,512]{1,0:T(8,128)(2,1)S(1)}, bf16[1024,512]{1,0:T(8,128)(2,1)S(1)}, u32[]{:S(2)}, u32[]{:S(2)}) %collective-permute-start.21) | collective-permute-done | bytes 1048608 | tf_op jit(solution)/shard_map/cotangent/ppermute | solution.py:46
  183.7 10.3 attn_forward.2
  194.0 16.7 %collective-permute-done.29.refs_4_.refs_8_ = bf16[2,2,256,512]{3,2,1,0:T(8,128)(2,1)S(1)} collective-permute-done((bf16[2,2,256,512]{3,2,1,0:T(8,128)(2,1)}, bf16[2,2,256,512]{3,2,1,0:T(8,128)(2,1)S(1)}, u32[]{:S(2)}, u32[]{:S(2)}) %collective-permute-start.29) | collective-permute-done | bytes 1048608 | tf_op jit(solution)/shard_map/pairs1/ppermute | solution.py:37
  216.5 20.2 %collective-permute-done.24.refs_2_ = bf16[1024,512]{1,0:T(8,128)(2,1)S(1)} collective-permute-done((bf16[1024,512]{1,0:T(8,128)(2,1)S(1)}, bf16[1024,512]{1,0:T(8,128)(2,1)S(1)}, u32[]{:S(2)}, u32[]{:S(2)}) %collective-permute-start.24) | collective-permute-done | bytes 1048608 | tf_op jit(solution)/shard_map/cotangent/ppermute | solution.py:55
  245.1 10.9 %collective-permute-done.26.refs_1_ = bf16[512,512]{1,0:T(8,128)(2,1)S(1)} collective-permute-done((bf16[512,512]{1,0:T(8,128)(2,1)S(1)}, bf16[512,512]{1,0:T(8,128)(2,1)S(1)}, u32[]{:S(2)}, u32[]{:S(2)}) %collective-permute-start.26) | collective-permute-done | bytes 524320 | tf_op jit(solution)/shard_map/heads0/ppermute | solution.py:46
  260.8 10.0 collective-permute-done.34.refs_2_
  275.5 10.3 attn_forward.3
  290.7 14.0 %collective-permute-done.36.refs_3_ = bf16[512,512]{1,0:T(8,128)(2,1)} collective-permute-done((bf16[512,512]{1,0:T(8,128)(2,1)}, bf16[512,512]{1,0:T(8,128)(2,1)}, u32[]{:S(2)}, u32[]{:S(2)}) %collective-permute-start.36) | collective-permute-done | bytes 524320 | tf_op jit(solution)/shard_map/heads0/ppermute | solution.py:65
  304.7 12.2 %middle_rows.2 = (bf16[512,2048]{1,0:T(8,128)(2,1)}, f32[512,2048]{1,0:T(8,128)}, f32[512,1]{1,0:T(8,128)}, bf16[512,2048]{1,0:T(8,128)(2,1)}, f32[512,16]{1,0:T(8,128)}, /*index=5*/f32[512,16]{1,0:T(8,128)}) custom-call(s32[1]{0:T(128)} %bitcast.info, bf16[512,512]{1,0:T(8,128)(2,1)} %bitcast.110, bf16[512,512]{1,0:T(8,128)(2,1)} %copy-done.55, ...), custom_call_target="tpu_custom_call" | custom-call | flops 42949672 | bytes 209715 | tf_op jit(solution)/shard_map/middle_rows/pallas_call | solution.py:624
  326.0 36.9 %expert_hidden.2 = (bf16[512,4096]{1,0:T(8,128)(2,1)}, bf16[512,4096]{1,0:T(8,128)(2,1)}, bf16[512,4096]{1,0:T(8,128)(2,1)}, f32[512,16]{1,0:T(8,128)}) custom-call(s32[4]{0:T(128)} %pad_add_fusion.2.info, bf16[512,2048]{1,0:T(8,128)(2,1)} %get-tuple-element.211.x_ref.refs_0_, bf16[1024,2048]{1,0:T(8,128)(2,1)} %joined_rows.1.g_ref.refs_0_.refs_6_, ...), custom_call_target="tpu_custom_call" | custom-call | flops 257698032 | bytes 629145 | tf_op jit(solution)/shard_map/expert_hidden/pallas_call | solution.py:916
  364.8 31.1 %expert_back.2 = (bf16[128,2048]{1,0:T(8,128)(2,1)}, bf16[128,2048]{1,0:T(8,128)(2,1)}, bf16[128,2048]{1,0:T(8,128)(2,1)}, bf16[128,2048]{1,0:T(8,128)(2,1)}, f32[512,16]{1,0:T(8,128)}, /*index=5*/f32[16,2048]{1,0:T(8,128)}) custom-call(s32[4]{0:T(128)} %pad_add_fusion.2.info, bf16[512,4096]{1,0:T(8,128)(2,1)} %get-tuple-element.215.gp_ref.refs_2_, ...), custom_call_target="tpu_custom_call" | custom-call | flops 171798688 | bytes 461373 | tf_op jit(solution)/shard_map/expert_back/pallas_call | solution.py:989
  401.9 12.2 %middle_rows.3 = (bf16[512,2048]{1,0:T(8,128)(2,1)}, f32[512,2048]{1,0:T(8,128)}, f32[512,1]{1,0:T(8,128)}, bf16[512,2048]{1,0:T(8,128)(2,1)}, f32[512,16]{1,0:T(8,128)}, /*index=5*/f32[512,16]{1,0:T(8,128)}) custom-call(s32[1]{0:T(128)} %bitcast.info, bf16[512,512]{1,0:T(8,128)(2,1)} %bitcast.115, bf16[512,512]{1,0:T(8,128)(2,1)} %copy-done.53, ...), custom_call_target="tpu_custom_call" | custom-call | flops 42949672 | bytes 209715 | tf_op jit(solution)/shard_map/middle_rows/pallas_call | solution.py:624
  414.1 37.0 %expert_hidden.3 = (bf16[512,4096]{1,0:T(8,128)(2,1)}, bf16[512,4096]{1,0:T(8,128)(2,1)}, bf16[512,4096]{1,0:T(8,128)(2,1)}, f32[512,16]{1,0:T(8,128)}) custom-call(s32[4]{0:T(128)} %pad_add_fusion.info, bf16[512,2048]{1,0:T(8,128)(2,1)} %get-tuple-element.225.x_ref.refs_1_, bf16[1024,2048]{1,0:T(8,128)(2,1)} %joined_rows.1.g_ref.refs_0_.refs_6_, ...), custom_call_target="tpu_custom_call" | custom-call | flops 257698032 | bytes 629145 | tf_op jit(solution)/shard_map/expert_hidden/pallas_call | solution.py:916
  451.1 23.2 %weight_grad.4 = bf16[2048,4096]{1,0:T(8,128)(2,1)} custom-call(bf16[1024,2048]{1,0:T(8,128)(2,1)} %joined_rows.1.g_ref.refs_0_.refs_6_, bf16[512,4096]{1,0:T(8,128)(2,1)} %get-tuple-element.214.refs_1_.hidden_ref, bf16[512,4096]{1,0:T(8,128)(2,1)} %get-tuple-element.228.refs_2_.hidden_ref), custom_call_target="tpu_custom_call" | custom-call | flops 171798688 | bytes 293601 | tf_op jit(solution)/shard_map/weight_grad/pallas_call | solution.py:674
  475.4 9.4 middle_back.2
  484.9 16.9 %mixture.2 = (bf16[768,512]{1,0:T(8,128)(2,1)}, bf16[768,512]{1,0:T(8,128)(2,1)}, bf16[768,512]{1,0:T(8,128)(2,1)}, bf16[768,512]{1,0:T(8,128)(2,1)}) custom-call(s32[4]{0:T(128)} %pad_add_fusion.2.info, bf16[512,4096]{1,0:T(8,128)(2,1)} %get-tuple-element.214.refs_1_.hidden_ref, bf16[4096,2048]{1,0:T(8,128)(2,1)} %bitcast.77, ...), custom_call_target="tpu_custom_call" | custom-call | flops 85899344 | bytes 230686 | tf_op jit(solution)/shard_map/mixture/pallas_call | solution.py:1044
  506.4 32.5 %expert_back.3 = (bf16[128,2048]{1,0:T(8,128)(2,1)}, bf16[128,2048]{1,0:T(8,128)(2,1)}, bf16[128,2048]{1,0:T(8,128)(2,1)}, bf16[128,2048]{1,0:T(8,128)(2,1)}, f32[512,16]{1,0:T(8,128)}, /*index=5*/f32[16,2048]{1,0:T(8,128)}) custom-call(s32[4]{0:T(128)} %pad_add_fusion.info, bf16[512,4096]{1,0:T(8,128)(2,1)} %get-tuple-element.278.gp_ref.refs_3_, ...), custom_call_target="tpu_custom_call" | custom-call | flops 171798688 | bytes 461373 | tf_op jit(solution)/shard_map/expert_back/pallas_call | solution.py:989
  543.6 23.4 %weight_grad.5 = bf16[2048,4096]{1,0:T(8,128)(2,1)} custom-call(bf16[512,2048]{1,0:T(8,128)(2,1)} %get-tuple-element.211.x_ref.refs_0_, bf16[512,2048]{1,0:T(8,128)(2,1)} %get-tuple-element.225.x_ref.refs_1_, bf16[512,4096]{1,0:T(8,128)(2,1)} %get-tuple-element.216.up_ref.refs_2_, bf16[512,4096]{1,0:T(8,128)(2,1)} %get-tuple-element.254.up_ref.refs_3_), custom_call_target="tpu_custom_call" | custom-call | flops 171798688 | bytes 293601 | tf_op jit(solution)/shard_map/weight_grad/pallas_call | solution.py:674
  568.2 13.6 %attn_backward.2 = (bf16[2,256,512]{2,1,0:T(8,128)(2,1)}, bf16[4,2,2,256,512]{4,3,2,1,0:T(8,128)(2,1)}, bf16[4,2,2,256,512]{4,3,2,1,0:T(8,128)(2,1)}) custom-call(s32[4]{0:T(128)} %pad_add_fusion.2.info, bf16[2,256,512]{2,1,0:T(8,128)(2,1)} %get-tuple-element.192.q_ref, f32[2,256,512]{2,1,0:T(8,128)} %get-tuple-element.256.full_ref, ...), custom_call_target="tpu_custom_call" | custom-call | flops 107374184 | bytes 209715 | tf_op jit(solution)/shard_map/attn_backward/pallas_call | solution.py:839
  581.8 18.7 %collective-permute-done.50.refs_2_ = bf16[128,2048]{1,0:T(8,128)(2,1)S(1)} collective-permute-done((bf16[128,2048]{1,0:T(8,128)(2,1)}, bf16[128,2048]{1,0:T(8,128)(2,1)S(1)}, u32[]{:S(2)}, u32[]{:S(2)}) %collective-permute-start.50) | collective-permute-done | bytes 524320 | tf_op jit(solution)/shard_map/ffn_grad1/ppermute | solution.py:33
  601.3 9.4 middle_back.3
  610.9 15.9 %mixture.3 = (bf16[768,512]{1,0:T(8,128)(2,1)}, bf16[768,512]{1,0:T(8,128)(2,1)}, bf16[768,512]{1,0:T(8,128)(2,1)}, bf16[768,512]{1,0:T(8,128)(2,1)}) custom-call(s32[4]{0:T(128)} %pad_add_fusion.info, bf16[512,4096]{1,0:T(8,128)(2,1)} %get-tuple-element.228.refs_2_.hidden_ref, bf16[4096,2048]{1,0:T(8,128)(2,1)} %bitcast.78, ...), custom_call_target="tpu_custom_call" | custom-call | flops 85899344 | bytes 230686 | tf_op jit(solution)/shard_map/mixture/pallas_call | solution.py:1044
  626.7 10.3 collective-permute-start.52
  653.9 10.7 collective-permute-start.57
  668.4 23.2 %weight_grad.6 = bf16[2048,4096]{1,0:T(8,128)(2,1)} custom-call(bf16[512,2048]{1,0:T(8,128)(2,1)} %get-tuple-element.211.x_ref.refs_0_, bf16[512,2048]{1,0:T(8,128)(2,1)} %get-tuple-element.225.x_ref.refs_1_, bf16[512,4096]{1,0:T(8,128)(2,1)} %get-tuple-element.215.gp_ref.refs_2_, bf16[512,4096]{1,0:T(8,128)(2,1)} %get-tuple-element.278.gp_ref.refs_3_), custom_call_target="tpu_custom_call" | custom-call | flops 171798688 | bytes 293601 | tf_op jit(solution)/shard_map/weight_grad/pallas_call | solution.py:674
  691.6 8.1 weight_grad.7
  708.0 13.3 %attn_backward.3 = (bf16[2,256,512]{2,1,0:T(8,128)(2,1)}, bf16[4,2,2,256,512]{4,3,2,1,0:T(8,128)(2,1)}, bf16[4,2,2,256,512]{4,3,2,1,0:T(8,128)(2,1)}) custom-call(s32[4]{0:T(128)} %pad_add_fusion.info, bf16[2,256,512]{2,1,0:T(8,128)(2,1)} %get-tuple-element.198.q_ref, f32[2,256,512]{2,1,0:T(8,128)} %get-tuple-element.285.full_ref, ...), custom_call_target="tpu_custom_call" | custom-call | flops 107374184 | bytes 209715 | tf_op jit(solution)/shard_map/attn_backward/pallas_call | solution.py:839
  736.5 37.3 %collective-permute-done.59.refs_2_.refs_6_ = bf16[2,2,256,512]{3,2,1,0:T(8,128)(2,1)S(1)} collective-permute-done((bf16[2,2,256,512]{3,2,1,0:T(8,128)(2,1)}, bf16[2,2,256,512]{3,2,1,0:T(8,128)(2,1)S(1)}, u32[]{:S(2)}, u32[]{:S(2)}) %collective-permute-start.59) | collective-permute-done | bytes 1048608 | tf_op jit(solution)/shard_map/pair_sides0/ppermute | solution.py:37
  797.7 11.6 %back_first.2 = (bf16[512,1536]{1,0:T(8,128)(2,1)}, f32[1,2048]{1,0:T(1,128)}, bf16[528,512]{1,0:T(8,128)(2,1)}, bf16[528,512]{1,0:T(8,128)(2,1)}, bf16[528,512]{1,0:T(8,128)(2,1)}, /*index=5*/bf16[528,512]{1,0:T(8,128)(2,1)}) custom-call(s32[4]{0:T(128)} %pad_add_fusion.2.info, bf16[2,256,512]{2,1,0:T(8,128)(2,1)} %get-tuple-element.257.refs_0_, ...), custom_call_target="tpu_custom_call" | custom-call | flops 32212254 | bytes 146800 | tf_op jit(solution)/shard_map/back_first/pallas_call | solution.py:487
  813.8 8.8 collective-permute-done.67.refs_4_
  836.5 30.0 %collective-permute-done.68.refs_2_.refs_6_ = bf16[2,2,256,512]{3,2,1,0:T(8,128)(2,1)S(1)} collective-permute-done((bf16[2,2,256,512]{3,2,1,0:T(8,128)(2,1)}, bf16[2,2,256,512]{3,2,1,0:T(8,128)(2,1)S(1)}, u32[]{:S(2)}, u32[]{:S(2)}) %collective-permute-start.68) | collective-permute-done | bytes 1048608 | tf_op jit(solution)/shard_map/pair_sides1/ppermute | solution.py:37
  866.5 9.1 collective-permute-done.70.refs_3_.refs_7_
  891.1 11.7 %back_first.3 = (bf16[512,1536]{1,0:T(8,128)(2,1)}, f32[1,2048]{1,0:T(1,128)}, bf16[528,512]{1,0:T(8,128)(2,1)}, bf16[528,512]{1,0:T(8,128)(2,1)}, bf16[528,512]{1,0:T(8,128)(2,1)}, /*index=5*/bf16[528,512]{1,0:T(8,128)(2,1)}) custom-call(s32[4]{0:T(128)} %pad_add_fusion.info, bf16[2,256,512]{2,1,0:T(8,128)(2,1)} %get-tuple-element.288.refs_0_, ...), custom_call_target="tpu_custom_call" | custom-call | flops 32212254 | bytes 146800 | tf_op jit(solution)/shard_map/back_first/pallas_call | solution.py:487
  903.0 8.2 relative_grads.2
  918.7 9.3 relative_grads.3
  928.4 22.6 %collective-permute-done.76.refs_6_ = bf16[528,512]{1,0:T(8,128)(2,1)S(1)} collective-permute-done((bf16[528,512]{1,0:T(8,128)(2,1)S(1)}, bf16[528,512]{1,0:T(8,128)(2,1)S(1)}, u32[]{:S(2)}, u32[]{:S(2)}) %collective-permute-start.76) | collective-permute-done | bytes 540704 | tf_op jit(solution)/shard_map/first1/ppermute | solution.py:33
  980.2 25.7 %collective-permute-done.80 = f32[20,2048]{1,0:T(8,128)S(1)} collective-permute-done((f32[20,2048]{1,0:T(8,128)S(1)}, f32[20,2048]{1,0:T(8,128)S(1)}, u32[]{:S(2)}, u32[]{:S(2)}) %collective-permute-start.80) | collective-permute-done | bytes 163872 | tf_op jit(solution)/shard_map/small/ppermute | solution.py:37
  1028.7 10.3 collective-permute-done.86
  1041.4 8.2 collective-permute-done.84
  1064.6 10.6 collective-permute-done.88
  (435 shorter events, 315.5 us)
Async XLA Ops:
  7.2 297.5 %all-gather.2.cloned.1.call-start = ((), (), s32[]{:S(2)}) async-start(), calls=%async_computation.4 | async-start | bytes 8650752 | tf_op jit(solution)/shard_map/all_gather | solution.py:1284
  114.3 496.4 %reduce-scatter.5.cloned.1.call-start = ((), (), s32[]{:S(2)}) async-start(), calls=%async_computation.5 | async-start | bytes 18874368 | tf_op jit(solution)/shard_map/reduce_scatter | solution.py:1416
  132.9 38.5 %collective-permute-start.18 = (bf16[3,2,2,256,512]{4,3,2,1,0:T(8,128)(2,1)S(1)}, bf16[3,2,2,256,512]{4,3,2,1,0:T(8,128)(2,1)}, u32[]{:S(2)}, u32[]{:S(2)}) collective-permute-start(bf16[3,2,2,256,512]{4,3,2,1,0:T(8,128)(2,1)S(1)} %pad_maximum_fusion), channel_id=1, source_target_pairs={{0,4},{4,0},{8,12},{12,8},{16,20},{20,16},{24,28},{28,24},{1,5},{5... | collective-permute-start | bytes 9437192 | tf_op jit(solution)/shard_map/pairs0/ppermute | solution.py:37
  135.4 36.1 %collective-permute-start.21 = (bf16[1024,512]{1,0:T(8,128)(2,1)S(1)}, bf16[1024,512]{1,0:T(8,128)(2,1)S(1)}, u32[]{:S(2)}, u32[]{:S(2)}) collective-permute-start(bf16[1024,512]{1,0:T(8,128)(2,1)S(1)} %bitcast.100), channel_id=1, source_target_pairs={{0,1},{1,0},{2,3},{3,2},{4,5},{5,4},{6,7},{7,6},{8,9},{9,8},{10,11... | collective-permute-start | bytes 3145736 | tf_op jit(solution)/shard_map/cotangent/ppermute | solution.py:46
  175.7 35.0 %collective-permute-start.29 = (bf16[2,2,256,512]{3,2,1,0:T(8,128)(2,1)}, bf16[2,2,256,512]{3,2,1,0:T(8,128)(2,1)S(1)}, u32[]{:S(2)}, u32[]{:S(2)}) collective-permute-start(bf16[2,2,256,512]{3,2,1,0:T(8,128)(2,1)} %get-tuple-element.190.refs_0_.refs_4_), channel_id=1, source_target_pairs={{0,16},{4,20},{8,24},{12,28},{16,0},{20,4},{24,8},{28,12},{1,17},{... | collective-permute-start | bytes 3145736 | tf_op jit(solution)/shard_map/pairs1/ppermute | solution.py:37
  176.8 33.9 %collective-permute-start.28 = (bf16[2,2,256,512]{3,2,1,0:T(8,128)(2,1)}, bf16[2,2,256,512]{3,2,1,0:T(8,128)(2,1)S(1)}, u32[]{:S(2)}, u32[]{:S(2)}) collective-permute-start(bf16[2,2,256,512]{3,2,1,0:T(8,128)(2,1)} %get-tuple-element.190.refs_0_.refs_4_), channel_id=1, source_target_pairs={{0,8},{4,12},{8,0},{12,4},{16,24},{20,28},{24,16},{28,20},{1,9},{5... | collective-permute-start | bytes 3145736 | tf_op jit(solution)/shard_map/pairs1/ppermute | solution.py:37
  211.1 61.6 %collective-permute-start.30 = (bf16[3,2,2,256,512]{4,3,2,1,0:T(8,128)(2,1)S(1)}, bf16[3,2,2,256,512]{4,3,2,1,0:T(8,128)(2,1)S(1)}, u32[]{:S(2)}, u32[]{:S(2)}) collective-permute-start(bf16[3,2,2,256,512]{4,3,2,1,0:T(8,128)(2,1)S(1)} %pad_maximum_fusion.1), channel_id=1, source_target_pairs={{0,4},{4,0},{8,12},{12,8},{16,20},{20,16},{24,28},{28,24},{1,5},{5... | collective-permute-start | bytes 9437192 | tf_op jit(solution)/shard_map/pairs1/ppermute | solution.py:37
  214.4 30.4 %collective-permute-start.31 = (bf16[1,2,256,512]{3,2,1,0:T(8,128)(2,1)S(1)}, bf16[1,2,256,512]{3,2,1,0:T(8,128)(2,1)S(1)}, u32[]{:S(2)}, u32[]{:S(2)}) collective-permute-start(bf16[1,2,256,512]{3,2,1,0:T(8,128)(2,1)S(1)} %slice.170), channel_id=1, source_target_pairs={{0,8},{4,12},{8,0},{12,4},{16,24},{20,28},{24,16},{28,20},{1,9},{5... | collective-permute-start | bytes 1572872 | tf_op jit(solution)/shard_map/pairs1/ppermute | solution.py:37
  216.0 28.9 %collective-permute-start.32 = (bf16[1,2,256,512]{3,2,1,0:T(8,128)(2,1)S(1)}, bf16[1,2,256,512]{3,2,1,0:T(8,128)(2,1)S(1)}, u32[]{:S(2)}, u32[]{:S(2)}) collective-permute-start(bf16[1,2,256,512]{3,2,1,0:T(8,128)(2,1)S(1)} %slice.171), channel_id=1, source_target_pairs={{0,16},{4,20},{8,24},{12,28},{16,0},{20,4},{24,8},{28,12},{1,17},{... | collective-permute-start | bytes 1572872 | tf_op jit(solution)/shard_map/pairs1/ppermute | solution.py:37
  245.0 29.5 %collective-permute-start.33 = (bf16[2,2,256,512]{3,2,1,0:T(8,128)(2,1)S(1)}, bf16[2,2,256,512]{3,2,1,0:T(8,128)(2,1)S(1)}, u32[]{:S(2)}, u32[]{:S(2)}) collective-permute-start(bf16[2,2,256,512]{3,2,1,0:T(8,128)(2,1)S(1)} %pad_maximum_fusion.4), channel_id=1, source_target_pairs={{0,4},{4,0},{8,12},{12,8},{16,20},{20,16},{24,28},{28,24},{1,5},{5... | collective-permute-start | bytes 3145736 | tf_op jit(solution)/shard_map/pairs1/ppermute | solution.py:37
  259.8 60.1 %collective-permute-start.37 = (bf16[1024,512]{1,0:T(8,128)(2,1)}, bf16[1024,512]{1,0:T(8,128)(2,1)S(1)}, u32[]{:S(2)}, u32[]{:S(2)}) collective-permute-start(bf16[1024,512]{1,0:T(8,128)(2,1)} %collective-permute-done.25.refs_5_), channel_id=1, source_target_pairs={{0,1},{1,0},{2,3},{3,2},{4,5},{5,4},{6,7},{7,6},{8,9},{9,8},{10,11... | collective-permute-start | bytes 3145736 | tf_op jit(solution)/shard_map/cotangent/ppermute | solution.py:65
  270.9 33.8 %collective-permute-start.36 = (bf16[512,512]{1,0:T(8,128)(2,1)}, bf16[512,512]{1,0:T(8,128)(2,1)}, u32[]{:S(2)}, u32[]{:S(2)}) collective-permute-start(bf16[512,512]{1,0:T(8,128)(2,1)} %collective-permute-done.35.refs_5_), channel_id=1, source_target_pairs={{0,1},{1,0},{2,3},{3,2},{4,5},{5,4},{6,7},{7,6},{8,9},{9,8},{10,11... | collective-permute-start | bytes 1572872 | tf_op jit(solution)/shard_map/heads0/ppermute | solution.py:65
  285.8 31.1 %collective-permute-start.39 = (bf16[512,512]{1,0:T(8,128)(2,1)}, bf16[512,512]{1,0:T(8,128)(2,1)S(1)}, u32[]{:S(2)}, u32[]{:S(2)}) collective-permute-start(bf16[512,512]{1,0:T(8,128)(2,1)} %bitcast.113), channel_id=1, source_target_pairs={{0,0},{1,2},{2,1},{3,3},{4,4},{5,6},{6,5},{7,7},{8,8},{9,10},{10,9... | collective-permute-start | bytes 1572872 | tf_op jit(solution)/shard_map/heads1/ppermute | solution.py:46
  287.5 29.4 %collective-permute-start.38 = (bf16[512,512]{1,0:T(8,128)(2,1)}, bf16[512,512]{1,0:T(8,128)(2,1)S(1)}, u32[]{:S(2)}, u32[]{:S(2)}) collective-permute-start(bf16[512,512]{1,0:T(8,128)(2,1)} %bitcast.114), channel_id=1, source_target_pairs={{0,1},{1,0},{2,3},{3,2},{4,5},{5,4},{6,7},{7,6},{8,9},{9,8},{10,11... | collective-permute-start | bytes 1572872 | tf_op jit(solution)/shard_map/heads1/ppermute | solution.py:46
  317.0 45.9 %collective-permute-start.40 = (bf16[512,512]{1,0:T(8,128)(2,1)S(1)}, bf16[512,512]{1,0:T(8,128)(2,1)S(1)}, u32[]{:S(2)}, u32[]{:S(2)}) collective-permute-start(bf16[512,512]{1,0:T(8,128)(2,1)S(1)} %collective-permute-done.39.refs_4_), channel_id=1, source_target_pairs={{0,1},{1,0},{2,3},{3,2},{4,5},{5,4},{6,7},{7,6},{8,9},{9,8},{10,11... | collective-permute-start | bytes 1572872 | tf_op jit(solution)/shard_map/heads1/ppermute | solution.py:55
  318.8 44.1 %collective-permute-start.41 = (bf16[512,512]{1,0:T(8,128)(2,1)S(1)}, bf16[512,512]{1,0:T(8,128)(2,1)S(1)}, u32[]{:S(2)}, u32[]{:S(2)}) collective-permute-start(bf16[512,512]{1,0:T(8,128)(2,1)S(1)} %collective-permute-done.38.refs_1_), channel_id=1, source_target_pairs={{0,0},{1,2},{2,1},{3,3},{4,4},{5,6},{6,5},{7,7},{8,8},{9,10},{10,9... | collective-permute-start | bytes 1572872 | tf_op jit(solution)/shard_map/heads1/ppermute | solution.py:56
  362.9 38.2 %collective-permute-start.42 = (bf16[512,512]{1,0:T(8,128)(2,1)S(1)}, bf16[512,512]{1,0:T(8,128)(2,1)S(1)}, u32[]{:S(2)}, u32[]{:S(2)}) collective-permute-start(bf16[512,512]{1,0:T(8,128)(2,1)S(1)} %collective-permute-done.41.refs_5_), channel_id=1, source_target_pairs={{0,1},{1,0},{2,3},{3,2},{4,5},{5,4},{6,7},{7,6},{8,9},{9,8},{10,11... | collective-permute-start | bytes 1572872 | tf_op jit(solution)/shard_map/heads1/ppermute | solution.py:65
  395.9 78.4 %collective-permute-start.43 = (bf16[128,2048]{1,0:T(8,128)(2,1)}, bf16[128,2048]{1,0:T(8,128)(2,1)S(1)}, u32[]{:S(2)}, u32[]{:S(2)}) collective-permute-start(bf16[128,2048]{1,0:T(8,128)(2,1)} %get-tuple-element.230), channel_id=1, source_target_pairs={{0,1},{1,2},{2,3},{3,0},{4,5},{5,6},{6,7},{7,4},{8,9},{9,10},{10,1... | collective-permute-start | bytes 1572872 | tf_op jit(solution)/shard_map/ffn_grad0/ppermute | solution.py:33
  396.2 78.1 %collective-permute-start.44 = (bf16[128,2048]{1,0:T(8,128)(2,1)}, bf16[128,2048]{1,0:T(8,128)(2,1)S(1)}, u32[]{:S(2)}, u32[]{:S(2)}) collective-permute-start(bf16[128,2048]{1,0:T(8,128)(2,1)} %get-tuple-element.231), channel_id=1, source_target_pairs={{0,2},{1,3},{2,0},{3,1},{4,6},{5,7},{6,4},{7,5},{8,10},{9,11},{10,... | collective-permute-start | bytes 1572872 | tf_op jit(solution)/shard_map/ffn_grad0/ppermute | solution.py:33
  399.2 75.2 %collective-permute-start.45 = (bf16[128,2048]{1,0:T(8,128)(2,1)}, bf16[128,2048]{1,0:T(8,128)(2,1)S(1)}, u32[]{:S(2)}, u32[]{:S(2)}) collective-permute-start(bf16[128,2048]{1,0:T(8,128)(2,1)} %get-tuple-element.232), channel_id=1, source_target_pairs={{0,3},{1,0},{2,1},{3,2},{4,7},{5,4},{6,5},{7,6},{8,11},{9,8},{10,9... | collective-permute-start | bytes 1572872 | tf_op jit(solution)/shard_map/ffn_grad0/ppermute | solution.py:33
  484.9 324.5 %reduce-scatter.7.cloned.1.call-start = ((), (), s32[]{:S(2)}) async-start(), calls=%async_computation.6 | async-start | bytes 18874368 | tf_op jit(solution)/shard_map/reduce_scatter | solution.py:1416
  501.8 39.1 %collective-permute-start.46 = (bf16[768,512]{1,0:T(8,128)(2,1)}, bf16[768,512]{1,0:T(8,128)(2,1)S(1)}, u32[]{:S(2)}, u32[]{:S(2)}) collective-permute-start(bf16[768,512]{1,0:T(8,128)(2,1)} %get-tuple-element.245), channel_id=1, source_target_pairs={{0,1},{1,2},{2,3},{3,0},{4,5},{5,6},{6,7},{7,4},{8,9},{9,10},{10,1... | collective-permute-start | bytes 2359304 | tf_op jit(solution)/shard_map/mixture0/ppermute | solution.py:33
  502.5 64.5 %collective-permute-start.47 = (bf16[768,512]{1,0:T(8,128)(2,1)}, bf16[768,512]{1,0:T(8,128)(2,1)S(1)}, u32[]{:S(2)}, u32[]{:S(2)}) collective-permute-start(bf16[768,512]{1,0:T(8,128)(2,1)} %get-tuple-element.246), channel_id=1, source_target_pairs={{0,2},{1,3},{2,0},{3,1},{4,6},{5,7},{6,4},{7,5},{8,10},{9,11},{10,... | collective-permute-start | bytes 2359304 | tf_op jit(solution)/shard_map/mixture0/ppermute | solution.py:33
  503.2 63.9 %collective-permute-start.48 = (bf16[768,512]{1,0:T(8,128)(2,1)}, bf16[768,512]{1,0:T(8,128)(2,1)S(1)}, u32[]{:S(2)}, u32[]{:S(2)}) collective-permute-start(bf16[768,512]{1,0:T(8,128)(2,1)} %get-tuple-element.247), channel_id=1, source_target_pairs={{0,3},{1,0},{2,1},{3,2},{4,7},{5,4},{6,5},{7,6},{8,11},{9,8},{10,9... | collective-permute-start | bytes 2359304 | tf_op jit(solution)/shard_map/mixture0/ppermute | solution.py:33
  538.9 42.9 %collective-permute-start.49 = (bf16[128,2048]{1,0:T(8,128)(2,1)}, bf16[128,2048]{1,0:T(8,128)(2,1)S(1)}, u32[]{:S(2)}, u32[]{:S(2)}) collective-permute-start(bf16[128,2048]{1,0:T(8,128)(2,1)} %get-tuple-element.259), channel_id=1, source_target_pairs={{0,1},{1,2},{2,3},{3,0},{4,5},{5,6},{6,7},{7,4},{8,9},{9,10},{10,1... | collective-permute-start | bytes 1572872 | tf_op jit(solution)/shard_map/ffn_grad1/ppermute | solution.py:33
  539.5 61.0 %collective-permute-start.50 = (bf16[128,2048]{1,0:T(8,128)(2,1)}, bf16[128,2048]{1,0:T(8,128)(2,1)S(1)}, u32[]{:S(2)}, u32[]{:S(2)}) collective-permute-start(bf16[128,2048]{1,0:T(8,128)(2,1)} %get-tuple-element.260), channel_id=1, source_target_pairs={{0,2},{1,3},{2,0},{3,1},{4,6},{5,7},{6,4},{7,5},{8,10},{9,11},{10,... | collective-permute-start | bytes 1572872 | tf_op jit(solution)/shard_map/ffn_grad1/ppermute | solution.py:33
  541.0 59.6 %collective-permute-start.51 = (bf16[128,2048]{1,0:T(8,128)(2,1)}, bf16[128,2048]{1,0:T(8,128)(2,1)}, u32[]{:S(2)}, u32[]{:S(2)}) collective-permute-start(bf16[128,2048]{1,0:T(8,128)(2,1)} %get-tuple-element.261), channel_id=1, source_target_pairs={{0,3},{1,0},{2,1},{3,2},{4,7},{5,4},{6,5},{7,6},{8,11},{9,8},{10,9... | collective-permute-start | bytes 1572872 | tf_op jit(solution)/shard_map/ffn_grad1/ppermute | solution.py:33
  610.7 292.2 %reduce-scatter.9.cloned.1.call-start = ((), (), s32[]{:S(2)}) async-start(), calls=%async_computation.7 | async-start | bytes 9437184 | tf_op jit(solution)/shard_map/reduce_scatter | solution.py:1416
  610.8 28.9 %collective-permute-start.55 = (bf16[4,2,2,256,512]{4,3,2,1,0:T(8,128)(2,1)}, bf16[4,2,2,256,512]{4,3,2,1,0:T(8,128)(2,1)S(1)}, u32[]{:S(2)}, u32[]{:S(2)}) collective-permute-start(bf16[4,2,2,256,512]{4,3,2,1,0:T(8,128)(2,1)} %get-tuple-element.283), channel_id=1, source_target_pairs={{0,4},{4,0},{8,12},{12,8},{16,20},{20,16},{24,28},{28,24},{1,5},{5... | collective-permute-start | bytes 12582920 | tf_op jit(solution)/shard_map/pair_cores0/ppermute | solution.py:37
  626.7 79.8 %collective-permute-start.52 = (bf16[768,512]{1,0:T(8,128)(2,1)}, bf16[768,512]{1,0:T(8,128)(2,1)S(1)}, u32[]{:S(2)}, u32[]{:S(2)}) collective-permute-start(bf16[768,512]{1,0:T(8,128)(2,1)} %get-tuple-element.274), channel_id=1, source_target_pairs={{0,1},{1,2},{2,3},{3,0},{4,5},{5,6},{6,7},{7,4},{8,9},{9,10},{10,1... | collective-permute-start | bytes 2359304 | tf_op jit(solution)/shard_map/mixture1/ppermute | solution.py:33
  637.1 69.5 %collective-permute-start.53 = (bf16[768,512]{1,0:T(8,128)(2,1)}, bf16[768,512]{1,0:T(8,128)(2,1)S(1)}, u32[]{:S(2)}, u32[]{:S(2)}) collective-permute-start(bf16[768,512]{1,0:T(8,128)(2,1)} %get-tuple-element.275), channel_id=1, source_target_pairs={{0,2},{1,3},{2,0},{3,1},{4,6},{5,7},{6,4},{7,5},{8,10},{9,11},{10,... | collective-permute-start | bytes 2359304 | tf_op jit(solution)/shard_map/mixture1/ppermute | solution.py:33
  639.1 67.5 %collective-permute-start.54 = (bf16[768,512]{1,0:T(8,128)(2,1)}, bf16[768,512]{1,0:T(8,128)(2,1)S(1)}, u32[]{:S(2)}, u32[]{:S(2)}) collective-permute-start(bf16[768,512]{1,0:T(8,128)(2,1)} %get-tuple-element.276), channel_id=1, source_target_pairs={{0,3},{1,0},{2,1},{3,2},{4,7},{5,4},{6,5},{7,6},{8,11},{9,8},{10,9... | collective-permute-start | bytes 2359304 | tf_op jit(solution)/shard_map/mixture1/ppermute | solution.py:33
  646.9 52.8 %collective-permute-start.56 = (bf16[2,256,512]{2,1,0:T(8,128)(2,1)}, bf16[2,256,512]{2,1,0:T(8,128)(2,1)S(1)}, u32[]{:S(2)}, u32[]{:S(2)}) collective-permute-start(bf16[2,256,512]{2,1,0:T(8,128)(2,1)} %get-tuple-element.352), channel_id=1, source_target_pairs={{0,8},{4,12},{8,0},{12,4},{16,24},{20,28},{24,16},{28,20},{1,9},{5... | collective-permute-start | bytes 1572872 | tf_op jit(solution)/shard_map/pair_diagonal0/ppermute | solution.py:37
  653.9 49.3 %collective-permute-start.57 = (bf16[2,256,512]{2,1,0:T(8,128)(2,1)}, bf16[2,256,512]{2,1,0:T(8,128)(2,1)S(1)}, u32[]{:S(2)}, u32[]{:S(2)}) collective-permute-start(bf16[2,256,512]{2,1,0:T(8,128)(2,1)} %get-tuple-element.351), channel_id=1, source_target_pairs={{0,16},{4,20},{8,24},{12,28},{16,0},{20,4},{24,8},{28,12},{1,17},{... | collective-permute-start | bytes 1572872 | tf_op jit(solution)/shard_map/pair_diagonal0/ppermute | solution.py:37
  721.3 72.0 %collective-permute-start.58 = (bf16[4,2,2,256,512]{4,3,2,1,0:T(8,128)(2,1)}, bf16[4,2,2,256,512]{4,3,2,1,0:T(8,128)(2,1)S(1)}, u32[]{:S(2)}, u32[]{:S(2)}) collective-permute-start(bf16[4,2,2,256,512]{4,3,2,1,0:T(8,128)(2,1)} %get-tuple-element.287), channel_id=1, source_target_pairs={{0,4},{4,0},{8,12},{12,8},{16,20},{20,16},{24,28},{28,24},{1,5},{5... | collective-permute-start | bytes 12582920 | tf_op jit(solution)/shard_map/pair_cores1/ppermute | solution.py:37
  723.3 50.4 %collective-permute-start.59 = (bf16[2,2,256,512]{3,2,1,0:T(8,128)(2,1)}, bf16[2,2,256,512]{3,2,1,0:T(8,128)(2,1)S(1)}, u32[]{:S(2)}, u32[]{:S(2)}) collective-permute-start(bf16[2,2,256,512]{3,2,1,0:T(8,128)(2,1)} %add_blocks.9), channel_id=1, source_target_pairs={{0,8},{4,12},{8,0},{12,4},{16,24},{20,28},{24,16},{28,20},{1,9},{5... | collective-permute-start | bytes 3145736 | tf_op jit(solution)/shard_map/pair_sides0/ppermute | solution.py:37
  728.7 45.1 %collective-permute-start.60 = (bf16[2,2,256,512]{3,2,1,0:T(8,128)(2,1)}, bf16[2,2,256,512]{3,2,1,0:T(8,128)(2,1)S(1)}, u32[]{:S(2)}, u32[]{:S(2)}) collective-permute-start(bf16[2,2,256,512]{3,2,1,0:T(8,128)(2,1)} %add_blocks.10), channel_id=1, source_target_pairs={{0,16},{4,20},{8,24},{12,28},{16,0},{20,4},{24,8},{28,12},{1,17},{... | collective-permute-start | bytes 3145736 | tf_op jit(solution)/shard_map/pair_sides0/ppermute | solution.py:37
  809.4 266.9 %reduce-scatter.11.cloned.1.call-start = ((), (), s32[]{:S(2)}) async-start(), calls=%async_computation.8 | async-start | bytes 18874368 | tf_op jit(solution)/shard_map/reduce_scatter | solution.py:1416
  826.2 40.3 %collective-permute-start.68 = (bf16[2,2,256,512]{3,2,1,0:T(8,128)(2,1)}, bf16[2,2,256,512]{3,2,1,0:T(8,128)(2,1)S(1)}, u32[]{:S(2)}, u32[]{:S(2)}) collective-permute-start(bf16[2,2,256,512]{3,2,1,0:T(8,128)(2,1)} %add_blocks.13), channel_id=1, source_target_pairs={{0,8},{4,12},{8,0},{12,4},{16,24},{20,28},{24,16},{28,20},{1,9},{5... | collective-permute-start | bytes 3145736 | tf_op jit(solution)/shard_map/pair_sides1/ppermute | solution.py:37
  830.8 44.7 %collective-permute-start.70 = (bf16[2,2,256,512]{3,2,1,0:T(8,128)(2,1)}, bf16[2,2,256,512]{3,2,1,0:T(8,128)(2,1)S(1)}, u32[]{:S(2)}, u32[]{:S(2)}) collective-permute-start(bf16[2,2,256,512]{3,2,1,0:T(8,128)(2,1)} %add_blocks.14), channel_id=1, source_target_pairs={{0,16},{4,20},{8,24},{12,28},{16,0},{20,4},{24,8},{28,12},{1,17},{... | collective-permute-start | bytes 3145736 | tf_op jit(solution)/shard_map/pair_sides1/ppermute | solution.py:37
  832.6 51.2 %collective-permute-start.64 = (bf16[528,512]{1,0:T(8,128)(2,1)S(1)}, bf16[528,512]{1,0:T(8,128)(2,1)S(1)}, u32[]{:S(2)}, u32[]{:S(2)}) collective-permute-start(bf16[528,512]{1,0:T(8,128)(2,1)S(1)} %copy-done.90), channel_id=1, source_target_pairs={{0,1},{1,2},{2,3},{3,0},{4,5},{5,6},{6,7},{7,4},{8,9},{9,10},{10,1... | collective-permute-start | bytes 1622024 | tf_op jit(solution)/shard_map/first0/ppermute | solution.py:33
  832.6 53.1 %collective-permute-start.65 = (bf16[528,512]{1,0:T(8,128)(2,1)S(1)}, bf16[528,512]{1,0:T(8,128)(2,1)}, u32[]{:S(2)}, u32[]{:S(2)}) collective-permute-start(bf16[528,512]{1,0:T(8,128)(2,1)S(1)} %copy-done.89), channel_id=1, source_target_pairs={{0,2},{1,3},{2,0},{3,1},{4,6},{5,7},{6,4},{7,5},{8,10},{9,11},{10,... | collective-permute-start | bytes 1622024 | tf_op jit(solution)/shard_map/first0/ppermute | solution.py:33
  833.6 52.2 %collective-permute-start.66 = (bf16[528,512]{1,0:T(8,128)(2,1)S(1)}, bf16[528,512]{1,0:T(8,128)(2,1)}, u32[]{:S(2)}, u32[]{:S(2)}) collective-permute-start(bf16[528,512]{1,0:T(8,128)(2,1)S(1)} %copy-done.88), channel_id=1, source_target_pairs={{0,3},{1,0},{2,1},{3,2},{4,7},{5,4},{6,5},{7,6},{8,11},{9,8},{10,9... | collective-permute-start | bytes 1622024 | tf_op jit(solution)/shard_map/first0/ppermute | solution.py:33
  911.8 39.2 %collective-permute-start.76 = (bf16[528,512]{1,0:T(8,128)(2,1)S(1)}, bf16[528,512]{1,0:T(8,128)(2,1)S(1)}, u32[]{:S(2)}, u32[]{:S(2)}) collective-permute-start(bf16[528,512]{1,0:T(8,128)(2,1)S(1)} %copy-done.87), channel_id=1, source_target_pairs={{0,2},{1,3},{2,0},{3,1},{4,6},{5,7},{6,4},{7,5},{8,10},{9,11},{10,... | collective-permute-start | bytes 1622024 | tf_op jit(solution)/shard_map/first1/ppermute | solution.py:33
  913.9 37.2 %collective-permute-start.77 = (bf16[528,512]{1,0:T(8,128)(2,1)S(1)}, bf16[528,512]{1,0:T(8,128)(2,1)S(1)}, u32[]{:S(2)}, u32[]{:S(2)}) collective-permute-start(bf16[528,512]{1,0:T(8,128)(2,1)S(1)} %copy-done.86), channel_id=1, source_target_pairs={{0,3},{1,0},{2,1},{3,2},{4,7},{5,4},{6,5},{7,6},{8,11},{9,8},{10,9... | collective-permute-start | bytes 1622024 | tf_op jit(solution)/shard_map/first1/ppermute | solution.py:33
  960.3 58.7 %collective-permute-start.85 = (bf16[2,256,768]{2,1,0:T(8,128)(2,1)}, bf16[2,256,768]{2,1,0:T(8,128)(2,1)S(1)}, u32[]{:S(2)}, u32[]{:S(2)}) collective-permute-start(bf16[2,256,768]{2,1,0:T(8,128)(2,1)} %stack.42), channel_id=1, source_target_pairs={{0,16},{4,20},{8,24},{12,28},{16,0},{20,4},{24,8},{28,12},{1,17},{... | collective-permute-start | bytes 2359304 | tf_op jit(solution)/shard_map/weights/ppermute | solution.py:37
  973.6 32.3 %collective-permute-start.80 = (f32[20,2048]{1,0:T(8,128)S(1)}, f32[20,2048]{1,0:T(8,128)S(1)}, u32[]{:S(2)}, u32[]{:S(2)}) collective-permute-start(f32[20,2048]{1,0:T(8,128)S(1)} %add.213), channel_id=1, source_target_pairs={{0,16},{4,20},{8,24},{12,28},{16,0},{20,4},{24,8},{28,12},{1,17},{... | collective-permute-start | bytes 491528 | tf_op jit(solution)/shard_map/small/ppermute | solution.py:37
  975.1 53.5 %collective-permute-start.83 = (bf16[2,256,768]{2,1,0:T(8,128)(2,1)}, bf16[2,256,768]{2,1,0:T(8,128)(2,1)}, u32[]{:S(2)}, u32[]{:S(2)}) collective-permute-start(bf16[2,256,768]{2,1,0:T(8,128)(2,1)} %pad_maximum_fusion.6), channel_id=1, source_target_pairs={{0,8},{4,12},{8,0},{12,4},{16,24},{20,28},{24,16},{28,20},{1,9},{5... | collective-permute-start | bytes 2359304 | tf_op jit(solution)/shard_map/weights/ppermute | solution.py:37
  (138 other events, 1808.1 us)
Sparse Core Ops, SparseCore 0:
  114.4 96.4 all-gather.1
  485.0 114.4 reduce-scatter.4
  610.9 163.6 reduce-scatter.6
  809.6 86.7 reduce-scatter.8
  903.1 144.6 reduce-scatter.10

commit v4 on v3

--- a/solution.py
+++ b/solution.py
@@ -1482,7 +1482,7 @@
         [
             router0 + router1,
             (backs[0][0] + backs[1][0])[None, :],
-            (part0 + after(part1, finals[1]))[None, :],
+            (part0 + after(part1, own))[None, :],
             lax.dynamic_update_slice_in_dim(
                 jnp.zeros((2, all_cols), F32), gain0 + gain1, tp_rank * head_cols, 1
             ),

time: 1110 us -> 1080 us (0.973); the launches traced: 1090 us -> 1070 us
  waiting for transfers between devices: 377 us -> 361 us
    unnamed x184 -> x176, local copies, waits for them, and re-layouts: 24.6 us -> 22.9 us
  transfers between devices with their start and end apart: 95 -> 95, of which waited for: 40 -> 40; matrix products, arithmetic and copies ran while one was open for 4% -> 4% of each run, Pallas kernels for 40% -> 41%
where the time goes in v4:
time: 1080 us; the launch traced here: 1070 us
  Pallas kernels  461 us (43%)
  waiting for transfers between devices  361 us (33%)
  starting transfers between devices  166 us (15%)
  local copies, waits for them, and re-layouts  46.1 us (4%)
  other arithmetic  19.9 us (2%)
  between operations  15.5 us (1%)
    ppermute x32, waiting for transfers between devices, swap(): lax.ppermute(block, axis, [(i, i ^ mask) for i in range(lax.axis_size(axi...  192 us
    pallas_call x4, Pallas kernels, weight_grad(): pl.pallas_call(functools.partial(weight_grad_kernel, len(lefts), parts),...  77.9 us
    pallas_call x2, Pallas kernels, expert_hidden(): pl.pallas_call(functools.partial(expert_hidden_kernel, tile), grid_spec=p...  73.9 us
    pallas_call x2, Pallas kernels, expert_back(): pl.pallas_call(functools.partial(expert_back_kernel, count), grid_spec=pl...  63.6 us
    ppermute x32, starting transfers between devices, swap(): lax.ppermute(block, axis, [(i, i ^ mask) for i in range(lax.axis_size(axi...  61.3 us
    ppermute x33, waiting for transfers between devices, shift(): lax.ppermute(block, axis, [(i, (i + distance) % count) for i in range(cou...  59.5 us
    ppermute x33, starting transfers between devices, shift(): lax.ppermute(block, axis, [(i, (i + distance) % count) for i in range(cou...  50.9 us
    ppermute x5, waiting for transfers between devices, second_step(): lax.ppermute(after(b1, a1, *others), 'tp', OUTER)  40.8 us
  transfers between devices with their start and end apart: 95, of which 40 were waited for; matrix products, arithmetic and copies ran while one was open for 4% of the time, Pallas kernels for 41%

profile of v4, /device:TPU:0, one launch (start us, length us, event | category | flops | bytes accessed | tf_op | source)
XLA Modules:
  0.0 1069.1 jit_solution(12707649092764459126)
XLA Ops:
  16.5 11.6 %collective-permute-done.refs_1_ = bf16[512,512]{1,0:T(8,128)(2,1)S(1)} collective-permute-done((bf16[512,512]{1,0:T(8,128)(2,1)S(1)}, bf16[512,512]{1,0:T(8,128)(2,1)S(1)}, u32[]{:S(2)}, u32[]{:S(2)}) %collective-permute-start) | collective-permute-done | bytes 524320 | tf_op jit(solution)/shard_map/inputs0/ppermute | solution.py:46
  32.3 10.5 collective-permute-done.3.refs_2_
  44.7 9.8 collective-permute-done.4.refs_3_
  59.4 8.5 front.2
  89.1 9.5 collective-permute-done.12.refs_3_
  98.6 8.5 front.3
  117.4 13.6 %collective-permute-done.17.refs_4_.refs_8_ = bf16[2,2,256,512]{3,2,1,0:T(8,128)(2,1)S(1)} collective-permute-done((bf16[2,2,256,512]{3,2,1,0:T(8,128)(2,1)S(1)}, bf16[2,2,256,512]{3,2,1,0:T(8,128)(2,1)S(1)}, u32[]{:S(2)}, u32[]{:S(2)}) %collective-permute-start.17) | collective-permute-done | bytes 1048608 | tf_op jit(solution)/shard_map/pairs0/ppermute | solution.py:37
  140.0 18.1 %collective-permute-done.19.refs_6_.refs_10_ = bf16[1,2,256,512]{3,2,1,0:T(8,128)(2,1)S(1)} collective-permute-done((bf16[1,2,256,512]{3,2,1,0:T(8,128)(2,1)S(1)}, bf16[1,2,256,512]{3,2,1,0:T(8,128)(2,1)S(1)}, u32[]{:S(2)}, u32[]{:S(2)}) %collective-permute-start.19) | collective-permute-done | bytes 524320 | tf_op jit(solution)/shard_map/pairs0/ppermute | solution.py:37
  159.0 12.4 %collective-permute-done.21.refs_1_ = bf16[1024,512]{1,0:T(8,128)(2,1)S(1)} collective-permute-done((bf16[1024,512]{1,0:T(8,128)(2,1)S(1)}, bf16[1024,512]{1,0:T(8,128)(2,1)S(1)}, u32[]{:S(2)}, u32[]{:S(2)}) %collective-permute-start.21) | collective-permute-done | bytes 1048608 | tf_op jit(solution)/shard_map/cotangent/ppermute | solution.py:46
  183.1 10.3 attn_forward.2
  193.4 17.3 %collective-permute-done.29.refs_4_.refs_8_ = bf16[2,2,256,512]{3,2,1,0:T(8,128)(2,1)S(1)} collective-permute-done((bf16[2,2,256,512]{3,2,1,0:T(8,128)(2,1)}, bf16[2,2,256,512]{3,2,1,0:T(8,128)(2,1)S(1)}, u32[]{:S(2)}, u32[]{:S(2)}) %collective-permute-start.29) | collective-permute-done | bytes 1048608 | tf_op jit(solution)/shard_map/pairs1/ppermute | solution.py:37
  216.5 20.2 %collective-permute-done.24.refs_2_ = bf16[1024,512]{1,0:T(8,128)(2,1)S(1)} collective-permute-done((bf16[1024,512]{1,0:T(8,128)(2,1)S(1)}, bf16[1024,512]{1,0:T(8,128)(2,1)S(1)}, u32[]{:S(2)}, u32[]{:S(2)}) %collective-permute-start.24) | collective-permute-done | bytes 1048608 | tf_op jit(solution)/shard_map/cotangent/ppermute | solution.py:55
  245.1 10.9 %collective-permute-done.26.refs_1_ = bf16[512,512]{1,0:T(8,128)(2,1)S(1)} collective-permute-done((bf16[512,512]{1,0:T(8,128)(2,1)S(1)}, bf16[512,512]{1,0:T(8,128)(2,1)S(1)}, u32[]{:S(2)}, u32[]{:S(2)}) %collective-permute-start.26) | collective-permute-done | bytes 524320 | tf_op jit(solution)/shard_map/heads0/ppermute | solution.py:46
  260.8 10.0 collective-permute-done.34.refs_2_
  276.2 10.3 attn_forward.3
  290.9 13.7 %collective-permute-done.36.refs_3_ = bf16[512,512]{1,0:T(8,128)(2,1)} collective-permute-done((bf16[512,512]{1,0:T(8,128)(2,1)}, bf16[512,512]{1,0:T(8,128)(2,1)}, u32[]{:S(2)}, u32[]{:S(2)}) %collective-permute-start.36) | collective-permute-done | bytes 524320 | tf_op jit(solution)/shard_map/heads0/ppermute | solution.py:65
  304.7 12.3 %middle_rows.2 = (bf16[512,2048]{1,0:T(8,128)(2,1)}, f32[512,2048]{1,0:T(8,128)}, f32[512,1]{1,0:T(8,128)}, bf16[512,2048]{1,0:T(8,128)(2,1)}, f32[512,16]{1,0:T(8,128)}, /*index=5*/f32[512,16]{1,0:T(8,128)}) custom-call(s32[1]{0:T(128)} %bitcast.info, bf16[512,512]{1,0:T(8,128)(2,1)} %bitcast.110, bf16[512,512]{1,0:T(8,128)(2,1)} %copy-done.53, ...), custom_call_target="tpu_custom_call" | custom-call | flops 42949672 | bytes 209715 | tf_op jit(solution)/shard_map/middle_rows/pallas_call | solution.py:624
  325.0 36.9 %expert_hidden.2 = (bf16[512,4096]{1,0:T(8,128)(2,1)}, bf16[512,4096]{1,0:T(8,128)(2,1)}, bf16[512,4096]{1,0:T(8,128)(2,1)}, f32[512,16]{1,0:T(8,128)}) custom-call(s32[4]{0:T(128)} %pad_add_fusion.2.info, bf16[512,2048]{1,0:T(8,128)(2,1)} %get-tuple-element.211.x_ref.refs_0_, bf16[1024,2048]{1,0:T(8,128)(2,1)} %joined_rows.1.g_ref.refs_0_.refs_6_, ...), custom_call_target="tpu_custom_call" | custom-call | flops 257698032 | bytes 629145 | tf_op jit(solution)/shard_map/expert_hidden/pallas_call | solution.py:916
  363.8 31.1 %expert_back.2 = (bf16[128,2048]{1,0:T(8,128)(2,1)}, bf16[128,2048]{1,0:T(8,128)(2,1)}, bf16[128,2048]{1,0:T(8,128)(2,1)}, bf16[128,2048]{1,0:T(8,128)(2,1)}, f32[512,16]{1,0:T(8,128)}, /*index=5*/f32[16,2048]{1,0:T(8,128)}) custom-call(s32[4]{0:T(128)} %pad_add_fusion.2.info, bf16[512,4096]{1,0:T(8,128)(2,1)} %get-tuple-element.215.gp_ref.refs_2_, ...), custom_call_target="tpu_custom_call" | custom-call | flops 171798688 | bytes 461373 | tf_op jit(solution)/shard_map/expert_back/pallas_call | solution.py:989
  400.9 12.2 %middle_rows.3 = (bf16[512,2048]{1,0:T(8,128)(2,1)}, f32[512,2048]{1,0:T(8,128)}, f32[512,1]{1,0:T(8,128)}, bf16[512,2048]{1,0:T(8,128)(2,1)}, f32[512,16]{1,0:T(8,128)}, /*index=5*/f32[512,16]{1,0:T(8,128)}) custom-call(s32[1]{0:T(128)} %bitcast.info, bf16[512,512]{1,0:T(8,128)(2,1)} %bitcast.115, bf16[512,512]{1,0:T(8,128)(2,1)} %copy-done.51, ...), custom_call_target="tpu_custom_call" | custom-call | flops 42949672 | bytes 209715 | tf_op jit(solution)/shard_map/middle_rows/pallas_call | solution.py:624
  413.1 37.0 %expert_hidden.3 = (bf16[512,4096]{1,0:T(8,128)(2,1)}, bf16[512,4096]{1,0:T(8,128)(2,1)}, bf16[512,4096]{1,0:T(8,128)(2,1)}, f32[512,16]{1,0:T(8,128)}) custom-call(s32[4]{0:T(128)} %pad_add_fusion.info, bf16[512,2048]{1,0:T(8,128)(2,1)} %get-tuple-element.225.x_ref.refs_1_, bf16[1024,2048]{1,0:T(8,128)(2,1)} %joined_rows.1.g_ref.refs_0_.refs_6_, ...), custom_call_target="tpu_custom_call" | custom-call | flops 257698032 | bytes 629145 | tf_op jit(solution)/shard_map/expert_hidden/pallas_call | solution.py:916
  450.2 23.2 %weight_grad.4 = bf16[2048,4096]{1,0:T(8,128)(2,1)} custom-call(bf16[1024,2048]{1,0:T(8,128)(2,1)} %joined_rows.1.g_ref.refs_0_.refs_6_, bf16[512,4096]{1,0:T(8,128)(2,1)} %get-tuple-element.214.refs_1_.hidden_ref, bf16[512,4096]{1,0:T(8,128)(2,1)} %get-tuple-element.228.refs_2_.hidden_ref), custom_call_target="tpu_custom_call" | custom-call | flops 171798688 | bytes 293601 | tf_op jit(solution)/shard_map/weight_grad/pallas_call | solution.py:674
  474.5 9.4 middle_back.2
  484.0 16.9 %mixture.2 = (bf16[768,512]{1,0:T(8,128)(2,1)}, bf16[768,512]{1,0:T(8,128)(2,1)}, bf16[768,512]{1,0:T(8,128)(2,1)}, bf16[768,512]{1,0:T(8,128)(2,1)}) custom-call(s32[4]{0:T(128)} %pad_add_fusion.2.info, bf16[512,4096]{1,0:T(8,128)(2,1)} %get-tuple-element.214.refs_1_.hidden_ref, bf16[4096,2048]{1,0:T(8,128)(2,1)} %bitcast.77, ...), custom_call_target="tpu_custom_call" | custom-call | flops 85899344 | bytes 230686 | tf_op jit(solution)/shard_map/mixture/pallas_call | solution.py:1044
  505.5 32.5 %expert_back.3 = (bf16[128,2048]{1,0:T(8,128)(2,1)}, bf16[128,2048]{1,0:T(8,128)(2,1)}, bf16[128,2048]{1,0:T(8,128)(2,1)}, bf16[128,2048]{1,0:T(8,128)(2,1)}, f32[512,16]{1,0:T(8,128)}, /*index=5*/f32[16,2048]{1,0:T(8,128)}) custom-call(s32[4]{0:T(128)} %pad_add_fusion.info, bf16[512,4096]{1,0:T(8,128)(2,1)} %get-tuple-element.278.gp_ref.refs_3_, ...), custom_call_target="tpu_custom_call" | custom-call | flops 171798688 | bytes 461373 | tf_op jit(solution)/shard_map/expert_back/pallas_call | solution.py:989
  542.6 23.4 %weight_grad.5 = bf16[2048,4096]{1,0:T(8,128)(2,1)} custom-call(bf16[512,2048]{1,0:T(8,128)(2,1)} %get-tuple-element.211.x_ref.refs_0_, bf16[512,2048]{1,0:T(8,128)(2,1)} %get-tuple-element.225.x_ref.refs_1_, bf16[512,4096]{1,0:T(8,128)(2,1)} %get-tuple-element.216.up_ref.refs_2_, bf16[512,4096]{1,0:T(8,128)(2,1)} %get-tuple-element.254.up_ref.refs_3_), custom_call_target="tpu_custom_call" | custom-call | flops 171798688 | bytes 293601 | tf_op jit(solution)/shard_map/weight_grad/pallas_call | solution.py:674
  567.2 13.6 %attn_backward.2 = (bf16[2,256,512]{2,1,0:T(8,128)(2,1)}, bf16[4,2,2,256,512]{4,3,2,1,0:T(8,128)(2,1)}, bf16[4,2,2,256,512]{4,3,2,1,0:T(8,128)(2,1)}) custom-call(s32[4]{0:T(128)} %pad_add_fusion.2.info, bf16[2,256,512]{2,1,0:T(8,128)(2,1)} %get-tuple-element.192.q_ref, f32[2,256,512]{2,1,0:T(8,128)} %get-tuple-element.256.full_ref, ...), custom_call_target="tpu_custom_call" | custom-call | flops 107374184 | bytes 209715 | tf_op jit(solution)/shard_map/attn_backward/pallas_call | solution.py:839
  580.9 18.7 %collective-permute-done.50.refs_2_ = bf16[128,2048]{1,0:T(8,128)(2,1)S(1)} collective-permute-done((bf16[128,2048]{1,0:T(8,128)(2,1)}, bf16[128,2048]{1,0:T(8,128)(2,1)S(1)}, u32[]{:S(2)}, u32[]{:S(2)}) %collective-permute-start.50) | collective-permute-done | bytes 524320 | tf_op jit(solution)/shard_map/ffn_grad1/ppermute | solution.py:33
  600.4 9.4 middle_back.3
  610.0 15.9 %mixture.3 = (bf16[768,512]{1,0:T(8,128)(2,1)}, bf16[768,512]{1,0:T(8,128)(2,1)}, bf16[768,512]{1,0:T(8,128)(2,1)}, bf16[768,512]{1,0:T(8,128)(2,1)}) custom-call(s32[4]{0:T(128)} %pad_add_fusion.info, bf16[512,4096]{1,0:T(8,128)(2,1)} %get-tuple-element.228.refs_2_.hidden_ref, bf16[4096,2048]{1,0:T(8,128)(2,1)} %bitcast.78, ...), custom_call_target="tpu_custom_call" | custom-call | flops 85899344 | bytes 230686 | tf_op jit(solution)/shard_map/mixture/pallas_call | solution.py:1044
  625.8 10.3 collective-permute-start.52
  652.8 14.9 %collective-permute-start.57 = (bf16[2,256,512]{2,1,0:T(8,128)(2,1)}, bf16[2,256,512]{2,1,0:T(8,128)(2,1)S(1)}, u32[]{:S(2)}, u32[]{:S(2)}) collective-permute-start(bf16[2,256,512]{2,1,0:T(8,128)(2,1)} %get-tuple-element.351), channel_id=1, source_target_pairs={{0,16},{4,20},{8,24},{12,28},{16,0},{20,4},{24,8},{28,12},{1,17},{... | collective-permute-start | bytes 1572872 | tf_op jit(solution)/shard_map/pair_diagonal0/ppermute | solution.py:37
  671.4 23.2 %weight_grad.6 = bf16[2048,4096]{1,0:T(8,128)(2,1)} custom-call(bf16[512,2048]{1,0:T(8,128)(2,1)} %get-tuple-element.211.x_ref.refs_0_, bf16[512,2048]{1,0:T(8,128)(2,1)} %get-tuple-element.225.x_ref.refs_1_, bf16[512,4096]{1,0:T(8,128)(2,1)} %get-tuple-element.215.gp_ref.refs_2_, bf16[512,4096]{1,0:T(8,128)(2,1)} %get-tuple-element.278.gp_ref.refs_3_), custom_call_target="tpu_custom_call" | custom-call | flops 171798688 | bytes 293601 | tf_op jit(solution)/shard_map/weight_grad/pallas_call | solution.py:674
  694.7 8.1 weight_grad.7
  711.0 13.3 %attn_backward.3 = (bf16[2,256,512]{2,1,0:T(8,128)(2,1)}, bf16[4,2,2,256,512]{4,3,2,1,0:T(8,128)(2,1)}, bf16[4,2,2,256,512]{4,3,2,1,0:T(8,128)(2,1)}) custom-call(s32[4]{0:T(128)} %pad_add_fusion.info, bf16[2,256,512]{2,1,0:T(8,128)(2,1)} %get-tuple-element.198.q_ref, f32[2,256,512]{2,1,0:T(8,128)} %get-tuple-element.285.full_ref, ...), custom_call_target="tpu_custom_call" | custom-call | flops 107374184 | bytes 209715 | tf_op jit(solution)/shard_map/attn_backward/pallas_call | solution.py:839
  732.3 44.1 %collective-permute-done.59.refs_2_.refs_6_ = bf16[2,2,256,512]{3,2,1,0:T(8,128)(2,1)S(1)} collective-permute-done((bf16[2,2,256,512]{3,2,1,0:T(8,128)(2,1)}, bf16[2,2,256,512]{3,2,1,0:T(8,128)(2,1)S(1)}, u32[]{:S(2)}, u32[]{:S(2)}) %collective-permute-start.59) | collective-permute-done | bytes 1048608 | tf_op jit(solution)/shard_map/pair_sides0/ppermute | solution.py:37
  799.9 11.6 %back_first.2 = (bf16[512,1536]{1,0:T(8,128)(2,1)}, f32[1,2048]{1,0:T(1,128)}, bf16[528,512]{1,0:T(8,128)(2,1)}, bf16[528,512]{1,0:T(8,128)(2,1)}, bf16[528,512]{1,0:T(8,128)(2,1)}, /*index=5*/bf16[528,512]{1,0:T(8,128)(2,1)}) custom-call(s32[4]{0:T(128)} %pad_add_fusion.2.info, bf16[2,256,512]{2,1,0:T(8,128)(2,1)} %get-tuple-element.257.refs_0_, ...), custom_call_target="tpu_custom_call" | custom-call | flops 32212254 | bytes 146800 | tf_op jit(solution)/shard_map/back_first/pallas_call | solution.py:487
  815.4 10.1 collective-permute-done.67.refs_4_
  838.9 31.8 %collective-permute-done.68.refs_2_.refs_6_ = bf16[2,2,256,512]{3,2,1,0:T(8,128)(2,1)S(1)} collective-permute-done((bf16[2,2,256,512]{3,2,1,0:T(8,128)(2,1)}, bf16[2,2,256,512]{3,2,1,0:T(8,128)(2,1)S(1)}, u32[]{:S(2)}, u32[]{:S(2)}) %collective-permute-start.68) | collective-permute-done | bytes 1048608 | tf_op jit(solution)/shard_map/pair_sides1/ppermute | solution.py:37
  870.6 8.1 collective-permute-done.70.refs_3_.refs_7_
  894.4 11.7 %back_first.3 = (bf16[512,1536]{1,0:T(8,128)(2,1)}, f32[1,2048]{1,0:T(1,128)}, bf16[528,512]{1,0:T(8,128)(2,1)}, bf16[528,512]{1,0:T(8,128)(2,1)}, bf16[528,512]{1,0:T(8,128)(2,1)}, /*index=5*/bf16[528,512]{1,0:T(8,128)(2,1)}) custom-call(s32[4]{0:T(128)} %pad_add_fusion.info, bf16[2,256,512]{2,1,0:T(8,128)(2,1)} %get-tuple-element.288.refs_0_, ...), custom_call_target="tpu_custom_call" | custom-call | flops 32212254 | bytes 146800 | tf_op jit(solution)/shard_map/back_first/pallas_call | solution.py:487
  906.3 8.2 relative_grads.2
  922.0 9.8 relative_grads.3
  957.5 17.5 %collective-permute-done.76.refs_6_ = bf16[528,512]{1,0:T(8,128)(2,1)S(1)} collective-permute-done((bf16[528,512]{1,0:T(8,128)(2,1)}, bf16[528,512]{1,0:T(8,128)(2,1)S(1)}, u32[]{:S(2)}, u32[]{:S(2)}) %collective-permute-start.76) | collective-permute-done | bytes 540704 | tf_op jit(solution)/shard_map/first1/ppermute | solution.py:33
  982.5 9.4 collective-permute-start.81
  999.0 9.8 collective-permute-done.82
  1009.5 9.0 collective-permute-done.86
  1021.2 14.0 %collective-permute-done.84 = bf16[1,256,768]{2,1,0:T(8,128)(2,1)S(1)} collective-permute-done((bf16[1,256,768]{2,1,0:T(8,128)(2,1)S(1)}, bf16[1,256,768]{2,1,0:T(8,128)(2,1)S(1)}, u32[]{:S(2)}, u32[]{:S(2)}) %collective-permute-start.84) | collective-permute-done | bytes 393248 | tf_op jit(solution)/shard_map/weights/ppermute | solution.py:37
  (427 shorter events, 300.8 us)
Async XLA Ops:
  7.2 297.5 %all-gather.2.cloned.1.call-start = ((), (), s32[]{:S(2)}) async-start(), calls=%async_computation.4 | async-start | bytes 8650752 | tf_op jit(solution)/shard_map/all_gather | solution.py:1284
  114.2 495.6 %reduce-scatter.5.cloned.1.call-start = ((), (), s32[]{:S(2)}) async-start(), calls=%async_computation.5 | async-start | bytes 18874368 | tf_op jit(solution)/shard_map/reduce_scatter | solution.py:1416
  132.9 38.5 %collective-permute-start.18 = (bf16[3,2,2,256,512]{4,3,2,1,0:T(8,128)(2,1)S(1)}, bf16[3,2,2,256,512]{4,3,2,1,0:T(8,128)(2,1)}, u32[]{:S(2)}, u32[]{:S(2)}) collective-permute-start(bf16[3,2,2,256,512]{4,3,2,1,0:T(8,128)(2,1)S(1)} %pad_maximum_fusion), channel_id=1, source_target_pairs={{0,4},{4,0},{8,12},{12,8},{16,20},{20,16},{24,28},{28,24},{1,5},{5... | collective-permute-start | bytes 9437192 | tf_op jit(solution)/shard_map/pairs0/ppermute | solution.py:37
  135.3 36.1 %collective-permute-start.21 = (bf16[1024,512]{1,0:T(8,128)(2,1)S(1)}, bf16[1024,512]{1,0:T(8,128)(2,1)S(1)}, u32[]{:S(2)}, u32[]{:S(2)}) collective-permute-start(bf16[1024,512]{1,0:T(8,128)(2,1)S(1)} %bitcast.100), channel_id=1, source_target_pairs={{0,1},{1,0},{2,3},{3,2},{4,5},{5,4},{6,7},{7,6},{8,9},{9,8},{10,11... | collective-permute-start | bytes 3145736 | tf_op jit(solution)/shard_map/cotangent/ppermute | solution.py:46
  175.1 35.5 %collective-permute-start.29 = (bf16[2,2,256,512]{3,2,1,0:T(8,128)(2,1)}, bf16[2,2,256,512]{3,2,1,0:T(8,128)(2,1)S(1)}, u32[]{:S(2)}, u32[]{:S(2)}) collective-permute-start(bf16[2,2,256,512]{3,2,1,0:T(8,128)(2,1)} %get-tuple-element.190.refs_0_.refs_4_), channel_id=1, source_target_pairs={{0,16},{4,20},{8,24},{12,28},{16,0},{20,4},{24,8},{28,12},{1,17},{... | collective-permute-start | bytes 3145736 | tf_op jit(solution)/shard_map/pairs1/ppermute | solution.py:37
  176.2 34.5 %collective-permute-start.28 = (bf16[2,2,256,512]{3,2,1,0:T(8,128)(2,1)}, bf16[2,2,256,512]{3,2,1,0:T(8,128)(2,1)S(1)}, u32[]{:S(2)}, u32[]{:S(2)}) collective-permute-start(bf16[2,2,256,512]{3,2,1,0:T(8,128)(2,1)} %get-tuple-element.190.refs_0_.refs_4_), channel_id=1, source_target_pairs={{0,8},{4,12},{8,0},{12,4},{16,24},{20,28},{24,16},{28,20},{1,9},{5... | collective-permute-start | bytes 3145736 | tf_op jit(solution)/shard_map/pairs1/ppermute | solution.py:37
  211.0 62.4 %collective-permute-start.30 = (bf16[3,2,2,256,512]{4,3,2,1,0:T(8,128)(2,1)S(1)}, bf16[3,2,2,256,512]{4,3,2,1,0:T(8,128)(2,1)S(1)}, u32[]{:S(2)}, u32[]{:S(2)}) collective-permute-start(bf16[3,2,2,256,512]{4,3,2,1,0:T(8,128)(2,1)S(1)} %pad_maximum_fusion.1), channel_id=1, source_target_pairs={{0,4},{4,0},{8,12},{12,8},{16,20},{20,16},{24,28},{28,24},{1,5},{5... | collective-permute-start | bytes 9437192 | tf_op jit(solution)/shard_map/pairs1/ppermute | solution.py:37
  214.4 30.4 %collective-permute-start.31 = (bf16[1,2,256,512]{3,2,1,0:T(8,128)(2,1)S(1)}, bf16[1,2,256,512]{3,2,1,0:T(8,128)(2,1)S(1)}, u32[]{:S(2)}, u32[]{:S(2)}) collective-permute-start(bf16[1,2,256,512]{3,2,1,0:T(8,128)(2,1)S(1)} %slice.170), channel_id=1, source_target_pairs={{0,8},{4,12},{8,0},{12,4},{16,24},{20,28},{24,16},{28,20},{1,9},{5... | collective-permute-start | bytes 1572872 | tf_op jit(solution)/shard_map/pairs1/ppermute | solution.py:37
  216.0 28.9 %collective-permute-start.32 = (bf16[1,2,256,512]{3,2,1,0:T(8,128)(2,1)S(1)}, bf16[1,2,256,512]{3,2,1,0:T(8,128)(2,1)S(1)}, u32[]{:S(2)}, u32[]{:S(2)}) collective-permute-start(bf16[1,2,256,512]{3,2,1,0:T(8,128)(2,1)S(1)} %slice.171), channel_id=1, source_target_pairs={{0,16},{4,20},{8,24},{12,28},{16,0},{20,4},{24,8},{28,12},{1,17},{... | collective-permute-start | bytes 1572872 | tf_op jit(solution)/shard_map/pairs1/ppermute | solution.py:37
  245.0 30.2 %collective-permute-start.33 = (bf16[2,2,256,512]{3,2,1,0:T(8,128)(2,1)S(1)}, bf16[2,2,256,512]{3,2,1,0:T(8,128)(2,1)S(1)}, u32[]{:S(2)}, u32[]{:S(2)}) collective-permute-start(bf16[2,2,256,512]{3,2,1,0:T(8,128)(2,1)S(1)} %pad_maximum_fusion.4), channel_id=1, source_target_pairs={{0,4},{4,0},{8,12},{12,8},{16,20},{20,16},{24,28},{28,24},{1,5},{5... | collective-permute-start | bytes 3145736 | tf_op jit(solution)/shard_map/pairs1/ppermute | solution.py:37
  259.8 60.1 %collective-permute-start.37 = (bf16[1024,512]{1,0:T(8,128)(2,1)}, bf16[1024,512]{1,0:T(8,128)(2,1)}, u32[]{:S(2)}, u32[]{:S(2)}) collective-permute-start(bf16[1024,512]{1,0:T(8,128)(2,1)} %collective-permute-done.25.refs_5_), channel_id=1, source_target_pairs={{0,1},{1,0},{2,3},{3,2},{4,5},{5,4},{6,7},{7,6},{8,9},{9,8},{10,11... | collective-permute-start | bytes 3145736 | tf_op jit(solution)/shard_map/cotangent/ppermute | solution.py:65
  271.7 33.0 %collective-permute-start.36 = (bf16[512,512]{1,0:T(8,128)(2,1)}, bf16[512,512]{1,0:T(8,128)(2,1)}, u32[]{:S(2)}, u32[]{:S(2)}) collective-permute-start(bf16[512,512]{1,0:T(8,128)(2,1)} %collective-permute-done.35.refs_5_), channel_id=1, source_target_pairs={{0,1},{1,0},{2,3},{3,2},{4,5},{5,4},{6,7},{7,6},{8,9},{9,8},{10,11... | collective-permute-start | bytes 1572872 | tf_op jit(solution)/shard_map/heads0/ppermute | solution.py:65
  286.5 30.4 %collective-permute-start.39 = (bf16[512,512]{1,0:T(8,128)(2,1)}, bf16[512,512]{1,0:T(8,128)(2,1)S(1)}, u32[]{:S(2)}, u32[]{:S(2)}) collective-permute-start(bf16[512,512]{1,0:T(8,128)(2,1)} %bitcast.113), channel_id=1, source_target_pairs={{0,0},{1,2},{2,1},{3,3},{4,4},{5,6},{6,5},{7,7},{8,8},{9,10},{10,9... | collective-permute-start | bytes 1572872 | tf_op jit(solution)/shard_map/heads1/ppermute | solution.py:46
  288.2 28.8 %collective-permute-start.38 = (bf16[512,512]{1,0:T(8,128)(2,1)}, bf16[512,512]{1,0:T(8,128)(2,1)S(1)}, u32[]{:S(2)}, u32[]{:S(2)}) collective-permute-start(bf16[512,512]{1,0:T(8,128)(2,1)} %bitcast.114), channel_id=1, source_target_pairs={{0,1},{1,0},{2,3},{3,2},{4,5},{5,4},{6,7},{7,6},{8,9},{9,8},{10,11... | collective-permute-start | bytes 1572872 | tf_op jit(solution)/shard_map/heads1/ppermute | solution.py:46
  317.0 45.0 %collective-permute-start.40 = (bf16[512,512]{1,0:T(8,128)(2,1)S(1)}, bf16[512,512]{1,0:T(8,128)(2,1)S(1)}, u32[]{:S(2)}, u32[]{:S(2)}) collective-permute-start(bf16[512,512]{1,0:T(8,128)(2,1)S(1)} %collective-permute-done.39.refs_4_), channel_id=1, source_target_pairs={{0,1},{1,0},{2,3},{3,2},{4,5},{5,4},{6,7},{7,6},{8,9},{9,8},{10,11... | collective-permute-start | bytes 1572872 | tf_op jit(solution)/shard_map/heads1/ppermute | solution.py:55
  318.8 43.2 %collective-permute-start.41 = (bf16[512,512]{1,0:T(8,128)(2,1)S(1)}, bf16[512,512]{1,0:T(8,128)(2,1)S(1)}, u32[]{:S(2)}, u32[]{:S(2)}) collective-permute-start(bf16[512,512]{1,0:T(8,128)(2,1)S(1)} %collective-permute-done.38.refs_1_), channel_id=1, source_target_pairs={{0,0},{1,2},{2,1},{3,3},{4,4},{5,6},{6,5},{7,7},{8,8},{9,10},{10,9... | collective-permute-start | bytes 1572872 | tf_op jit(solution)/shard_map/heads1/ppermute | solution.py:56
  362.0 38.1 %collective-permute-start.42 = (bf16[512,512]{1,0:T(8,128)(2,1)S(1)}, bf16[512,512]{1,0:T(8,128)(2,1)S(1)}, u32[]{:S(2)}, u32[]{:S(2)}) collective-permute-start(bf16[512,512]{1,0:T(8,128)(2,1)S(1)} %collective-permute-done.41.refs_5_), channel_id=1, source_target_pairs={{0,1},{1,0},{2,3},{3,2},{4,5},{5,4},{6,7},{7,6},{8,9},{9,8},{10,11... | collective-permute-start | bytes 1572872 | tf_op jit(solution)/shard_map/heads1/ppermute | solution.py:65
  395.0 78.4 %collective-permute-start.43 = (bf16[128,2048]{1,0:T(8,128)(2,1)}, bf16[128,2048]{1,0:T(8,128)(2,1)S(1)}, u32[]{:S(2)}, u32[]{:S(2)}) collective-permute-start(bf16[128,2048]{1,0:T(8,128)(2,1)} %get-tuple-element.230), channel_id=1, source_target_pairs={{0,1},{1,2},{2,3},{3,0},{4,5},{5,6},{6,7},{7,4},{8,9},{9,10},{10,1... | collective-permute-start | bytes 1572872 | tf_op jit(solution)/shard_map/ffn_grad0/ppermute | solution.py:33
  395.3 78.1 %collective-permute-start.44 = (bf16[128,2048]{1,0:T(8,128)(2,1)}, bf16[128,2048]{1,0:T(8,128)(2,1)S(1)}, u32[]{:S(2)}, u32[]{:S(2)}) collective-permute-start(bf16[128,2048]{1,0:T(8,128)(2,1)} %get-tuple-element.231), channel_id=1, source_target_pairs={{0,2},{1,3},{2,0},{3,1},{4,6},{5,7},{6,4},{7,5},{8,10},{9,11},{10,... | collective-permute-start | bytes 1572872 | tf_op jit(solution)/shard_map/ffn_grad0/ppermute | solution.py:33
  398.2 75.2 %collective-permute-start.45 = (bf16[128,2048]{1,0:T(8,128)(2,1)}, bf16[128,2048]{1,0:T(8,128)(2,1)S(1)}, u32[]{:S(2)}, u32[]{:S(2)}) collective-permute-start(bf16[128,2048]{1,0:T(8,128)(2,1)} %get-tuple-element.232), channel_id=1, source_target_pairs={{0,3},{1,0},{2,1},{3,2},{4,7},{5,4},{6,5},{7,6},{8,11},{9,8},{10,9... | collective-permute-start | bytes 1572872 | tf_op jit(solution)/shard_map/ffn_grad0/ppermute | solution.py:33
  483.9 327.6 %reduce-scatter.7.cloned.1.call-start = ((), (), s32[]{:S(2)}) async-start(), calls=%async_computation.6 | async-start | bytes 18874368 | tf_op jit(solution)/shard_map/reduce_scatter | solution.py:1416
  500.8 39.1 %collective-permute-start.46 = (bf16[768,512]{1,0:T(8,128)(2,1)}, bf16[768,512]{1,0:T(8,128)(2,1)S(1)}, u32[]{:S(2)}, u32[]{:S(2)}) collective-permute-start(bf16[768,512]{1,0:T(8,128)(2,1)} %get-tuple-element.245), channel_id=1, source_target_pairs={{0,1},{1,2},{2,3},{3,0},{4,5},{5,6},{6,7},{7,4},{8,9},{9,10},{10,1... | collective-permute-start | bytes 2359304 | tf_op jit(solution)/shard_map/mixture0/ppermute | solution.py:33
  501.5 64.5 %collective-permute-start.47 = (bf16[768,512]{1,0:T(8,128)(2,1)}, bf16[768,512]{1,0:T(8,128)(2,1)S(1)}, u32[]{:S(2)}, u32[]{:S(2)}) collective-permute-start(bf16[768,512]{1,0:T(8,128)(2,1)} %get-tuple-element.246), channel_id=1, source_target_pairs={{0,2},{1,3},{2,0},{3,1},{4,6},{5,7},{6,4},{7,5},{8,10},{9,11},{10,... | collective-permute-start | bytes 2359304 | tf_op jit(solution)/shard_map/mixture0/ppermute | solution.py:33
  502.2 63.8 %collective-permute-start.48 = (bf16[768,512]{1,0:T(8,128)(2,1)}, bf16[768,512]{1,0:T(8,128)(2,1)S(1)}, u32[]{:S(2)}, u32[]{:S(2)}) collective-permute-start(bf16[768,512]{1,0:T(8,128)(2,1)} %get-tuple-element.247), channel_id=1, source_target_pairs={{0,3},{1,0},{2,1},{3,2},{4,7},{5,4},{6,5},{7,6},{8,11},{9,8},{10,9... | collective-permute-start | bytes 2359304 | tf_op jit(solution)/shard_map/mixture0/ppermute | solution.py:33
  538.0 42.9 %collective-permute-start.49 = (bf16[128,2048]{1,0:T(8,128)(2,1)}, bf16[128,2048]{1,0:T(8,128)(2,1)S(1)}, u32[]{:S(2)}, u32[]{:S(2)}) collective-permute-start(bf16[128,2048]{1,0:T(8,128)(2,1)} %get-tuple-element.259), channel_id=1, source_target_pairs={{0,1},{1,2},{2,3},{3,0},{4,5},{5,6},{6,7},{7,4},{8,9},{9,10},{10,1... | collective-permute-start | bytes 1572872 | tf_op jit(solution)/shard_map/ffn_grad1/ppermute | solution.py:33
  538.5 61.0 %collective-permute-start.50 = (bf16[128,2048]{1,0:T(8,128)(2,1)}, bf16[128,2048]{1,0:T(8,128)(2,1)S(1)}, u32[]{:S(2)}, u32[]{:S(2)}) collective-permute-start(bf16[128,2048]{1,0:T(8,128)(2,1)} %get-tuple-element.260), channel_id=1, source_target_pairs={{0,2},{1,3},{2,0},{3,1},{4,6},{5,7},{6,4},{7,5},{8,10},{9,11},{10,... | collective-permute-start | bytes 1572872 | tf_op jit(solution)/shard_map/ffn_grad1/ppermute | solution.py:33
  540.0 59.6 %collective-permute-start.51 = (bf16[128,2048]{1,0:T(8,128)(2,1)}, bf16[128,2048]{1,0:T(8,128)(2,1)}, u32[]{:S(2)}, u32[]{:S(2)}) collective-permute-start(bf16[128,2048]{1,0:T(8,128)(2,1)} %get-tuple-element.261), channel_id=1, source_target_pairs={{0,3},{1,0},{2,1},{3,2},{4,7},{5,4},{6,5},{7,6},{8,11},{9,8},{10,9... | collective-permute-start | bytes 1572872 | tf_op jit(solution)/shard_map/ffn_grad1/ppermute | solution.py:33
  609.8 296.3 %reduce-scatter.9.cloned.1.call-start = ((), (), s32[]{:S(2)}) async-start(), calls=%async_computation.7 | async-start | bytes 9437184 | tf_op jit(solution)/shard_map/reduce_scatter | solution.py:1416
  609.9 28.8 %collective-permute-start.55 = (bf16[4,2,2,256,512]{4,3,2,1,0:T(8,128)(2,1)}, bf16[4,2,2,256,512]{4,3,2,1,0:T(8,128)(2,1)S(1)}, u32[]{:S(2)}, u32[]{:S(2)}) collective-permute-start(bf16[4,2,2,256,512]{4,3,2,1,0:T(8,128)(2,1)} %get-tuple-element.283), channel_id=1, source_target_pairs={{0,4},{4,0},{8,12},{12,8},{16,20},{20,16},{24,28},{28,24},{1,5},{5... | collective-permute-start | bytes 12582920 | tf_op jit(solution)/shard_map/pair_cores0/ppermute | solution.py:37
  625.8 83.8 %collective-permute-start.52 = (bf16[768,512]{1,0:T(8,128)(2,1)}, bf16[768,512]{1,0:T(8,128)(2,1)S(1)}, u32[]{:S(2)}, u32[]{:S(2)}) collective-permute-start(bf16[768,512]{1,0:T(8,128)(2,1)} %get-tuple-element.274), channel_id=1, source_target_pairs={{0,1},{1,2},{2,3},{3,0},{4,5},{5,6},{6,7},{7,4},{8,9},{9,10},{10,1... | collective-permute-start | bytes 2359304 | tf_op jit(solution)/shard_map/mixture1/ppermute | solution.py:33
  636.1 73.5 %collective-permute-start.53 = (bf16[768,512]{1,0:T(8,128)(2,1)}, bf16[768,512]{1,0:T(8,128)(2,1)S(1)}, u32[]{:S(2)}, u32[]{:S(2)}) collective-permute-start(bf16[768,512]{1,0:T(8,128)(2,1)} %get-tuple-element.275), channel_id=1, source_target_pairs={{0,2},{1,3},{2,0},{3,1},{4,6},{5,7},{6,4},{7,5},{8,10},{9,11},{10,... | collective-permute-start | bytes 2359304 | tf_op jit(solution)/shard_map/mixture1/ppermute | solution.py:33
  638.3 71.4 %collective-permute-start.54 = (bf16[768,512]{1,0:T(8,128)(2,1)}, bf16[768,512]{1,0:T(8,128)(2,1)S(1)}, u32[]{:S(2)}, u32[]{:S(2)}) collective-permute-start(bf16[768,512]{1,0:T(8,128)(2,1)} %get-tuple-element.276), channel_id=1, source_target_pairs={{0,3},{1,0},{2,1},{3,2},{4,7},{5,4},{6,5},{7,6},{8,11},{9,8},{10,9... | collective-permute-start | bytes 2359304 | tf_op jit(solution)/shard_map/mixture1/ppermute | solution.py:33
  645.4 57.4 %collective-permute-start.56 = (bf16[2,256,512]{2,1,0:T(8,128)(2,1)}, bf16[2,256,512]{2,1,0:T(8,128)(2,1)S(1)}, u32[]{:S(2)}, u32[]{:S(2)}) collective-permute-start(bf16[2,256,512]{2,1,0:T(8,128)(2,1)} %get-tuple-element.352), channel_id=1, source_target_pairs={{0,8},{4,12},{8,0},{12,4},{16,24},{20,28},{24,16},{28,20},{1,9},{5... | collective-permute-start | bytes 1572872 | tf_op jit(solution)/shard_map/pair_diagonal0/ppermute | solution.py:37
  652.8 53.4 %collective-permute-start.57 = (bf16[2,256,512]{2,1,0:T(8,128)(2,1)}, bf16[2,256,512]{2,1,0:T(8,128)(2,1)S(1)}, u32[]{:S(2)}, u32[]{:S(2)}) collective-permute-start(bf16[2,256,512]{2,1,0:T(8,128)(2,1)} %get-tuple-element.351), channel_id=1, source_target_pairs={{0,16},{4,20},{8,24},{12,28},{16,0},{20,4},{24,8},{28,12},{1,17},{... | collective-permute-start | bytes 1572872 | tf_op jit(solution)/shard_map/pair_diagonal0/ppermute | solution.py:37
  724.4 71.1 %collective-permute-start.58 = (bf16[4,2,2,256,512]{4,3,2,1,0:T(8,128)(2,1)}, bf16[4,2,2,256,512]{4,3,2,1,0:T(8,128)(2,1)S(1)}, u32[]{:S(2)}, u32[]{:S(2)}) collective-permute-start(bf16[4,2,2,256,512]{4,3,2,1,0:T(8,128)(2,1)} %get-tuple-element.287), channel_id=1, source_target_pairs={{0,4},{4,0},{8,12},{12,8},{16,20},{20,16},{24,28},{28,24},{1,5},{5... | collective-permute-start | bytes 12582920 | tf_op jit(solution)/shard_map/pair_cores1/ppermute | solution.py:37
  726.4 50.0 %collective-permute-start.59 = (bf16[2,2,256,512]{3,2,1,0:T(8,128)(2,1)}, bf16[2,2,256,512]{3,2,1,0:T(8,128)(2,1)S(1)}, u32[]{:S(2)}, u32[]{:S(2)}) collective-permute-start(bf16[2,2,256,512]{3,2,1,0:T(8,128)(2,1)} %add_blocks.9), channel_id=1, source_target_pairs={{0,8},{4,12},{8,0},{12,4},{16,24},{20,28},{24,16},{28,20},{1,9},{5... | collective-permute-start | bytes 3145736 | tf_op jit(solution)/shard_map/pair_sides0/ppermute | solution.py:37
  730.3 46.5 %collective-permute-start.60 = (bf16[2,2,256,512]{3,2,1,0:T(8,128)(2,1)}, bf16[2,2,256,512]{3,2,1,0:T(8,128)(2,1)S(1)}, u32[]{:S(2)}, u32[]{:S(2)}) collective-permute-start(bf16[2,2,256,512]{3,2,1,0:T(8,128)(2,1)} %add_blocks.10), channel_id=1, source_target_pairs={{0,16},{4,20},{8,24},{12,28},{16,0},{20,4},{24,8},{28,12},{1,17},{... | collective-permute-start | bytes 3145736 | tf_op jit(solution)/shard_map/pair_sides0/ppermute | solution.py:37
  811.6 246.4 %reduce-scatter.11.cloned.1.call-start = ((), (), s32[]{:S(2)}) async-start(), calls=%async_computation.8 | async-start | bytes 18874368 | tf_op jit(solution)/shard_map/reduce_scatter | solution.py:1416
  829.0 41.6 %collective-permute-start.68 = (bf16[2,2,256,512]{3,2,1,0:T(8,128)(2,1)}, bf16[2,2,256,512]{3,2,1,0:T(8,128)(2,1)S(1)}, u32[]{:S(2)}, u32[]{:S(2)}) collective-permute-start(bf16[2,2,256,512]{3,2,1,0:T(8,128)(2,1)} %add_blocks.13), channel_id=1, source_target_pairs={{0,8},{4,12},{8,0},{12,4},{16,24},{20,28},{24,16},{28,20},{1,9},{5... | collective-permute-start | bytes 3145736 | tf_op jit(solution)/shard_map/pair_sides1/ppermute | solution.py:37
  833.3 45.4 %collective-permute-start.70 = (bf16[2,2,256,512]{3,2,1,0:T(8,128)(2,1)}, bf16[2,2,256,512]{3,2,1,0:T(8,128)(2,1)S(1)}, u32[]{:S(2)}, u32[]{:S(2)}) collective-permute-start(bf16[2,2,256,512]{3,2,1,0:T(8,128)(2,1)} %add_blocks.14), channel_id=1, source_target_pairs={{0,16},{4,20},{8,24},{12,28},{16,0},{20,4},{24,8},{28,12},{1,17},{... | collective-permute-start | bytes 3145736 | tf_op jit(solution)/shard_map/pair_sides1/ppermute | solution.py:37
  834.8 52.2 %collective-permute-start.64 = (bf16[528,512]{1,0:T(8,128)(2,1)S(1)}, bf16[528,512]{1,0:T(8,128)(2,1)S(1)}, u32[]{:S(2)}, u32[]{:S(2)}) collective-permute-start(bf16[528,512]{1,0:T(8,128)(2,1)S(1)} %copy-done.86), channel_id=1, source_target_pairs={{0,1},{1,2},{2,3},{3,0},{4,5},{5,6},{6,7},{7,4},{8,9},{9,10},{10,1... | collective-permute-start | bytes 1622024 | tf_op jit(solution)/shard_map/first0/ppermute | solution.py:33
  834.8 54.2 %collective-permute-start.65 = (bf16[528,512]{1,0:T(8,128)(2,1)S(1)}, bf16[528,512]{1,0:T(8,128)(2,1)}, u32[]{:S(2)}, u32[]{:S(2)}) collective-permute-start(bf16[528,512]{1,0:T(8,128)(2,1)S(1)} %copy-done.85), channel_id=1, source_target_pairs={{0,2},{1,3},{2,0},{3,1},{4,6},{5,7},{6,4},{7,5},{8,10},{9,11},{10,... | collective-permute-start | bytes 1622024 | tf_op jit(solution)/shard_map/first0/ppermute | solution.py:33
  836.6 52.4 %collective-permute-start.66 = (bf16[528,512]{1,0:T(8,128)(2,1)S(1)}, bf16[528,512]{1,0:T(8,128)(2,1)}, u32[]{:S(2)}, u32[]{:S(2)}) collective-permute-start(bf16[528,512]{1,0:T(8,128)(2,1)S(1)} %copy-done.84), channel_id=1, source_target_pairs={{0,3},{1,0},{2,1},{3,2},{4,7},{5,4},{6,5},{7,6},{8,11},{9,8},{10,9... | collective-permute-start | bytes 1622024 | tf_op jit(solution)/shard_map/first0/ppermute | solution.py:33
  936.0 39.1 %collective-permute-start.76 = (bf16[528,512]{1,0:T(8,128)(2,1)}, bf16[528,512]{1,0:T(8,128)(2,1)S(1)}, u32[]{:S(2)}, u32[]{:S(2)}) collective-permute-start(bf16[528,512]{1,0:T(8,128)(2,1)} %get-tuple-element.308), channel_id=1, source_target_pairs={{0,2},{1,3},{2,0},{3,1},{4,6},{5,7},{6,4},{7,5},{8,10},{9,11},{10,... | collective-permute-start | bytes 1622024 | tf_op jit(solution)/shard_map/first1/ppermute | solution.py:33
  938.4 36.7 %collective-permute-start.77 = (bf16[528,512]{1,0:T(8,128)(2,1)}, bf16[528,512]{1,0:T(8,128)(2,1)}, u32[]{:S(2)}, u32[]{:S(2)}) collective-permute-start(bf16[528,512]{1,0:T(8,128)(2,1)} %get-tuple-element.309), channel_id=1, source_target_pairs={{0,3},{1,0},{2,1},{3,2},{4,7},{5,4},{6,5},{7,6},{8,11},{9,8},{10,9... | collective-permute-start | bytes 1622024 | tf_op jit(solution)/shard_map/first1/ppermute | solution.py:33
  940.6 57.2 %collective-permute-start.85 = (bf16[2,256,768]{2,1,0:T(8,128)(2,1)}, bf16[2,256,768]{2,1,0:T(8,128)(2,1)}, u32[]{:S(2)}, u32[]{:S(2)}) collective-permute-start(bf16[2,256,768]{2,1,0:T(8,128)(2,1)} %stack.42), channel_id=1, source_target_pairs={{0,16},{4,20},{8,24},{12,28},{16,0},{20,4},{24,8},{28,12},{1,17},{... | collective-permute-start | bytes 2359304 | tf_op jit(solution)/shard_map/weights/ppermute | solution.py:37
  950.5 31.9 %collective-permute-start.80 = (f32[20,2048]{1,0:T(8,128)S(1)}, f32[20,2048]{1,0:T(8,128)S(1)}, u32[]{:S(2)}, u32[]{:S(2)}) collective-permute-start(f32[20,2048]{1,0:T(8,128)S(1)} %add.213), channel_id=1, source_target_pairs={{0,16},{4,20},{8,24},{12,28},{16,0},{20,4},{24,8},{28,12},{1,17},{... | collective-permute-start | bytes 491528 | tf_op jit(solution)/shard_map/small/ppermute | solution.py:37
  955.0 54.5 %collective-permute-start.83 = (bf16[2,256,768]{2,1,0:T(8,128)(2,1)S(1)}, bf16[2,256,768]{2,1,0:T(8,128)(2,1)S(1)}, u32[]{:S(2)}, u32[]{:S(2)}) collective-permute-start(bf16[2,256,768]{2,1,0:T(8,128)(2,1)S(1)} %pad_maximum_fusion.6), channel_id=1, source_target_pairs={{0,8},{4,12},{8,0},{12,4},{16,24},{20,28},{24,16},{28,20},{1,9},{5... | collective-permute-start | bytes 2359304 | tf_op jit(solution)/shard_map/weights/ppermute | solution.py:37
  (134 other events, 1777.7 us)
Sparse Core Ops, SparseCore 0:
  114.4 96.9 all-gather.1
  484.0 114.4 reduce-scatter.4
  610.0 167.8 reduce-scatter.6
  811.7 87.6 reduce-scatter.8
  906.3 147.0 reduce-scatter.10
